TPU v7x, 32 devices: a whole 2x2x4 slice. The times are simulated.
32 devices in a mesh: groups: 2 (over y), expert: 8 (over z, x), section: 2 (over core).
Axes of the slice: x: 2, y: 2, z: 4, core: 2. Of those that a mesh axis runs over, the one named last changes fastest.
Arguments:
- tokens: bfloat16 [2, 128, 7168], P(None, ('groups', 'expert')), parts along dimension 1, may hold values from -6 to 6
- routes: int32 [2, 2, 128, 4], P('section', None, ('groups', 'expert')), parts along dimension 2, may hold values from 0 to 15, all different within a row; in each aligned block of 8 rows (0 to 7, 8 to 15, ..., all dimensions but the last counted through in order) at most 3 rows name the same one
- norm_gain: float32 [2, 7168], P('section'), may hold values from 0.5 to 1.5
- router_weight: bfloat16 [2, 7168, 16], P('section'), may hold values from -0.125 to 0.125
- gate_weight: bfloat16 [2, 7168, 16384], P('section', None, 'expert'), may hold values from -0.0625 to 0.0625
- up_weight: bfloat16 [2, 7168, 16384], P('section', None, 'expert'), may hold values from -0.0625 to 0.0625
- down_weight: bfloat16 [2, 16384, 7168], P('section', 'expert'), may hold values from -0.375 to 0.375
Outputs:
- encoded: bfloat16 [2, 128, 7168], P('section', ('groups', 'expert')), parts along dimension 1
There are 2 independent parts, one for each index of `groups`. A program takes and returns all parts, laid end to end along the dimension named above; an argument that names none is the same for every part. Nothing has to cross between parts.
Inputs may be any that keep to these rules, and one draw needn't show every extreme that they name: `routes`: each token names 4 different experts. For every layer, micro-batch and aligned block of 8 tokens, no expert is named by more than 3 of the block's tokens.
All inputs are finite; a program needn't handle non-finite values.
Results may differ from a plain program's by a relative error of at most 0.0074.
Values may be sent and summed in bfloat16 or wider, within the bound.
No kernel may reach another device: no remote copies, remote signals or barrier semaphores. Data moves between devices by JAX's collectives and lax.ppermute only.
A program may use at most 256 MiB of HBM per device.

v0:
```python
import functools

import jax
import jax.numpy as jnp
from jax import lax
from jax.experimental import pallas as pl
from jax.experimental.pallas import tpu as pltpu
from jax.sharding import PartitionSpec as P

FF = 1024
EXPERTS = 16
EPSILON = 1e-06
CHUNKS = 2
LANES = 128
MIB = 1 << 20
IN_VMEM = pl.BlockSpec(memory_space=pltpu.VMEM)
ANYWHERE = pl.BlockSpec(memory_space=pl.ANY)


def bit_orders(count):
    bits = [1 << k for k in range(count.bit_length() - 1)]
    return bits, bits[1:2] + bits[:1] + bits[2:]


def block_of(order):
    table = [0]
    for bit in reversed(order):
        table = table + [b ^ bit for b in table]
    return table


def swap_tables(count):
    first, second = (block_of(order) for order in bit_orders(count))
    return [second.index(b) for b in first], [first.index(b) for b in second]


def exchange(value, level):
    count = lax.axis_size("expert")
    orders = bit_orders(count)
    pairs = [
        (2 * e + s, 2 * (e ^ orders[s][level]) + s) for e in range(count) for s in range(2)
    ]
    return lax.ppermute(value, ("expert", "section"), pairs)


def swap(value):
    return lax.ppermute(value, "section", [(0, 1), (1, 0)])


def add(left, right):
    return left.astype(jnp.float32) + right.astype(jnp.float32)


def reduce_to(value, last):
    level = 0
    while value.shape[0] > last:
        half = value.shape[0] // 2
        received = exchange(value[half:], level)
        value = add(value[:half], received)
        if half > 1:
            value = value.astype(jnp.bfloat16)
        level += 1
    return value, level


def after_token(value, token):
    return value + token[None]


class Arena:
    def __init__(self, weights, width, slots, top):
        self.weights, self.width, self.slots = weights, width, slots
        self.units = weights[0].shape[2]
        self.blocks = weights[0].shape[1] // width
        self.tile = min(256, self.units)
        self.loads = 3 * self.blocks
        self.slot_rows = width * self.units // self.tile
        self.nbytes = slots * self.slot_rows * self.tile * 2
        self.limit = top - self.nbytes
        self.type = pltpu.VMEM((slots * self.slot_rows, self.tile), weights[0].dtype)

    def at(self, load):
        return load % self.slots * self.slot_rows

    def down_load(self, block):
        return 2 * self.blocks + block

    def copies(self, load, sources, arena, sems):
        made = []
        if load < 2 * self.blocks:
            source, block, depth = sources[load % 2], load // 2, self.width
            corners = [(block * depth, t * self.tile) for t in range(self.units // self.tile)]
        else:
            source, block, depth = sources[2], load - 2 * self.blocks, self.units
            corners = [(0, block * self.width + t * self.tile) for t in range(self.width // self.tile)]
        for t, (row, column) in enumerate(corners):
            made.append(
                pltpu.make_async_copy(
                    source.at[0, pl.ds(row, depth), pl.ds(column, self.tile)],
                    arena.at[pl.ds(self.at(load) + t * depth, depth)],
                    sems.at[t],
                )
            )
        return made


def call(body, layer, place, arena, inputs, outputs, scratch, loads, name, after=None, token=None, zeros=False, specs=None):
    n_in, n_out = len(inputs), len(outputs)
    extra = [] if after is None else [after]
    held = [] if arena is None else [arena]
    most = max(place.units, place.width) // place.tile

    def kernel(*refs):
        refs = list(refs)
        ins, refs = refs[:n_in], refs[n_in:]
        sources, refs = refs[:3], refs[3 + len(extra) + len(held) :]
        outs, refs = refs[:n_out], refs[n_out:]
        memory, refs = refs[0], refs[1:]
        if token is not None:
            marker, refs = refs[0], refs[1:]
            marker[...] = jnp.zeros_like(marker)
        sems, refs = refs[0], refs[1:]
        flying = {}

        def start(load):
            flying[load] = place.copies(load, sources, memory, sems.at[loads.index(load)])
            for copy in flying[load]:
                copy.start()

        def wait(load):
            for copy in flying.pop(load, []):
                copy.wait()

        def work():
            body(ins, outs, refs, memory, start, wait)
            for load in list(flying):
                wait(load)

        if layer is None:
            work()
        else:
            here = lax.axis_index("section") == layer
            pl.when(here)(work)
            if zeros:

                @pl.when(jnp.logical_not(here))
                def _():
                    for out in outs:
                        out[...] = jnp.zeros_like(out)

    shapes = list(outputs) + [place.type]
    if token is not None:
        shapes.append(pltpu.VMEM(token, jnp.bfloat16))
    moved = max(len(loads), 1) * place.slot_rows * place.tile * 2
    results = pl.pallas_call(
        kernel,
        in_specs=(specs or [IN_VMEM] * n_in) + [ANYWHERE] * 3 + [IN_VMEM] * (len(extra) + len(held)),
        out_specs=[IN_VMEM] * len(shapes),
        out_shape=shapes,
        input_output_aliases={n_in + 3 + len(extra): n_out} if held else {},
        scratch_shapes=[pltpu.SemaphoreType.DMA((max(len(loads), 1), most))] + list(scratch),
        compiler_params=pltpu.CompilerParams(vmem_limit_bytes=place.limit),
        cost_estimate=pl.CostEstimate(flops=0, transcendentals=0, bytes_accessed=moved),
        name=name,
    )(*inputs, *place.weights, *extra, *held)
    return list(results)


def prepare(tokens, routes, width):
    micro, rows, _ = tokens.shape
    top = routes.shape[2]
    block = micro * rows

    def kernel(tokens_ref, routes_ref, *outs):
        section = lax.axis_index("section")
        for c in range(CHUNKS):
            at = pl.multiple_of((2 * c + section) * width, LANES)
            both = [tokens_ref[m, :, pl.ds(at, width)].astype(jnp.float32) for m in range(micro)]
            outs[c][0, :, :width] = jnp.concatenate(both, 0).astype(jnp.bfloat16)
        lane = lax.broadcasted_iota(jnp.int32, (rows, LANES), 1)
        eye = lax.broadcasted_iota(jnp.int32, (rows, rows), 0) == lax.broadcasted_iota(
            jnp.int32, (rows, rows), 1
        )
        named = []
        for m in range(micro):
            value = jnp.zeros((rows, LANES), jnp.float32)
            for k in range(top):
                line = jnp.broadcast_to(routes_ref[0, m, k : k + 1].astype(jnp.float32), (rows, rows))
                column = jnp.sum(jnp.where(eye, line, 0.0), axis=1, keepdims=True)
                value = jnp.where(lane == k, column, value)
            named.append(value)
        outs[0][0, :, width:] = jnp.concatenate(named, 0).astype(jnp.bfloat16)

    shapes = [
        jax.ShapeDtypeStruct((1, block, width + (LANES if c == 0 else 0)), jnp.bfloat16)
        for c in range(CHUNKS)
    ]
    return pl.pallas_call(
        kernel,
        in_specs=[IN_VMEM] * 2,
        out_specs=[IN_VMEM] * CHUNKS,
        out_shape=shapes,
        name="prepare",
    )(tokens, routes)


def layer_body(place, top, ins, outs, scratch, memory, start, wait):
    pairs = [ins[2 * c : 2 * c + 2] for c in range(CHUNKS)]
    gain, router, named = ins[2 * CHUNKS :]
    scaled, stats, gate_sum, up_sum, hidden, routes, sem = scratch
    count, rows, width = outs[0].shape
    tile, units, blocks = place.tile, place.units, place.blocks
    model_width = gain.shape[1]
    section = lax.axis_index("section")
    tables = swap_tables(count)
    lane = lax.broadcasted_iota(jnp.int32, (rows, LANES), 1)
    bring = pltpu.make_async_copy(named.at[:, :, pl.ds(width, LANES)], routes, sem)
    bring.start()

    def used(load):
        if load + place.slots < place.loads:
            start(load + place.slots)

    def block_for_other(p):
        return jnp.where(section == 0, tables[0][p], tables[1][p])

    for chunk, (own, other) in enumerate(pairs):
        mine_at = pl.multiple_of((2 * chunk + section) * width, LANES)
        theirs_at = pl.multiple_of((2 * chunk + 1 - section) * width, LANES)
        mine_gain = gain[:, pl.ds(mine_at, width)]
        theirs_gain = gain[:, pl.ds(theirs_at, width)]
        for p in range(count):
            at = pl.ds(p * rows, rows)
            mine = own[p, :, :width].astype(jnp.float32)
            theirs = other[block_for_other(p), :, :width].astype(jnp.float32)
            scaled[at, pl.ds(mine_at, width)] = (mine * mine_gain).astype(jnp.bfloat16)
            scaled[at, pl.ds(theirs_at, width)] = (theirs * theirs_gain).astype(jnp.bfloat16)
            square = jnp.sum(mine * mine + theirs * theirs, axis=-1, keepdims=True)
            square = jnp.where(lane == EXPERTS, square, 0.0)
            stats[at, :] = square if chunk == 0 else stats[at, :] + square
    stats[:, :EXPERTS] = lax.dot_general(
        scaled[...], router[0], (((1,), (1,)), ((), ())), preferred_element_type=jnp.float32
    )
    values = stats[...]
    lanes = lax.broadcasted_iota(jnp.int32, values.shape, 1)
    total = jnp.sum(jnp.where(lanes == EXPERTS, values, 0.0), axis=-1, keepdims=True)
    factor = lax.rsqrt(total / model_width + EPSILON)
    affinity = jax.nn.sigmoid(values * factor)
    bring.wait()
    experts = routes[...].astype(jnp.float32).reshape(values.shape)
    hit = jnp.zeros(values.shape, jnp.bool_)
    for k in range(top):
        hit = hit | (experts[:, k : k + 1] == lanes.astype(jnp.float32))
    picked = jnp.where(hit & (lanes < EXPERTS), affinity, 0.0)
    gates = picked / jnp.sum(picked, axis=-1, keepdims=True)
    unit_at = lax.axis_index("expert") * units

    for block in range(blocks):
        value = scaled.at[:, block * width : (block + 1) * width]
        for side, sums in enumerate((gate_sum, up_sum)):
            load = 2 * block + side
            wait(load)
            for t in range(units // tile):
                at = slice(t * tile, (t + 1) * tile)
                part = jnp.dot(
                    value[...],
                    memory[pl.ds(place.at(load) + t * width, width)],
                    preferred_element_type=jnp.float32,
                )
                if block > 0:
                    part += sums[:, at]
                if block < blocks - 1 or side == 0:
                    sums[:, at] = part
                    continue
                expert = (unit_at + t * tile) // FF
                weight = jnp.sum(jnp.where(lanes == expert, gates, 0.0), axis=-1, keepdims=True)
                gated = jax.nn.silu(gate_sum[:, at] * factor) * (part * (factor * weight))
                hidden[:, at] = gated.astype(jnp.bfloat16)
            used(load)

    for chunk in range(CHUNKS):
        places = []
        for side in range(2):
            load = place.down_load(2 * chunk + side)
            wait(load)
            places.append(place.at(load))
        for own in range(2):
            out = outs[2 * chunk + own]
            side = section if own else 1 - section
            base = jnp.where(side == 0, places[0], places[1])
            for t in range(width // tile):
                at = pl.multiple_of(base + t * units, 16)
                part = jnp.dot(
                    hidden[...], memory[pl.ds(at, units)], preferred_element_type=jnp.float32
                ).astype(jnp.bfloat16)
                to = slice(t * tile, (t + 1) * tile)
                for p in range(count):
                    out[p if own else block_for_other(p), :, to] = part[p * rows : (p + 1) * rows]
        for side in range(2):
            used(place.down_load(2 * chunk + side))


def run_layer(layer, place, arena, pairs, gain, router, named, top):
    count, rows, _ = pairs[0][0].shape
    total = count * rows
    shape = jax.ShapeDtypeStruct((count, rows, place.width), jnp.bfloat16)
    scratch = [
        pltpu.VMEM((total, gain.shape[1]), jnp.bfloat16),
        pltpu.VMEM((total, LANES), jnp.float32),
        pltpu.VMEM((total, place.units), jnp.float32),
        pltpu.VMEM((total, place.units), jnp.float32),
        pltpu.VMEM((total, place.units), jnp.bfloat16),
        pltpu.VMEM((count, rows, LANES), jnp.bfloat16),
        pltpu.SemaphoreType.DMA,
    ]
    inputs = [value for pair in pairs for value in pair] + [gain, router, named]
    specs = [IN_VMEM] * (len(inputs) - 1) + [ANYWHERE]
    results = call(
        functools.partial(layer_body, place, top),
        layer, place, arena, inputs, [shape] * (2 * CHUNKS), scratch,
        list(range(place.slots, place.loads)), "layer", zeros=True, specs=specs,
    )
    return results[:-1], results[-1]


def run_layer_plainly(layer, weights, pairs, gain, router, named, top):
    count, rows, _ = pairs[0][0].shape
    model_width = gain.shape[1]
    width = model_width // (2 * CHUNKS)
    units = weights[0].shape[2]
    first = lax.axis_index("section") == 0
    tables = jnp.array(swap_tables(count), jnp.int32)
    table = jnp.where(first, tables[0], tables[1])
    back = jnp.where(first, tables[1], tables[0])
    columns = []
    for own, other in pairs:
        own, other = own[:, :, :width], other[:, :, :width][table]
        columns += [jnp.where(first, own, other), jnp.where(first, other, own)]
    values = jnp.concatenate(columns, axis=-1).reshape(count * rows, model_width).astype(jnp.float32)
    factor = lax.rsqrt(jnp.mean(values * values, axis=-1, keepdims=True) + EPSILON)
    scaled = (values * gain).astype(jnp.bfloat16)

    def product(left, right):
        return jnp.dot(left, right, preferred_element_type=jnp.float32)

    affinity = jax.nn.sigmoid(product(scaled, router[0].T) * factor)
    experts = named[:, :, width : width + top].reshape(count * rows, top).astype(jnp.int32)
    hit = jnp.any(experts[:, :, None] == jnp.arange(EXPERTS, dtype=jnp.int32), axis=1)
    picked = jnp.where(hit, affinity, 0.0)
    gates = picked / jnp.sum(picked, axis=-1, keepdims=True)
    of_unit = (lax.axis_index("expert") * units + jnp.arange(units, dtype=jnp.int32)) // FF
    weight = jnp.take(gates, of_unit, axis=1)
    up_part = product(scaled, weights[1][0]) * (factor * weight)
    hidden = (jax.nn.silu(product(scaled, weights[0][0]) * factor) * up_part).astype(jnp.bfloat16)
    out = product(hidden, weights[2][0]).astype(jnp.bfloat16)
    out = out.reshape(count, rows, CHUNKS, 2, width)
    out = jnp.where(lax.axis_index("section") == layer, out, jnp.zeros_like(out))
    parts = []
    for c in range(CHUNKS):
        left, right = out[:, :, c, 0], out[:, :, c, 1]
        parts += [jnp.where(first, right, left)[back], jnp.where(first, left, right)]
    return parts


def fetch(place, arena, loads, after, token):
    def body(ins, outs, scratch, memory, start, wait):
        for load in loads:
            start(load)

    return call(body, None, place, arena, [], [], [], loads, "fetch", after=after, token=token)


def local(tokens, routes, norm_gain, router_weight, gate_weight, up_weight, down_weight):
    count = lax.axis_size("expert")
    micro, rows, model_width = tokens.shape
    width = model_width // (2 * CHUNKS)
    top = routes.shape[-1]
    section = lax.axis_index("section")
    first = section == 0
    deepest = count.bit_length() - 2
    router = jnp.swapaxes(router_weight, 1, 2)
    weights = (gate_weight, up_weight, down_weight)
    held = count * micro * rows <= 2 * LANES
    place = Arena(weights, width, 6, 62 * MIB)

    def partials(layer, pairs):
        nonlocal arena
        if held:
            parts, arena = run_layer(layer, place, arena, pairs, norm_gain, router, named, top)
        else:
            parts = run_layer_plainly(layer, weights, pairs, norm_gain, router, named, top)
        moved = [swap(parts[2 * c]) for c in range(CHUNKS)]
        return [add(parts[2 * c + 1], moved[c]).astype(jnp.bfloat16) for c in range(CHUNKS)]

    gathered = list(prepare(tokens, jnp.swapaxes(routes, 2, 3), width))
    arena = None
    loads = list(range(place.slots))
    for level in reversed(range(deepest + 1)):
        received = [exchange(value, level) for value in gathered]
        if held:
            todo, loads = (loads[:2], loads[2:]) if level > 0 else (loads, [])
            arena, token = fetch(place, arena, todo, gathered[0], received[0].shape[1:])
            received[0] = after_token(received[0], token)
        gathered = [jnp.concatenate(pair, axis=0) for pair in zip(gathered, received)]
    named = gathered[0]
    moved = partials(0, [(value, swap(value)) for value in gathered])

    after = list(moved)
    for level in range(deepest):
        for c in range(CHUNKS):
            half = after[c].shape[0] // 2
            received = exchange(after[c][half:], level)
            after[c] = add(after[c][:half], received).astype(jnp.bfloat16)
    for c in range(CHUNKS):
        value = add(after[c], jnp.flip(exchange(after[c], deepest), axis=0))
        residual = gathered[c][:2, :, :width].astype(jnp.float32)
        after[c] = (residual + value).astype(jnp.bfloat16)
    own_after = [value[:1] for value in after]
    for level in reversed(range(deepest)):
        for c in range(CHUNKS):
            after[c] = jnp.concatenate([after[c], exchange(after[c], level)], axis=0)
    sums = partials(1, [(value, swap(value)) for value in after])
    results = []
    for c in range(CHUNKS):
        value, _ = reduce_to(sums[c], 1)
        value = (own_after[c].astype(jnp.float32) + value).astype(jnp.bfloat16)
        results.append(value.reshape(micro, rows, width))
    result = jnp.stack(results, axis=2)
    keep = jnp.where(first, result[0], result[1])
    received = swap(jnp.where(first, result[1], result[0]))
    both = jnp.where(
        first, jnp.stack([keep, received], axis=2), jnp.stack([received, keep], axis=2)
    )
    return both.reshape(1, rows, model_width)


def solution(mesh):
    placed = (
        P(None, ("groups", "expert"), None),
        P("section", None, ("groups", "expert"), None),
        P("section", None),
        P("section", None, None),
        P("section", None, "expert"),
        P("section", None, "expert"),
        P("section", "expert", None),
    )
    return jax.shard_map(
        local,
        mesh=mesh,
        in_specs=placed,
        out_specs=P("section", ("groups", "expert"), None),
        check_vma=False,
    )
```

profile of v0, /device:TPU:0, one launch (start us, length us, event | category | flops | bytes accessed | tf_op | source)
XLA Modules:
  0.0 148.5 jit_solution(7399520437282279769)
XLA Ops:
  0.0 1.7 %prepare.1 = (bf16[1,16,1920]{2,1,0:T(8,128)(2,1)}, bf16[1,16,1792]{2,1,0:T(8,128)(2,1)}) custom-call(bf16[2,8,7168]{2,1,0:T(8,128)(2,1)} %tokens_ref.1, s32[1,2,4,8]{3,2,1,0:T(4,128)} %bitcast.29), custom_call_target="tpu_custom_call" | custom-call | tf_op jit(solution)/shard_map/prepare/pallas_call | solution.py:198
  1.7 4.0 %collective-permute-start = (bf16[1,16,1920]{2,1,0:T(8,128)(2,1)}, bf16[1,16,1920]{2,1,0:T(8,128)(2,1)S(1)}, u32[]{:S(2)}, u32[]{:S(2)}) collective-permute-start(bf16[1,16,1920]{2,1,0:T(8,128)(2,1)} %get-tuple-element.22.refs_3_), channel_id=1, source_target_pairs={{0,8},{1,9},{2,10},{3,11},{4,12},{5,13},{6,14},{7,15},{8,0},{9,1},... | collective-permute-start | bytes 184328 | tf_op jit(solution)/shard_map/ppermute | solution.py:43
  5.7 0.9 constant_dynamic-update-slice_fusion.1
  6.6 6.4 %fetch.3 = (bf16[86016,256]{1,0:T(8,128)(2,1)S(1)}, bf16[16,1920]{1,0:T(8,128)(2,1)S(1)}) custom-call(bf16[1,7168,2048]{2,1,0:T(8,128)(2,1)} %refs_7_.3, bf16[1,7168,2048]{2,1,0:T(8,128)(2,1)} %refs_8_.3, bf16[1,2048,7168]{2,1,0:T(8,128)(2,1)} %refs_9_.3, bf16[1,16,1920]{2,1,0:T(8,128)(2,1)} %get-tuple-element.22.refs_3_), custom_call_target="tpu_custom_call" | custom-call | bytes 14680064 | tf_op jit(solution)/shard_map/fetch/pallas_call | solution.py:155
  13.1 1.9 %collective-permute-start.1 = (bf16[2,16,1920]{2,1,0:T(8,128)(2,1)S(1)}, bf16[2,16,1920]{2,1,0:T(8,128)(2,1)S(1)}, u32[]{:S(2)}, u32[]{:S(2)}) collective-permute-start(bf16[2,16,1920]{2,1,0:T(8,128)(2,1)S(1)} %pad_maximum_fusion.7.refs_3_), channel_id=1, source_target_pairs={{0,4},{1,3},{2,6},{3,1},{4,0},{5,7},{6,2},{7,5},{8,12},{9,11},{10,... | collective-permute-start | bytes 368648 | tf_op jit(solution)/shard_map/ppermute | solution.py:43
  15.3 6.5 %fetch.4 = (bf16[86016,256]{1,0:T(8,128)(2,1)S(1)}, bf16[16,1920]{1,0:T(8,128)(2,1)S(1)}) custom-call(bf16[1,7168,2048]{2,1,0:T(8,128)(2,1)} %refs_7_.3, bf16[1,7168,2048]{2,1,0:T(8,128)(2,1)} %refs_8_.3, bf16[1,2048,7168]{2,1,0:T(8,128)(2,1)} %refs_9_.3, bf16[2,16,1920]{2,1,0:T(8,128)(2,1)} %copy-done.7, ...), custom_call_target="tpu_custom_call", output_to_operand_aliasing={{0}: (4, {})} | custom-call | bytes 14680064 | tf_op jit(solution)/shard_map/fetch/pallas_call | solution.py:155
  21.8 1.9 %collective-permute-start.2 = (bf16[4,16,1920]{2,1,0:T(8,128)(2,1)S(1)}, bf16[4,16,1920]{2,1,0:T(8,128)(2,1)S(1)}, u32[]{:S(2)}, u32[]{:S(2)}) collective-permute-start(bf16[4,16,1920]{2,1,0:T(8,128)(2,1)S(1)} %pad_maximum_fusion.3.refs_3_), channel_id=1, source_target_pairs={{0,2},{1,5},{2,0},{3,7},{4,6},{5,1},{6,4},{7,3},{8,10},{9,13},{10,... | collective-permute-start | bytes 737288 | tf_op jit(solution)/shard_map/ppermute | solution.py:43
  24.1 6.5 %fetch.5 = (bf16[86016,256]{1,0:T(8,128)(2,1)S(1)}, bf16[16,1920]{1,0:T(8,128)(2,1)S(1)}) custom-call(bf16[1,7168,2048]{2,1,0:T(8,128)(2,1)} %refs_7_.3, bf16[1,7168,2048]{2,1,0:T(8,128)(2,1)} %refs_8_.3, bf16[1,2048,7168]{2,1,0:T(8,128)(2,1)} %refs_9_.3, bf16[4,16,1920]{2,1,0:T(8,128)(2,1)} %copy-done.4, ...), custom_call_target="tpu_custom_call", output_to_operand_aliasing={{0}: (4, {})} | custom-call | bytes 14680064 | tf_op jit(solution)/shard_map/fetch/pallas_call | solution.py:155
  30.8 1.0 constant_dynamic-update-slice_fusion.2.refs_2_
  32.3 1.4 collective-permute-done.7.refs_3_
  33.8 0.8 copy-done.10
  34.7 22.8 %layer.2 = (bf16[8,16,1792]{2,1,0:T(8,128)(2,1)}, bf16[8,16,1792]{2,1,0:T(8,128)(2,1)}, bf16[8,16,1792]{2,1,0:T(8,128)(2,1)}, bf16[8,16,1792]{2,1,0:T(8,128)(2,1)}, bf16[86016,256]{1,0:T(8,128)(2,1)S(1)}) custom-call(bf16[8,16,1920]{2,1,0:T(8,128)(2,1)} %copy-done, bf16[8,16,1920]{2,1,0:T(8,128)(2,1)} %copy-done.6, ...), custom_call_target="tpu_custom_call", output_to_operand_aliasing={{4}: (10, {})} | custom-call | bytes 44040192 | tf_op jit(solution)/shard_map/layer/pallas_call | solution.py:155
  58.1 1.5 %collective-permute-done.15 = bf16[8,16,1792]{2,1,0:T(8,128)(2,1)S(1)} collective-permute-done((bf16[8,16,1792]{2,1,0:T(8,128)(2,1)}, bf16[8,16,1792]{2,1,0:T(8,128)(2,1)S(1)}, u32[]{:S(2)}, u32[]{:S(2)}) %collective-permute-start.15) | collective-permute-done | bytes 458784 | tf_op jit(solution)/shard_map/ppermute | solution.py:47
  59.7 1.1 add_convert_fusion.2
  60.8 1.9 %collective-permute-start.16 = (bf16[4,16,1792]{2,1,0:T(8,128)(2,1)S(1)}, bf16[4,16,1792]{2,1,0:T(8,128)(2,1)S(1)}, u32[]{:S(2)}, u32[]{:S(2)}) collective-permute-start(bf16[4,16,1792]{2,1,0:T(8,128)(2,1)S(1)} %slice.110), channel_id=1, source_target_pairs={{0,2},{1,5},{2,0},{3,7},{4,6},{5,1},{6,4},{7,3},{8,10},{9,13},{10,... | collective-permute-start | bytes 688136 | tf_op jit(solution)/shard_map/ppermute | solution.py:43
  62.7 1.1 add_convert_fusion.3
  64.1 2.8 %collective-permute-done.16 = bf16[4,16,1792]{2,1,0:T(8,128)(2,1)S(1)} collective-permute-done((bf16[4,16,1792]{2,1,0:T(8,128)(2,1)S(1)}, bf16[4,16,1792]{2,1,0:T(8,128)(2,1)S(1)}, u32[]{:S(2)}, u32[]{:S(2)}) %collective-permute-start.16) | collective-permute-done | bytes 229408 | tf_op jit(solution)/shard_map/ppermute | solution.py:43
  67.0 1.9 %collective-permute-start.17 = (bf16[2,16,1792]{2,1,0:T(8,128)(2,1)S(1)}, bf16[2,16,1792]{2,1,0:T(8,128)(2,1)S(1)}, u32[]{:S(2)}, u32[]{:S(2)}) collective-permute-start(bf16[2,16,1792]{2,1,0:T(8,128)(2,1)S(1)} %slice.112), channel_id=1, source_target_pairs={{0,4},{1,3},{2,6},{3,1},{4,0},{5,7},{6,2},{7,5},{8,12},{9,11},{10,... | collective-permute-start | bytes 344072 | tf_op jit(solution)/shard_map/ppermute | solution.py:43
  68.9 1.8 %collective-permute-done.9 = bf16[4,16,1792]{2,1,0:T(8,128)(2,1)S(1)} collective-permute-done((bf16[4,16,1792]{2,1,0:T(8,128)(2,1)S(1)}, bf16[4,16,1792]{2,1,0:T(8,128)(2,1)S(1)}, u32[]{:S(2)}, u32[]{:S(2)}) %collective-permute-start.9) | collective-permute-done | bytes 229408 | tf_op jit(solution)/shard_map/ppermute | solution.py:43
  70.8 1.5 collective-permute-start.10
  72.3 2.7 %collective-permute-start.18 = (bf16[2,16,1792]{2,1,0:T(8,128)(2,1)S(1)}, bf16[2,16,1792]{2,1,0:T(8,128)(2,1)S(1)}, u32[]{:S(2)}, u32[]{:S(2)}) collective-permute-start(bf16[2,16,1792]{2,1,0:T(8,128)(2,1)S(1)} %add_convert_fusion.11), channel_id=1, source_target_pairs={{0,8},{1,9},{2,10},{3,11},{4,12},{5,13},{6,14},{7,15},{8,0},{9,1},... | collective-permute-start | bytes 344072 | tf_op jit(solution)/shard_map/ppermute | solution.py:43
  75.0 2.0 %collective-permute-done.10 = bf16[2,16,1792]{2,1,0:T(8,128)(2,1)S(1)} collective-permute-done((bf16[2,16,1792]{2,1,0:T(8,128)(2,1)S(1)}, bf16[2,16,1792]{2,1,0:T(8,128)(2,1)S(1)}, u32[]{:S(2)}, u32[]{:S(2)}) %collective-permute-start.10) | collective-permute-done | bytes 114720 | tf_op jit(solution)/shard_map/ppermute | solution.py:43
  76.9 2.0 %collective-permute-start.11 = (bf16[2,16,1792]{2,1,0:T(8,128)(2,1)S(1)}, bf16[2,16,1792]{2,1,0:T(8,128)(2,1)S(1)}, u32[]{:S(2)}, u32[]{:S(2)}) collective-permute-start(bf16[2,16,1792]{2,1,0:T(8,128)(2,1)S(1)} %add_convert_fusion.13), channel_id=1, source_target_pairs={{0,8},{1,9},{2,10},{3,11},{4,12},{5,13},{6,14},{7,15},{8,0},{9,1},... | collective-permute-start | bytes 344072 | tf_op jit(solution)/shard_map/ppermute | solution.py:43
  79.0 4.3 %collective-permute-done.18 = bf16[2,16,1792]{2,1,0:T(8,128)(2,1)S(1)} collective-permute-done((bf16[2,16,1792]{2,1,0:T(8,128)(2,1)S(1)}, bf16[2,16,1792]{2,1,0:T(8,128)(2,1)S(1)}, u32[]{:S(2)}, u32[]{:S(2)}) %collective-permute-start.18) | collective-permute-done | bytes 114720 | tf_op jit(solution)/shard_map/ppermute | solution.py:43
  83.6 1.2 collective-permute-done.11
  85.6 3.6 %collective-permute-done.19 = bf16[2,16,1792]{2,1,0:T(8,128)(2,1)S(1)} collective-permute-done((bf16[2,16,1792]{2,1,0:T(8,128)(2,1)S(1)}, bf16[2,16,1792]{2,1,0:T(8,128)(2,1)S(1)}, u32[]{:S(2)}, u32[]{:S(2)}) %collective-permute-start.19) | collective-permute-done | bytes 114720 | tf_op jit(solution)/shard_map/ppermute | solution.py:43
  89.2 1.6 %collective-permute-start.20 = (bf16[4,16,1792]{2,1,0:T(8,128)(2,1)S(1)}, bf16[4,16,1792]{2,1,0:T(8,128)(2,1)S(1)}, u32[]{:S(2)}, u32[]{:S(2)}) collective-permute-start(bf16[4,16,1792]{2,1,0:T(8,128)(2,1)S(1)} %pad_maximum_fusion.6), channel_id=1, source_target_pairs={{0,2},{1,5},{2,0},{3,7},{4,6},{5,1},{6,4},{7,3},{8,10},{9,13},{10,... | collective-permute-start | bytes 688136 | tf_op jit(solution)/shard_map/ppermute | solution.py:43
  90.8 0.8 collective-permute-done.12
  91.6 1.6 %collective-permute-start.13 = (bf16[4,16,1792]{2,1,0:T(8,128)(2,1)S(1)}, bf16[4,16,1792]{2,1,0:T(8,128)(2,1)S(1)}, u32[]{:S(2)}, u32[]{:S(2)}) collective-permute-start(bf16[4,16,1792]{2,1,0:T(8,128)(2,1)S(1)} %pad_maximum_fusion.5), channel_id=1, source_target_pairs={{0,2},{1,5},{2,0},{3,7},{4,6},{5,1},{6,4},{7,3},{8,10},{9,13},{10,... | collective-permute-start | bytes 688136 | tf_op jit(solution)/shard_map/ppermute | solution.py:43
  93.3 2.0 %collective-permute-done.20 = bf16[4,16,1792]{2,1,0:T(8,128)(2,1)S(1)} collective-permute-done((bf16[4,16,1792]{2,1,0:T(8,128)(2,1)S(1)}, bf16[4,16,1792]{2,1,0:T(8,128)(2,1)S(1)}, u32[]{:S(2)}, u32[]{:S(2)}) %collective-permute-start.20) | collective-permute-done | bytes 229408 | tf_op jit(solution)/shard_map/ppermute | solution.py:43
  95.4 2.3 %collective-permute-done.13 = bf16[4,16,1792]{2,1,0:T(8,128)(2,1)S(1)} collective-permute-done((bf16[4,16,1792]{2,1,0:T(8,128)(2,1)S(1)}, bf16[4,16,1792]{2,1,0:T(8,128)(2,1)S(1)}, u32[]{:S(2)}, u32[]{:S(2)}) %collective-permute-start.13) | collective-permute-done | bytes 229408 | tf_op jit(solution)/shard_map/ppermute | solution.py:43
  97.9 1.8 %collective-permute-done.14.refs_1_ = bf16[8,16,1792]{2,1,0:T(8,128)(2,1)S(1)} collective-permute-done((bf16[8,16,1792]{2,1,0:T(8,128)(2,1)S(1)}, bf16[8,16,1792]{2,1,0:T(8,128)(2,1)S(1)}, u32[]{:S(2)}, u32[]{:S(2)}) %collective-permute-start.14) | collective-permute-done | bytes 458784 | tf_op jit(solution)/shard_map/ppermute | solution.py:47
  99.7 0.8 copy-done.9
  100.5 3.3 %layer.3 = (bf16[8,16,1792]{2,1,0:T(8,128)(2,1)}, bf16[8,16,1792]{2,1,0:T(8,128)(2,1)}, bf16[8,16,1792]{2,1,0:T(8,128)(2,1)}, bf16[8,16,1792]{2,1,0:T(8,128)(2,1)}, bf16[86016,256]{1,0:T(8,128)(2,1)S(1)}) custom-call(bf16[8,16,1792]{2,1,0:T(8,128)(2,1)} %copy-done.2, bf16[8,16,1792]{2,1,0:T(8,128)(2,1)} %copy-done.9, ...), custom_call_target="tpu_custom_call", output_to_operand_aliasing={{4}: (10, {})} | custom-call | bytes 44040192 | tf_op jit(solution)/shard_map/layer/pallas_call | solution.py:155
  103.8 19.8 %collective-permute-start.22 = (bf16[8,16,1792]{2,1,0:T(8,128)(2,1)}, bf16[8,16,1792]{2,1,0:T(8,128)(2,1)S(1)}, u32[]{:S(2)}, u32[]{:S(2)}) collective-permute-start(bf16[8,16,1792]{2,1,0:T(8,128)(2,1)} %get-tuple-element.36), channel_id=1, source_target_pairs={{0,1},{1,0},{2,3},{3,2},{4,5},{5,4},{6,7},{7,6},{8,9},{9,8},{10,11... | collective-permute-start | bytes 1376264 | tf_op jit(solution)/shard_map/ppermute | solution.py:47
  123.7 1.6 %collective-permute-done.22 = bf16[8,16,1792]{2,1,0:T(8,128)(2,1)S(1)} collective-permute-done((bf16[8,16,1792]{2,1,0:T(8,128)(2,1)}, bf16[8,16,1792]{2,1,0:T(8,128)(2,1)S(1)}, u32[]{:S(2)}, u32[]{:S(2)}) %collective-permute-start.22) | collective-permute-done | bytes 458784 | tf_op jit(solution)/shard_map/ppermute | solution.py:47
  125.2 1.1 add_convert_fusion.1
  126.4 1.6 %collective-permute-start.23 = (bf16[4,16,1792]{2,1,0:T(8,128)(2,1)S(1)}, bf16[4,16,1792]{2,1,0:T(8,128)(2,1)S(1)}, u32[]{:S(2)}, u32[]{:S(2)}) collective-permute-start(bf16[4,16,1792]{2,1,0:T(8,128)(2,1)S(1)} %slice.114), channel_id=1, source_target_pairs={{0,2},{1,5},{2,0},{3,7},{4,6},{5,1},{6,4},{7,3},{8,10},{9,13},{10,... | collective-permute-start | bytes 688136 | tf_op jit(solution)/shard_map/ppermute | solution.py:43
  128.0 1.1 add_convert_fusion
  129.7 2.8 %collective-permute-done.23 = bf16[4,16,1792]{2,1,0:T(8,128)(2,1)S(1)} collective-permute-done((bf16[4,16,1792]{2,1,0:T(8,128)(2,1)S(1)}, bf16[4,16,1792]{2,1,0:T(8,128)(2,1)S(1)}, u32[]{:S(2)}, u32[]{:S(2)}) %collective-permute-start.23) | collective-permute-done | bytes 229408 | tf_op jit(solution)/shard_map/ppermute | solution.py:43
  132.6 3.1 %collective-permute-done.27 = bf16[4,16,1792]{2,1,0:T(8,128)(2,1)S(1)} collective-permute-done((bf16[4,16,1792]{2,1,0:T(8,128)(2,1)S(1)}, bf16[4,16,1792]{2,1,0:T(8,128)(2,1)S(1)}, u32[]{:S(2)}, u32[]{:S(2)}) %collective-permute-start.27) | collective-permute-done | bytes 229408 | tf_op jit(solution)/shard_map/ppermute | solution.py:43
  135.9 1.5 %collective-permute-done.24 = bf16[2,16,1792]{2,1,0:T(8,128)(2,1)S(1)} collective-permute-done((bf16[2,16,1792]{2,1,0:T(8,128)(2,1)S(1)}, bf16[2,16,1792]{2,1,0:T(8,128)(2,1)S(1)}, u32[]{:S(2)}, u32[]{:S(2)}) %collective-permute-start.24) | collective-permute-done | bytes 114720 | tf_op jit(solution)/shard_map/ppermute | solution.py:43
  137.5 1.7 %collective-permute-start.25 = (bf16[1,16,1792]{2,1,0:T(8,128)(2,1)S(1)}, bf16[1,16,1792]{2,1,0:T(8,128)(2,1)S(1)}, u32[]{:S(2)}, u32[]{:S(2)}) collective-permute-start(bf16[1,16,1792]{2,1,0:T(8,128)(2,1)S(1)} %slice.118), channel_id=1, source_target_pairs={{0,8},{1,9},{2,10},{3,11},{4,12},{5,13},{6,14},{7,15},{8,0},{9,1},... | collective-permute-start | bytes 172040 | tf_op jit(solution)/shard_map/ppermute | solution.py:43
  139.1 2.2 %collective-permute-done.28 = bf16[2,16,1792]{2,1,0:T(8,128)(2,1)S(1)} collective-permute-done((bf16[2,16,1792]{2,1,0:T(8,128)(2,1)S(1)}, bf16[2,16,1792]{2,1,0:T(8,128)(2,1)S(1)}, u32[]{:S(2)}, u32[]{:S(2)}) %collective-permute-start.28) | collective-permute-done | bytes 114720 | tf_op jit(solution)/shard_map/ppermute | solution.py:43
  141.3 0.9 collective-permute-start.29
  142.2 2.1 %collective-permute-done.25 = bf16[1,16,1792]{2,1,0:T(8,128)(2,1)S(1)} collective-permute-done((bf16[1,16,1792]{2,1,0:T(8,128)(2,1)S(1)}, bf16[1,16,1792]{2,1,0:T(8,128)(2,1)S(1)}, u32[]{:S(2)}, u32[]{:S(2)}) %collective-permute-start.25) | collective-permute-done | bytes 57376 | tf_op jit(solution)/shard_map/ppermute | solution.py:43
  144.3 2.2 %collective-permute-done.29 = bf16[1,16,1792]{2,1,0:T(8,128)(2,1)S(1)} collective-permute-done((bf16[1,16,1792]{2,1,0:T(8,128)(2,1)S(1)}, bf16[1,16,1792]{2,1,0:T(8,128)(2,1)S(1)}, u32[]{:S(2)}, u32[]{:S(2)}) %collective-permute-start.29) | collective-permute-done | bytes 57376 | tf_op jit(solution)/shard_map/ppermute | solution.py:43
  146.6 1.2 collective-permute-done.30
  (89 shorter events, 5.8 us)
Async XLA Ops:
  1.7 11.4 %collective-permute-start = (bf16[1,16,1920]{2,1,0:T(8,128)(2,1)}, bf16[1,16,1920]{2,1,0:T(8,128)(2,1)S(1)}, u32[]{:S(2)}, u32[]{:S(2)}) collective-permute-start(bf16[1,16,1920]{2,1,0:T(8,128)(2,1)} %get-tuple-element.22.refs_3_), channel_id=1, source_target_pairs={{0,8},{1,9},{2,10},{3,11},{4,12},{5,13},{6,14},{7,15},{8,0},{9,1},... | collective-permute-start | bytes 184328 | tf_op jit(solution)/shard_map/ppermute | solution.py:43
  5.7 9.4 %collective-permute-start.4 = (bf16[1,16,1792]{2,1,0:T(8,128)(2,1)}, bf16[1,16,1792]{2,1,0:T(8,128)(2,1)S(1)}, u32[]{:S(2)}, u32[]{:S(2)}) collective-permute-start(bf16[1,16,1792]{2,1,0:T(8,128)(2,1)} %get-tuple-element.28), channel_id=1, source_target_pairs={{0,8},{1,9},{2,10},{3,11},{4,12},{5,13},{6,14},{7,15},{8,0},{9,1},... | collective-permute-start | bytes 172040 | tf_op jit(solution)/shard_map/ppermute | solution.py:43
  6.6 6.5 %copy-start.3 = (bf16[1,16,1920]{2,1,0:T(8,128)(2,1)S(1)}, bf16[1,16,1920]{2,1,0:T(8,128)(2,1)}, u32[]{:S(2)}) copy-start(bf16[1,16,1920]{2,1,0:T(8,128)(2,1)} %get-tuple-element.22.refs_3_) | copy-start | bytes 184324
  13.1 2.2 %copy-start.7 = (bf16[2,16,1920]{2,1,0:T(8,128)(2,1)}, bf16[2,16,1920]{2,1,0:T(8,128)(2,1)S(1)}, u32[]{:S(2)}) copy-start(bf16[2,16,1920]{2,1,0:T(8,128)(2,1)S(1)} %pad_maximum_fusion.7.refs_3_) | copy-start | bytes 368644
  13.1 8.6 %collective-permute-start.1 = (bf16[2,16,1920]{2,1,0:T(8,128)(2,1)S(1)}, bf16[2,16,1920]{2,1,0:T(8,128)(2,1)S(1)}, u32[]{:S(2)}, u32[]{:S(2)}) collective-permute-start(bf16[2,16,1920]{2,1,0:T(8,128)(2,1)S(1)} %pad_maximum_fusion.7.refs_3_), channel_id=1, source_target_pairs={{0,4},{1,3},{2,6},{3,1},{4,0},{5,7},{6,2},{7,5},{8,12},{9,11},{10,... | collective-permute-start | bytes 368648 | tf_op jit(solution)/shard_map/ppermute | solution.py:43
  15.1 8.6 %collective-permute-start.5 = (bf16[2,16,1792]{2,1,0:T(8,128)(2,1)S(1)}, bf16[2,16,1792]{2,1,0:T(8,128)(2,1)S(1)}, u32[]{:S(2)}, u32[]{:S(2)}) collective-permute-start(bf16[2,16,1792]{2,1,0:T(8,128)(2,1)S(1)} %get-tuple-element.39), channel_id=1, source_target_pairs={{0,4},{1,3},{2,6},{3,1},{4,0},{5,7},{6,2},{7,5},{8,12},{9,11},{10,... | collective-permute-start | bytes 344072 | tf_op jit(solution)/shard_map/ppermute | solution.py:43
  15.3 8.4 %copy-start.11 = (bf16[1,16,1792]{2,1,0:T(8,128)(2,1)S(1)}, bf16[1,16,1792]{2,1,0:T(8,128)(2,1)}, u32[]{:S(2)}) copy-start(bf16[1,16,1792]{2,1,0:T(8,128)(2,1)} %get-tuple-element.28) | copy-start | bytes 172036
  21.8 2.2 %copy-start.4 = (bf16[4,16,1920]{2,1,0:T(8,128)(2,1)}, bf16[4,16,1920]{2,1,0:T(8,128)(2,1)S(1)}, u32[]{:S(2)}) copy-start(bf16[4,16,1920]{2,1,0:T(8,128)(2,1)S(1)} %pad_maximum_fusion.3.refs_3_) | copy-start | bytes 737284
  21.8 8.7 %collective-permute-start.2 = (bf16[4,16,1920]{2,1,0:T(8,128)(2,1)S(1)}, bf16[4,16,1920]{2,1,0:T(8,128)(2,1)S(1)}, u32[]{:S(2)}, u32[]{:S(2)}) collective-permute-start(bf16[4,16,1920]{2,1,0:T(8,128)(2,1)S(1)} %pad_maximum_fusion.3.refs_3_), channel_id=1, source_target_pairs={{0,2},{1,5},{2,0},{3,7},{4,6},{5,1},{6,4},{7,3},{8,10},{9,13},{10,... | collective-permute-start | bytes 737288 | tf_op jit(solution)/shard_map/ppermute | solution.py:43
  23.7 7.0 %collective-permute-start.6 = (bf16[4,16,1792]{2,1,0:T(8,128)(2,1)S(1)}, bf16[4,16,1792]{2,1,0:T(8,128)(2,1)}, u32[]{:S(2)}, u32[]{:S(2)}) collective-permute-start(bf16[4,16,1792]{2,1,0:T(8,128)(2,1)S(1)} %pad_maximum_fusion.4), channel_id=1, source_target_pairs={{0,2},{1,5},{2,0},{3,7},{4,6},{5,1},{6,4},{7,3},{8,10},{9,13},{10,... | collective-permute-start | bytes 688136 | tf_op jit(solution)/shard_map/ppermute | solution.py:43
  30.7 3.9 %copy-start = (bf16[8,16,1920]{2,1,0:T(8,128)(2,1)}, bf16[8,16,1920]{2,1,0:T(8,128)(2,1)S(1)}, u32[]{:S(2)}) copy-start(bf16[8,16,1920]{2,1,0:T(8,128)(2,1)S(1)} %pad_maximum_fusion.refs_0_.refs_6_) | copy-start | bytes 1474564
  30.7 3.1 %collective-permute-start.3 = (bf16[8,16,1920]{2,1,0:T(8,128)(2,1)S(1)}, bf16[8,16,1920]{2,1,0:T(8,128)(2,1)S(1)}, u32[]{:S(2)}, u32[]{:S(2)}) collective-permute-start(bf16[8,16,1920]{2,1,0:T(8,128)(2,1)S(1)} %pad_maximum_fusion.refs_0_.refs_6_), channel_id=1, source_target_pairs={{0,1},{1,0},{2,3},{3,2},{4,5},{5,4},{6,7},{7,6},{8,9},{9,8},{10,11... | collective-permute-start | bytes 1474568 | tf_op jit(solution)/shard_map/ppermute | solution.py:47
  31.8 2.7 %copy-start.5 = (bf16[8,16,1792]{2,1,0:T(8,128)(2,1)}, bf16[8,16,1792]{2,1,0:T(8,128)(2,1)S(1)}, u32[]{:S(2)}) copy-start(bf16[8,16,1792]{2,1,0:T(8,128)(2,1)S(1)} %constant_dynamic-update-slice_fusion.2.refs_2_) | copy-start | bytes 1376260
  31.8 1.9 %collective-permute-start.7 = (bf16[8,16,1792]{2,1,0:T(8,128)(2,1)S(1)}, bf16[8,16,1792]{2,1,0:T(8,128)(2,1)S(1)}, u32[]{:S(2)}, u32[]{:S(2)}) collective-permute-start(bf16[8,16,1792]{2,1,0:T(8,128)(2,1)S(1)} %constant_dynamic-update-slice_fusion.2.refs_2_), channel_id=1, source_target_pairs={{0,1},{1,0},{2,3},{3,2},{4,5},{5,4},{6,7},{7,6},{8,9},{9,8},{10,11... | collective-permute-start | bytes 1376264 | tf_op jit(solution)/shard_map/ppermute | solution.py:47
  33.7 0.8 copy-start.10
  33.8 1.0 copy-start.6
  57.6 2.1 %collective-permute-start.15 = (bf16[8,16,1792]{2,1,0:T(8,128)(2,1)}, bf16[8,16,1792]{2,1,0:T(8,128)(2,1)S(1)}, u32[]{:S(2)}, u32[]{:S(2)}) collective-permute-start(bf16[8,16,1792]{2,1,0:T(8,128)(2,1)} %get-tuple-element.33), channel_id=1, source_target_pairs={{0,1},{1,0},{2,3},{3,2},{4,5},{5,4},{6,7},{7,6},{8,9},{9,8},{10,11... | collective-permute-start | bytes 1376264 | tf_op jit(solution)/shard_map/ppermute | solution.py:47
  57.7 5.0 %collective-permute-start.8 = (bf16[8,16,1792]{2,1,0:T(8,128)(2,1)}, bf16[8,16,1792]{2,1,0:T(8,128)(2,1)S(1)}, u32[]{:S(2)}, u32[]{:S(2)}) collective-permute-start(bf16[8,16,1792]{2,1,0:T(8,128)(2,1)} %get-tuple-element.31), channel_id=1, source_target_pairs={{0,1},{1,0},{2,3},{3,2},{4,5},{5,4},{6,7},{7,6},{8,9},{9,8},{10,11... | collective-permute-start | bytes 1376264 | tf_op jit(solution)/shard_map/ppermute | solution.py:47
  60.8 6.1 %collective-permute-start.16 = (bf16[4,16,1792]{2,1,0:T(8,128)(2,1)S(1)}, bf16[4,16,1792]{2,1,0:T(8,128)(2,1)S(1)}, u32[]{:S(2)}, u32[]{:S(2)}) collective-permute-start(bf16[4,16,1792]{2,1,0:T(8,128)(2,1)S(1)} %slice.110), channel_id=1, source_target_pairs={{0,2},{1,5},{2,0},{3,7},{4,6},{5,1},{6,4},{7,3},{8,10},{9,13},{10,... | collective-permute-start | bytes 688136 | tf_op jit(solution)/shard_map/ppermute | solution.py:43
  63.8 6.9 %collective-permute-start.9 = (bf16[4,16,1792]{2,1,0:T(8,128)(2,1)S(1)}, bf16[4,16,1792]{2,1,0:T(8,128)(2,1)S(1)}, u32[]{:S(2)}, u32[]{:S(2)}) collective-permute-start(bf16[4,16,1792]{2,1,0:T(8,128)(2,1)S(1)} %slice.105), channel_id=1, source_target_pairs={{0,2},{1,5},{2,0},{3,7},{4,6},{5,1},{6,4},{7,3},{8,10},{9,13},{10,... | collective-permute-start | bytes 688136 | tf_op jit(solution)/shard_map/ppermute | solution.py:43
  67.0 5.3 %collective-permute-start.17 = (bf16[2,16,1792]{2,1,0:T(8,128)(2,1)S(1)}, bf16[2,16,1792]{2,1,0:T(8,128)(2,1)S(1)}, u32[]{:S(2)}, u32[]{:S(2)}) collective-permute-start(bf16[2,16,1792]{2,1,0:T(8,128)(2,1)S(1)} %slice.112), channel_id=1, source_target_pairs={{0,4},{1,3},{2,6},{3,1},{4,0},{5,7},{6,2},{7,5},{8,12},{9,11},{10,... | collective-permute-start | bytes 344072 | tf_op jit(solution)/shard_map/ppermute | solution.py:43
  70.8 6.1 %collective-permute-start.10 = (bf16[2,16,1792]{2,1,0:T(8,128)(2,1)S(1)}, bf16[2,16,1792]{2,1,0:T(8,128)(2,1)S(1)}, u32[]{:S(2)}, u32[]{:S(2)}) collective-permute-start(bf16[2,16,1792]{2,1,0:T(8,128)(2,1)S(1)} %slice.107), channel_id=1, source_target_pairs={{0,4},{1,3},{2,6},{3,1},{4,0},{5,7},{6,2},{7,5},{8,12},{9,11},{10,... | collective-permute-start | bytes 344072 | tf_op jit(solution)/shard_map/ppermute | solution.py:43
  72.3 11.0 %collective-permute-start.18 = (bf16[2,16,1792]{2,1,0:T(8,128)(2,1)S(1)}, bf16[2,16,1792]{2,1,0:T(8,128)(2,1)S(1)}, u32[]{:S(2)}, u32[]{:S(2)}) collective-permute-start(bf16[2,16,1792]{2,1,0:T(8,128)(2,1)S(1)} %add_convert_fusion.11), channel_id=1, source_target_pairs={{0,8},{1,9},{2,10},{3,11},{4,12},{5,13},{6,14},{7,15},{8,0},{9,1},... | collective-permute-start | bytes 344072 | tf_op jit(solution)/shard_map/ppermute | solution.py:43
  76.9 7.8 %collective-permute-start.11 = (bf16[2,16,1792]{2,1,0:T(8,128)(2,1)S(1)}, bf16[2,16,1792]{2,1,0:T(8,128)(2,1)S(1)}, u32[]{:S(2)}, u32[]{:S(2)}) collective-permute-start(bf16[2,16,1792]{2,1,0:T(8,128)(2,1)S(1)} %add_convert_fusion.13), channel_id=1, source_target_pairs={{0,8},{1,9},{2,10},{3,11},{4,12},{5,13},{6,14},{7,15},{8,0},{9,1},... | collective-permute-start | bytes 344072 | tf_op jit(solution)/shard_map/ppermute | solution.py:43
  83.4 5.8 %collective-permute-start.19 = (bf16[2,16,1792]{2,1,0:T(8,128)(2,1)S(1)}, bf16[2,16,1792]{2,1,0:T(8,128)(2,1)S(1)}, u32[]{:S(2)}, u32[]{:S(2)}) collective-permute-start(bf16[2,16,1792]{2,1,0:T(8,128)(2,1)S(1)} %add_convert_fusion.10), channel_id=1, source_target_pairs={{0,4},{1,3},{2,6},{3,1},{4,0},{5,7},{6,2},{7,5},{8,12},{9,11},{10,... | collective-permute-start | bytes 344072 | tf_op jit(solution)/shard_map/ppermute | solution.py:43
  84.8 6.8 %collective-permute-start.12 = (bf16[2,16,1792]{2,1,0:T(8,128)(2,1)S(1)}, bf16[2,16,1792]{2,1,0:T(8,128)(2,1)S(1)}, u32[]{:S(2)}, u32[]{:S(2)}) collective-permute-start(bf16[2,16,1792]{2,1,0:T(8,128)(2,1)S(1)} %add_convert_fusion.12), channel_id=1, source_target_pairs={{0,4},{1,3},{2,6},{3,1},{4,0},{5,7},{6,2},{7,5},{8,12},{9,11},{10,... | collective-permute-start | bytes 344072 | tf_op jit(solution)/shard_map/ppermute | solution.py:43
  89.2 6.1 %collective-permute-start.20 = (bf16[4,16,1792]{2,1,0:T(8,128)(2,1)S(1)}, bf16[4,16,1792]{2,1,0:T(8,128)(2,1)S(1)}, u32[]{:S(2)}, u32[]{:S(2)}) collective-permute-start(bf16[4,16,1792]{2,1,0:T(8,128)(2,1)S(1)} %pad_maximum_fusion.6), channel_id=1, source_target_pairs={{0,2},{1,5},{2,0},{3,7},{4,6},{5,1},{6,4},{7,3},{8,10},{9,13},{10,... | collective-permute-start | bytes 688136 | tf_op jit(solution)/shard_map/ppermute | solution.py:43
  91.6 6.1 %collective-permute-start.13 = (bf16[4,16,1792]{2,1,0:T(8,128)(2,1)S(1)}, bf16[4,16,1792]{2,1,0:T(8,128)(2,1)S(1)}, u32[]{:S(2)}, u32[]{:S(2)}) collective-permute-start(bf16[4,16,1792]{2,1,0:T(8,128)(2,1)S(1)} %pad_maximum_fusion.5), channel_id=1, source_target_pairs={{0,2},{1,5},{2,0},{3,7},{4,6},{5,1},{6,4},{7,3},{8,10},{9,13},{10,... | collective-permute-start | bytes 688136 | tf_op jit(solution)/shard_map/ppermute | solution.py:43
  95.3 5.1 %copy-start.1 = (bf16[8,16,1792]{2,1,0:T(8,128)(2,1)}, bf16[8,16,1792]{2,1,0:T(8,128)(2,1)S(1)}, u32[]{:S(2)}) copy-start(bf16[8,16,1792]{2,1,0:T(8,128)(2,1)S(1)} %pad_maximum_fusion.2.refs_2_) | copy-start | bytes 1376260
  95.3 2.5 %collective-permute-start.21 = (bf16[8,16,1792]{2,1,0:T(8,128)(2,1)S(1)}, bf16[8,16,1792]{2,1,0:T(8,128)(2,1)S(1)}, u32[]{:S(2)}, u32[]{:S(2)}) collective-permute-start(bf16[8,16,1792]{2,1,0:T(8,128)(2,1)S(1)} %pad_maximum_fusion.2.refs_2_), channel_id=1, source_target_pairs={{0,1},{1,0},{2,3},{3,2},{4,5},{5,4},{6,7},{7,6},{8,9},{9,8},{10,11... | collective-permute-start | bytes 1376264 | tf_op jit(solution)/shard_map/ppermute | solution.py:47
  97.8 2.7 %copy-start.2 = (bf16[8,16,1792]{2,1,0:T(8,128)(2,1)}, bf16[8,16,1792]{2,1,0:T(8,128)(2,1)S(1)}, u32[]{:S(2)}) copy-start(bf16[8,16,1792]{2,1,0:T(8,128)(2,1)S(1)} %pad_maximum_fusion.1.refs_0_) | copy-start | bytes 1376260
  97.8 1.9 %collective-permute-start.14 = (bf16[8,16,1792]{2,1,0:T(8,128)(2,1)S(1)}, bf16[8,16,1792]{2,1,0:T(8,128)(2,1)S(1)}, u32[]{:S(2)}, u32[]{:S(2)}) collective-permute-start(bf16[8,16,1792]{2,1,0:T(8,128)(2,1)S(1)} %pad_maximum_fusion.1.refs_0_), channel_id=1, source_target_pairs={{0,1},{1,0},{2,3},{3,2},{4,5},{5,4},{6,7},{7,6},{8,9},{9,8},{10,11... | collective-permute-start | bytes 1376264 | tf_op jit(solution)/shard_map/ppermute | solution.py:47
  97.9 2.6 %copy-start.8 = (bf16[8,16,1792]{2,1,0:T(8,128)(2,1)}, bf16[8,16,1792]{2,1,0:T(8,128)(2,1)S(1)}, u32[]{:S(2)}) copy-start(bf16[8,16,1792]{2,1,0:T(8,128)(2,1)S(1)} %collective-permute-done.21.refs_3_) | copy-start | bytes 1376260
  99.7 0.8 copy-start.9
  103.8 21.5 %collective-permute-start.22 = (bf16[8,16,1792]{2,1,0:T(8,128)(2,1)}, bf16[8,16,1792]{2,1,0:T(8,128)(2,1)S(1)}, u32[]{:S(2)}, u32[]{:S(2)}) collective-permute-start(bf16[8,16,1792]{2,1,0:T(8,128)(2,1)} %get-tuple-element.36), channel_id=1, source_target_pairs={{0,1},{1,0},{2,3},{3,2},{4,5},{5,4},{6,7},{7,6},{8,9},{9,8},{10,11... | collective-permute-start | bytes 1376264 | tf_op jit(solution)/shard_map/ppermute | solution.py:47
  123.6 4.4 %collective-permute-start.26 = (bf16[8,16,1792]{2,1,0:T(8,128)(2,1)}, bf16[8,16,1792]{2,1,0:T(8,128)(2,1)S(1)}, u32[]{:S(2)}, u32[]{:S(2)}) collective-permute-start(bf16[8,16,1792]{2,1,0:T(8,128)(2,1)} %get-tuple-element.38), channel_id=1, source_target_pairs={{0,1},{1,0},{2,3},{3,2},{4,5},{5,4},{6,7},{7,6},{8,9},{9,8},{10,11... | collective-permute-start | bytes 1376264 | tf_op jit(solution)/shard_map/ppermute | solution.py:47
  126.4 6.1 %collective-permute-start.23 = (bf16[4,16,1792]{2,1,0:T(8,128)(2,1)S(1)}, bf16[4,16,1792]{2,1,0:T(8,128)(2,1)S(1)}, u32[]{:S(2)}, u32[]{:S(2)}) collective-permute-start(bf16[4,16,1792]{2,1,0:T(8,128)(2,1)S(1)} %slice.114), channel_id=1, source_target_pairs={{0,2},{1,5},{2,0},{3,7},{4,6},{5,1},{6,4},{7,3},{8,10},{9,13},{10,... | collective-permute-start | bytes 688136 | tf_op jit(solution)/shard_map/ppermute | solution.py:43
  129.2 6.6 %collective-permute-start.27 = (bf16[4,16,1792]{2,1,0:T(8,128)(2,1)S(1)}, bf16[4,16,1792]{2,1,0:T(8,128)(2,1)S(1)}, u32[]{:S(2)}, u32[]{:S(2)}) collective-permute-start(bf16[4,16,1792]{2,1,0:T(8,128)(2,1)S(1)} %slice.121), channel_id=1, source_target_pairs={{0,2},{1,5},{2,0},{3,7},{4,6},{5,1},{6,4},{7,3},{8,10},{9,13},{10,... | collective-permute-start | bytes 688136 | tf_op jit(solution)/shard_map/ppermute | solution.py:43
  132.6 4.9 %collective-permute-start.24 = (bf16[2,16,1792]{2,1,0:T(8,128)(2,1)S(1)}, bf16[2,16,1792]{2,1,0:T(8,128)(2,1)S(1)}, u32[]{:S(2)}, u32[]{:S(2)}) collective-permute-start(bf16[2,16,1792]{2,1,0:T(8,128)(2,1)S(1)} %slice.116), channel_id=1, source_target_pairs={{0,4},{1,3},{2,6},{3,1},{4,0},{5,7},{6,2},{7,5},{8,12},{9,11},{10,... | collective-permute-start | bytes 344072 | tf_op jit(solution)/shard_map/ppermute | solution.py:43
  135.8 5.5 %collective-permute-start.28 = (bf16[2,16,1792]{2,1,0:T(8,128)(2,1)S(1)}, bf16[2,16,1792]{2,1,0:T(8,128)(2,1)S(1)}, u32[]{:S(2)}, u32[]{:S(2)}) collective-permute-start(bf16[2,16,1792]{2,1,0:T(8,128)(2,1)S(1)} %slice.123), channel_id=1, source_target_pairs={{0,4},{1,3},{2,6},{3,1},{4,0},{5,7},{6,2},{7,5},{8,12},{9,11},{10,... | collective-permute-start | bytes 344072 | tf_op jit(solution)/shard_map/ppermute | solution.py:43
  137.5 6.8 %collective-permute-start.25 = (bf16[1,16,1792]{2,1,0:T(8,128)(2,1)S(1)}, bf16[1,16,1792]{2,1,0:T(8,128)(2,1)S(1)}, u32[]{:S(2)}, u32[]{:S(2)}) collective-permute-start(bf16[1,16,1792]{2,1,0:T(8,128)(2,1)S(1)} %slice.118), channel_id=1, source_target_pairs={{0,8},{1,9},{2,10},{3,11},{4,12},{5,13},{6,14},{7,15},{8,0},{9,1},... | collective-permute-start | bytes 172040 | tf_op jit(solution)/shard_map/ppermute | solution.py:43
  141.3 5.1 %collective-permute-start.29 = (bf16[1,16,1792]{2,1,0:T(8,128)(2,1)S(1)}, bf16[1,16,1792]{2,1,0:T(8,128)(2,1)S(1)}, u32[]{:S(2)}, u32[]{:S(2)}) collective-permute-start(bf16[1,16,1792]{2,1,0:T(8,128)(2,1)S(1)} %slice.125), channel_id=1, source_target_pairs={{0,8},{1,9},{2,10},{3,11},{4,12},{5,13},{6,14},{7,15},{8,0},{9,1},... | collective-permute-start | bytes 172040 | tf_op jit(solution)/shard_map/ppermute | solution.py:43
  146.5 1.3 collective-permute-start.30
where the time goes:
time: 149 us
  starting transfers between devices  48.9 us (33%)
  Pallas kernels  47.2 us (32%)
  waiting for transfers between devices  42.1 us (28%)
  other arithmetic  5.39 us (4%)
  local copies, waits for them, and re-layouts  4.49 us (3%)
    pallas_call x5, Pallas kernels, call(): pl.pallas_call(kernel, in_specs=(specs or [IN_VMEM] * n_in) + [ANYWHERE]...  45.5 us
    ppermute x22, waiting for transfers between devices, exchange(): return lax.ppermute(value, ('expert', 'section'), pairs)  34.6 us
    ppermute x22, starting transfers between devices, exchange(): return lax.ppermute(value, ('expert', 'section'), pairs)  27.7 us
    ppermute x9, starting transfers between devices, swap(): return lax.ppermute(value, 'section', [(0, 1), (1, 0)])  21.2 us
    ppermute x9, waiting for transfers between devices, swap(): return lax.ppermute(value, 'section', [(0, 1), (1, 0)])  7.53 us
    convert_element_type x4, other arithmetic, partials(): add(parts[2 * c + 1], moved[c]).astype(jnp.bfloat16)  4.5 us
  transfers between devices with their start and end apart: 31, of which 20 were waited for; matrix products, arithmetic and copies ran while one was open for 5% of the time, Pallas kernels for 13%

commit v1 on v0

--- a/solution.py
+++ b/solution.py
@@ -12,7 +12,10 @@
 EPSILON = 1e-06
 CHUNKS = 2
 LANES = 128
-MIB = 1 << 20
+SLOTS = 6
+RESIDENT = 6
+FETCHES = (2, 2, 2)
+TOP = 60 << 20
 IN_VMEM = pl.BlockSpec(memory_space=pltpu.VMEM)
 ANYWHERE = pl.BlockSpec(memory_space=pl.ANY)
 
@@ -51,16 +54,17 @@
     return left.astype(jnp.float32) + right.astype(jnp.float32)
 
 
-def reduce_to(value, last):
-    level = 0
-    while value.shape[0] > last:
-        half = value.shape[0] // 2
-        received = exchange(value[half:], level)
-        value = add(value[:half], received)
-        if half > 1:
-            value = value.astype(jnp.bfloat16)
-        level += 1
-    return value, level
+def next_step(value, level):
+    half = value.shape[0] // 2
+    received = exchange(value[half:], level)
+    return add(value[:half], received).astype(jnp.bfloat16)
+
+
+def cross(value, flip, to_other):
+    count = lax.axis_size("expert")
+    bit = bit_orders(count)[0][-1] if flip else 0
+    pairs = [(2 * e + s, 2 * (e ^ bit) + (s ^ to_other)) for e in range(count) for s in range(2)]
+    return lax.ppermute(value, ("expert", "section"), pairs)
 
 
 def after_token(value, token):
@@ -68,7 +72,8 @@
 
 
 class Arena:
-    def __init__(self, weights, width, slots, top):
+    def __init__(self, weights, width, slots, resident, top):
+        self.resident = resident
         self.weights, self.width, self.slots = weights, width, slots
         self.units = weights[0].shape[2]
         self.blocks = weights[0].shape[1] // width
@@ -154,7 +159,7 @@
     moved = max(len(loads), 1) * place.slot_rows * place.tile * 2
     results = pl.pallas_call(
         kernel,
-        in_specs=(specs or [IN_VMEM] * n_in) + [ANYWHERE] * 3 + [IN_VMEM] * (len(extra) + len(held)),
+        in_specs=(specs or [IN_VMEM] * n_in) + [ANYWHERE] * (3 + len(extra)) + [IN_VMEM] * len(held),
         out_specs=[IN_VMEM] * len(shapes),
         out_shape=shapes,
         input_output_aliases={n_in + 3 + len(extra): n_out} if held else {},
@@ -171,12 +176,12 @@
     top = routes.shape[2]
     block = micro * rows
 
-    def kernel(tokens_ref, routes_ref, *outs):
+    def kernel(tokens_ref, routes_ref, out):
         section = lax.axis_index("section")
         for c in range(CHUNKS):
             at = pl.multiple_of((2 * c + section) * width, LANES)
             both = [tokens_ref[m, :, pl.ds(at, width)].astype(jnp.float32) for m in range(micro)]
-            outs[c][0, :, :width] = jnp.concatenate(both, 0).astype(jnp.bfloat16)
+            out[0, :, c * width : (c + 1) * width] = jnp.concatenate(both, 0).astype(jnp.bfloat16)
         lane = lax.broadcasted_iota(jnp.int32, (rows, LANES), 1)
         eye = lax.broadcasted_iota(jnp.int32, (rows, rows), 0) == lax.broadcasted_iota(
             jnp.int32, (rows, rows), 1
@@ -189,24 +194,19 @@
                 column = jnp.sum(jnp.where(eye, line, 0.0), axis=1, keepdims=True)
                 value = jnp.where(lane == k, column, value)
             named.append(value)
-        outs[0][0, :, width:] = jnp.concatenate(named, 0).astype(jnp.bfloat16)
-
-    shapes = [
-        jax.ShapeDtypeStruct((1, block, width + (LANES if c == 0 else 0)), jnp.bfloat16)
-        for c in range(CHUNKS)
-    ]
+        out[0, :, CHUNKS * width :] = jnp.concatenate(named, 0).astype(jnp.bfloat16)
+
     return pl.pallas_call(
         kernel,
         in_specs=[IN_VMEM] * 2,
-        out_specs=[IN_VMEM] * CHUNKS,
-        out_shape=shapes,
+        out_specs=IN_VMEM,
+        out_shape=jax.ShapeDtypeStruct((1, block, CHUNKS * width + LANES), jnp.bfloat16),
         name="prepare",
     )(tokens, routes)
 
 
-def layer_body(place, top, ins, outs, scratch, memory, start, wait):
-    pairs = [ins[2 * c : 2 * c + 2] for c in range(CHUNKS)]
-    gain, router, named = ins[2 * CHUNKS :]
+def layer_body(place, top, together, ins, outs, scratch, memory, start, wait):
+    gain, router, named = ins[-3:]
     scaled, stats, gate_sum, up_sum, hidden, routes, sem = scratch
     count, rows, width = outs[0].shape
     tile, units, blocks = place.tile, place.units, place.blocks
@@ -214,8 +214,10 @@
     section = lax.axis_index("section")
     tables = swap_tables(count)
     lane = lax.broadcasted_iota(jnp.int32, (rows, LANES), 1)
-    bring = pltpu.make_async_copy(named.at[:, :, pl.ds(width, LANES)], routes, sem)
+    bring = pltpu.make_async_copy(named.at[:, :, pl.ds(CHUNKS * width, LANES)], routes, sem)
     bring.start()
+    for load in range(place.resident, place.slots):
+        start(load)
 
     def used(load):
         if load + place.slots < place.loads:
@@ -224,15 +226,17 @@
     def block_for_other(p):
         return jnp.where(section == 0, tables[0][p], tables[1][p])
 
-    for chunk, (own, other) in enumerate(pairs):
+    for chunk in range(CHUNKS):
+        own, other = ins[:2] if together else ins[2 * chunk : 2 * chunk + 2]
+        columns = slice(chunk * width, (chunk + 1) * width) if together else slice(0, width)
         mine_at = pl.multiple_of((2 * chunk + section) * width, LANES)
         theirs_at = pl.multiple_of((2 * chunk + 1 - section) * width, LANES)
         mine_gain = gain[:, pl.ds(mine_at, width)]
         theirs_gain = gain[:, pl.ds(theirs_at, width)]
         for p in range(count):
             at = pl.ds(p * rows, rows)
-            mine = own[p, :, :width].astype(jnp.float32)
-            theirs = other[block_for_other(p), :, :width].astype(jnp.float32)
+            mine = own[p, :, columns].astype(jnp.float32)
+            theirs = other[block_for_other(p), :, columns].astype(jnp.float32)
             scaled[at, pl.ds(mine_at, width)] = (mine * mine_gain).astype(jnp.bfloat16)
             scaled[at, pl.ds(theirs_at, width)] = (theirs * theirs_gain).astype(jnp.bfloat16)
             square = jnp.sum(mine * mine + theirs * theirs, axis=-1, keepdims=True)
@@ -303,7 +307,7 @@
 def run_layer(layer, place, arena, pairs, gain, router, named, top):
     count, rows, _ = pairs[0][0].shape
     total = count * rows
-    shape = jax.ShapeDtypeStruct((count, rows, place.width), jnp.bfloat16)
+    shape = pltpu.VMEM((count, rows, place.width), jnp.bfloat16)
     scratch = [
         pltpu.VMEM((total, gain.shape[1]), jnp.bfloat16),
         pltpu.VMEM((total, LANES), jnp.float32),
@@ -316,9 +320,9 @@
     inputs = [value for pair in pairs for value in pair] + [gain, router, named]
     specs = [IN_VMEM] * (len(inputs) - 1) + [ANYWHERE]
     results = call(
-        functools.partial(layer_body, place, top),
+        functools.partial(layer_body, place, top, len(pairs) == 1),
         layer, place, arena, inputs, [shape] * (2 * CHUNKS), scratch,
-        list(range(place.slots, place.loads)), "layer", zeros=True, specs=specs,
+        list(range(place.resident, place.loads)), "layer", zeros=True, specs=specs,
     )
     return results[:-1], results[-1]
 
@@ -333,8 +337,12 @@
     table = jnp.where(first, tables[0], tables[1])
     back = jnp.where(first, tables[1], tables[0])
     columns = []
+    if len(pairs) == 1:
+        pairs = [
+            [side[:, :, c * width : (c + 1) * width] for side in pairs[0]] for c in range(CHUNKS)
+        ]
     for own, other in pairs:
-        own, other = own[:, :, :width], other[:, :, :width][table]
+        other = other[table]
         columns += [jnp.where(first, own, other), jnp.where(first, other, own)]
     values = jnp.concatenate(columns, axis=-1).reshape(count * rows, model_width).astype(jnp.float32)
     factor = lax.rsqrt(jnp.mean(values * values, axis=-1, keepdims=True) + EPSILON)
@@ -344,7 +352,7 @@
         return jnp.dot(left, right, preferred_element_type=jnp.float32)
 
     affinity = jax.nn.sigmoid(product(scaled, router[0].T) * factor)
-    experts = named[:, :, width : width + top].reshape(count * rows, top).astype(jnp.int32)
+    experts = named[:, :, CHUNKS * width : CHUNKS * width + top].reshape(count * rows, top).astype(jnp.int32)
     hit = jnp.any(experts[:, :, None] == jnp.arange(EXPERTS, dtype=jnp.int32), axis=1)
     picked = jnp.where(hit, affinity, 0.0)
     gates = picked / jnp.sum(picked, axis=-1, keepdims=True)
@@ -381,7 +389,7 @@
     router = jnp.swapaxes(router_weight, 1, 2)
     weights = (gate_weight, up_weight, down_weight)
     held = count * micro * rows <= 2 * LANES
-    place = Arena(weights, width, 6, 62 * MIB)
+    place = Arena(weights, width, SLOTS, RESIDENT, TOP)
 
     def partials(layer, pairs):
         nonlocal arena
@@ -392,45 +400,50 @@
         moved = [swap(parts[2 * c]) for c in range(CHUNKS)]
         return [add(parts[2 * c + 1], moved[c]).astype(jnp.bfloat16) for c in range(CHUNKS)]
 
-    gathered = list(prepare(tokens, jnp.swapaxes(routes, 2, 3), width))
+    gathered = prepare(tokens, jnp.swapaxes(routes, 2, 3), width)
     arena = None
-    loads = list(range(place.slots))
+    loads = list(range(RESIDENT))
+    fetches = FETCHES
     for level in reversed(range(deepest + 1)):
-        received = [exchange(value, level) for value in gathered]
-        if held:
-            todo, loads = (loads[:2], loads[2:]) if level > 0 else (loads, [])
-            arena, token = fetch(place, arena, todo, gathered[0], received[0].shape[1:])
-            received[0] = after_token(received[0], token)
-        gathered = [jnp.concatenate(pair, axis=0) for pair in zip(gathered, received)]
-    named = gathered[0]
-    moved = partials(0, [(value, swap(value)) for value in gathered])
+        received = exchange(gathered, level)
+        if held and fetches:
+            todo, loads, fetches = loads[: fetches[0]], loads[fetches[0] :], fetches[1:]
+            arena, token = fetch(place, arena, todo, gathered, received.shape[1:])
+            received = after_token(received, token)
+        gathered = jnp.concatenate([gathered, received], axis=0)
+    if held and loads:
+        arena, _ = fetch(place, arena, loads, gathered, (8, LANES))
+    named = gathered
+    moved = partials(0, [(gathered, swap(gathered))])
 
     after = list(moved)
     for level in range(deepest):
-        for c in range(CHUNKS):
-            half = after[c].shape[0] // 2
-            received = exchange(after[c][half:], level)
-            after[c] = add(after[c][:half], received).astype(jnp.bfloat16)
+        after = [next_step(value, level) for value in after]
     for c in range(CHUNKS):
         value = add(after[c], jnp.flip(exchange(after[c], deepest), axis=0))
-        residual = gathered[c][:2, :, :width].astype(jnp.float32)
+        residual = gathered[:2, :, c * width : (c + 1) * width].astype(jnp.float32)
         after[c] = (residual + value).astype(jnp.bfloat16)
     own_after = [value[:1] for value in after]
     for level in reversed(range(deepest)):
         for c in range(CHUNKS):
             after[c] = jnp.concatenate([after[c], exchange(after[c], level)], axis=0)
     sums = partials(1, [(value, swap(value)) for value in after])
-    results = []
-    for c in range(CHUNKS):
-        value, _ = reduce_to(sums[c], 1)
-        value = (own_after[c].astype(jnp.float32) + value).astype(jnp.bfloat16)
-        results.append(value.reshape(micro, rows, width))
-    result = jnp.stack(results, axis=2)
-    keep = jnp.where(first, result[0], result[1])
-    received = swap(jnp.where(first, result[1], result[0]))
-    both = jnp.where(
-        first, jnp.stack([keep, received], axis=2), jnp.stack([received, keep], axis=2)
-    )
+    for level in range(deepest):
+        sums = [next_step(value, level) for value in sums]
+    ours = jnp.stack([add(value[0], own[0]) for value, own in zip(sums, own_after)], axis=1)
+    theirs = jnp.stack([value[1] for value in sums], axis=1)
+
+    def of_micro(value, mine):
+        value = value.reshape(micro, rows, CHUNKS, width)
+        return jnp.where(first == mine, value[0], value[1])
+
+    keep = of_micro(ours, True)
+    near = cross(of_micro(ours, False).astype(jnp.bfloat16), False, 1)
+    far_same = cross(of_micro(theirs, True), True, 0)
+    far_other = cross(of_micro(theirs, False), True, 1)
+    same = (keep + far_same.astype(jnp.float32)).astype(jnp.bfloat16)
+    other = add(near, far_other).astype(jnp.bfloat16)
+    both = jnp.where(first, jnp.stack([same, other], axis=2), jnp.stack([other, same], axis=2))
     return both.reshape(1, rows, model_width)
 
 

time: 149 us -> 140 us (0.940)
  Pallas kernels: 47.2 us -> 42 us
  other arithmetic: 5.39 us -> 1.45 us
  local copies, waits for them, and re-layouts: 4.49 us -> 2.63 us
    pallas_call x5, Pallas kernels: 45.5 us -> 40.3 us  [call(): pl.pallas_call(kernel, in_specs=(specs or [IN_VMEM] * n_in) + [ANYWHERE]...]
    convert_element_type x4, other arithmetic: 4.5 us -> 0.43 us  [partials(): add(parts[2 * c + 1], moved[c]).astype(jnp.bfloat16)]
    ppermute x0 -> x3, waiting for transfers between devices: none -> 3.52 us  [cross(): return lax.ppermute(value, ('expert', 'section'), pairs)]
    ppermute x0 -> x3, starting transfers between devices: none -> 3.18 us  [cross(): return lax.ppermute(value, ('expert', 'section'), pairs)]
    ppermute x22 -> x17, starting transfers between devices: 27.7 us -> 25.6 us  [exchange(): return lax.ppermute(value, ('expert', 'section'), pairs)]
    ppermute x22 -> x17, waiting for transfers between devices: 34.6 us -> 32.6 us  [exchange(): return lax.ppermute(value, ('expert', 'section'), pairs)]
    ppermute x9 -> x7, waiting for transfers between devices: 7.53 us -> 6.96 us  [swap(): return lax.ppermute(value, 'section', [(0, 1), (1, 0)])]
    ppermute x9 -> x7, starting transfers between devices: 21.2 us -> 20.7 us  [swap(): return lax.ppermute(value, 'section', [(0, 1), (1, 0)])]
  transfers between devices with their start and end apart: 31 -> 27, of which waited for: 20 -> 21; matrix products, arithmetic and copies ran while one was open for 5% -> 1% of each run, Pallas kernels for 13% -> 12%
where the time goes in v1:
time: 140 us; the launch traced here: 139 us
  starting transfers between devices  49.5 us (35%)
  waiting for transfers between devices  43.1 us (31%)
  Pallas kernels  42 us (30%)
  local copies, waits for them, and re-layouts  2.63 us (2%)
  other arithmetic  1.45 us (1%)
    pallas_call x5, Pallas kernels, call(): pl.pallas_call(kernel, in_specs=(specs or [IN_VMEM] * n_in) + [ANYWHERE]...  40.3 us
    ppermute x17, waiting for transfers between devices, exchange(): return lax.ppermute(value, ('expert', 'section'), pairs)  32.6 us
    ppermute x17, starting transfers between devices, exchange(): return lax.ppermute(value, ('expert', 'section'), pairs)  25.6 us
    ppermute x7, starting transfers between devices, swap(): return lax.ppermute(value, 'section', [(0, 1), (1, 0)])  20.7 us
    ppermute x7, waiting for transfers between devices, swap(): return lax.ppermute(value, 'section', [(0, 1), (1, 0)])  6.96 us
    ppermute x3, waiting for transfers between devices, cross(): return lax.ppermute(value, ('expert', 'section'), pairs)  3.52 us
    ppermute x3, starting transfers between devices, cross(): return lax.ppermute(value, ('expert', 'section'), pairs)  3.18 us
  transfers between devices with their start and end apart: 27, of which 21 were waited for; matrix products, arithmetic and copies ran while one was open for 1% of the time, Pallas kernels for 12%

profile of v1, /device:TPU:0, one launch (start us, length us, event | category | flops | bytes accessed | tf_op | source)
XLA Modules:
  0.0 139.1 jit_solution(11574707487261270062)
XLA Ops:
  0.0 1.7 %prepare.1.refs_3_ = bf16[1,16,3712]{2,1,0:T(8,128)(2,1)} custom-call(bf16[2,8,7168]{2,1,0:T(8,128)(2,1)} %tokens_ref.1, s32[1,2,4,8]{3,2,1,0:T(4,128)} %bitcast.18), custom_call_target="tpu_custom_call" | custom-call | tf_op jit(solution)/shard_map/prepare/pallas_call | solution.py:199
  1.7 4.0 %collective-permute-start = (bf16[1,16,3712]{2,1,0:T(8,128)(2,1)}, bf16[1,16,3712]{2,1,0:T(8,128)(2,1)S(1)}, u32[]{:S(2)}, u32[]{:S(2)}) collective-permute-start(bf16[1,16,3712]{2,1,0:T(8,128)(2,1)} %prepare.1.refs_3_), channel_id=1, source_target_pairs={{0,8},{1,9},{2,10},{3,11},{4,12},{5,13},{6,14},{7,15},{8,0},{9,1},... | collective-permute-start | bytes 356360 | tf_op jit(solution)/shard_map/ppermute | solution.py:46
  5.7 5.5 %fetch.3 = (bf16[86016,256]{1,0:T(8,128)(2,1)S(1)}, bf16[16,3712]{1,0:T(8,128)(2,1)S(1)}) custom-call(bf16[1,7168,2048]{2,1,0:T(8,128)(2,1)} %refs_7_.3, bf16[1,7168,2048]{2,1,0:T(8,128)(2,1)} %refs_8_.1, bf16[1,2048,7168]{2,1,0:T(8,128)(2,1)} %refs_9_.1, bf16[1,16,3712]{2,1,0:T(8,128)(2,1)} %prepare.1.refs_3_), custom_call_target="tpu_custom_call" | custom-call | bytes 14680064 | tf_op jit(solution)/shard_map/fetch/pallas_call | solution.py:160
  11.3 0.5 collective-permute-done
  11.8 1.2 collective-permute-start.1
  13.0 5.5 %fetch.4 = (bf16[86016,256]{1,0:T(8,128)(2,1)S(1)}, bf16[16,3712]{1,0:T(8,128)(2,1)S(1)}) custom-call(bf16[1,7168,2048]{2,1,0:T(8,128)(2,1)} %refs_7_.3, bf16[1,7168,2048]{2,1,0:T(8,128)(2,1)} %refs_8_.1, bf16[1,2048,7168]{2,1,0:T(8,128)(2,1)} %refs_9_.1, bf16[2,16,3712]{2,1,0:T(8,128)(2,1)} %copy-done.5, ...), custom_call_target="tpu_custom_call", output_to_operand_aliasing={{0}: (4, {})} | custom-call | bytes 14680064 | tf_op jit(solution)/shard_map/fetch/pallas_call | solution.py:160
  18.7 1.6 %collective-permute-start.2 = (bf16[4,16,3712]{2,1,0:T(8,128)(2,1)S(1)}, bf16[4,16,3712]{2,1,0:T(8,128)(2,1)S(1)}, u32[]{:S(2)}, u32[]{:S(2)}) collective-permute-start(bf16[4,16,3712]{2,1,0:T(8,128)(2,1)S(1)} %pad_maximum_fusion.1.refs_3_), channel_id=1, source_target_pairs={{0,2},{1,5},{2,0},{3,7},{4,6},{5,1},{6,4},{7,3},{8,10},{9,13},{10,... | collective-permute-start | bytes 1425416 | tf_op jit(solution)/shard_map/ppermute | solution.py:46
  20.3 5.5 %fetch.5 = (bf16[86016,256]{1,0:T(8,128)(2,1)S(1)}, bf16[16,3712]{1,0:T(8,128)(2,1)S(1)}) custom-call(bf16[1,7168,2048]{2,1,0:T(8,128)(2,1)} %refs_7_.3, bf16[1,7168,2048]{2,1,0:T(8,128)(2,1)} %refs_8_.1, bf16[1,2048,7168]{2,1,0:T(8,128)(2,1)} %refs_9_.1, bf16[4,16,3712]{2,1,0:T(8,128)(2,1)} %copy-done.2, ...), custom_call_target="tpu_custom_call", output_to_operand_aliasing={{0}: (4, {})} | custom-call | bytes 14680064 | tf_op jit(solution)/shard_map/fetch/pallas_call | solution.py:160
  25.8 1.6 %collective-permute-done.2 = bf16[4,16,3712]{2,1,0:T(8,128)(2,1)S(1)} collective-permute-done((bf16[4,16,3712]{2,1,0:T(8,128)(2,1)S(1)}, bf16[4,16,3712]{2,1,0:T(8,128)(2,1)S(1)}, u32[]{:S(2)}, u32[]{:S(2)}) %collective-permute-start.2) | collective-permute-done | bytes 475168 | tf_op jit(solution)/shard_map/ppermute | solution.py:46
  27.7 2.5 %collective-permute-done.3.refs_1_ = bf16[8,16,3712]{2,1,0:T(8,128)(2,1)S(1)} collective-permute-done((bf16[8,16,3712]{2,1,0:T(8,128)(2,1)S(1)}, bf16[8,16,3712]{2,1,0:T(8,128)(2,1)S(1)}, u32[]{:S(2)}, u32[]{:S(2)}) %collective-permute-start.3) | collective-permute-done | bytes 950304 | tf_op jit(solution)/shard_map/ppermute | solution.py:50
  30.2 0.9 copy-done.6
  31.1 21.6 %layer.2 = (bf16[8,16,1792]{2,1,0:T(8,128)(2,1)S(1)}, bf16[8,16,1792]{2,1,0:T(8,128)(2,1)S(1)}, bf16[8,16,1792]{2,1,0:T(8,128)(2,1)S(1)}, bf16[8,16,1792]{2,1,0:T(8,128)(2,1)S(1)}, bf16[86016,256]{1,0:T(8,128)(2,1)S(1)}) custom-call(bf16[8,16,3712]{2,1,0:T(8,128)(2,1)} %copy-done, bf16[8,16,3712]{2,1,0:T(8,128)(2,1)} %copy-done.6, ...), custom_call_target="tpu_custom_call", output_to_operand_aliasing={{4}: (8, {})} | custom-call | bytes 44040192 | tf_op jit(solution)/shard_map/layer/pallas_call | solution.py:160
  53.3 1.3 collective-permute-done.4
  54.8 1.6 %collective-permute-start.5 = (bf16[4,16,1792]{2,1,0:T(8,128)(2,1)S(1)}, bf16[4,16,1792]{2,1,0:T(8,128)(2,1)S(1)}, u32[]{:S(2)}, u32[]{:S(2)}) collective-permute-start(bf16[4,16,1792]{2,1,0:T(8,128)(2,1)S(1)} %slice.123), channel_id=1, source_target_pairs={{0,2},{1,5},{2,0},{3,7},{4,6},{5,1},{6,4},{7,3},{8,10},{9,13},{10,... | collective-permute-start | bytes 688136 | tf_op jit(solution)/shard_map/ppermute | solution.py:46
  56.5 0.6 collective-permute-start.12
  57.1 3.8 %collective-permute-done.5 = bf16[4,16,1792]{2,1,0:T(8,128)(2,1)S(1)} collective-permute-done((bf16[4,16,1792]{2,1,0:T(8,128)(2,1)S(1)}, bf16[4,16,1792]{2,1,0:T(8,128)(2,1)S(1)}, u32[]{:S(2)}, u32[]{:S(2)}) %collective-permute-start.5) | collective-permute-done | bytes 229408 | tf_op jit(solution)/shard_map/ppermute | solution.py:46
  60.9 1.0 collective-permute-start.6
  61.9 1.8 %collective-permute-done.12 = bf16[4,16,1792]{2,1,0:T(8,128)(2,1)S(1)} collective-permute-done((bf16[4,16,1792]{2,1,0:T(8,128)(2,1)S(1)}, bf16[4,16,1792]{2,1,0:T(8,128)(2,1)S(1)}, u32[]{:S(2)}, u32[]{:S(2)}) %collective-permute-start.12) | collective-permute-done | bytes 229408 | tf_op jit(solution)/shard_map/ppermute | solution.py:46
  63.8 1.0 collective-permute-start.13
  64.8 1.0 collective-permute-done.6
  65.8 3.0 %collective-permute-start.7 = (bf16[2,16,1792]{2,1,0:T(8,128)(2,1)S(1)}, bf16[2,16,1792]{2,1,0:T(8,128)(2,1)S(1)}, u32[]{:S(2)}, u32[]{:S(2)}) collective-permute-start(bf16[2,16,1792]{2,1,0:T(8,128)(2,1)S(1)} %add_convert_fusion.13), channel_id=1, source_target_pairs={{0,8},{1,9},{2,10},{3,11},{4,12},{5,13},{6,14},{7,15},{8,0},{9,1},... | collective-permute-start | bytes 344072 | tf_op jit(solution)/shard_map/ppermute | solution.py:46
  68.9 3.0 %collective-permute-start.14 = (bf16[2,16,1792]{2,1,0:T(8,128)(2,1)S(1)}, bf16[2,16,1792]{2,1,0:T(8,128)(2,1)S(1)}, u32[]{:S(2)}, u32[]{:S(2)}) collective-permute-start(bf16[2,16,1792]{2,1,0:T(8,128)(2,1)S(1)} %add_convert_fusion.11), channel_id=1, source_target_pairs={{0,8},{1,9},{2,10},{3,11},{4,12},{5,13},{6,14},{7,15},{8,0},{9,1},... | collective-permute-start | bytes 344072 | tf_op jit(solution)/shard_map/ppermute | solution.py:46
  71.9 4.7 %collective-permute-done.7 = bf16[2,16,1792]{2,1,0:T(8,128)(2,1)S(1)} collective-permute-done((bf16[2,16,1792]{2,1,0:T(8,128)(2,1)S(1)}, bf16[2,16,1792]{2,1,0:T(8,128)(2,1)S(1)}, u32[]{:S(2)}, u32[]{:S(2)}) %collective-permute-start.7) | collective-permute-done | bytes 114720 | tf_op jit(solution)/shard_map/ppermute | solution.py:46
  76.6 1.5 %collective-permute-done.14 = bf16[2,16,1792]{2,1,0:T(8,128)(2,1)S(1)} collective-permute-done((bf16[2,16,1792]{2,1,0:T(8,128)(2,1)S(1)}, bf16[2,16,1792]{2,1,0:T(8,128)(2,1)S(1)}, u32[]{:S(2)}, u32[]{:S(2)}) %collective-permute-start.14) | collective-permute-done | bytes 114720 | tf_op jit(solution)/shard_map/ppermute | solution.py:46
  78.3 2.0 %collective-permute-start.8 = (bf16[2,16,1792]{2,1,0:T(8,128)(2,1)S(1)}, bf16[2,16,1792]{2,1,0:T(8,128)(2,1)S(1)}, u32[]{:S(2)}, u32[]{:S(2)}) collective-permute-start(bf16[2,16,1792]{2,1,0:T(8,128)(2,1)S(1)} %get-tuple-element.36), channel_id=1, source_target_pairs={{0,4},{1,3},{2,6},{3,1},{4,0},{5,7},{6,2},{7,5},{8,12},{9,11},{10,... | collective-permute-start | bytes 344072 | tf_op jit(solution)/shard_map/ppermute | solution.py:46
  80.3 2.8 %collective-permute-done.15 = bf16[2,16,1792]{2,1,0:T(8,128)(2,1)S(1)} collective-permute-done((bf16[2,16,1792]{2,1,0:T(8,128)(2,1)S(1)}, bf16[2,16,1792]{2,1,0:T(8,128)(2,1)S(1)}, u32[]{:S(2)}, u32[]{:S(2)}) %collective-permute-start.15) | collective-permute-done | bytes 114720 | tf_op jit(solution)/shard_map/ppermute | solution.py:46
  83.1 1.6 %collective-permute-start.16 = (bf16[4,16,1792]{2,1,0:T(8,128)(2,1)S(1)}, bf16[4,16,1792]{2,1,0:T(8,128)(2,1)S(1)}, u32[]{:S(2)}, u32[]{:S(2)}) collective-permute-start(bf16[4,16,1792]{2,1,0:T(8,128)(2,1)S(1)} %pad_maximum_fusion.6), channel_id=1, source_target_pairs={{0,2},{1,5},{2,0},{3,7},{4,6},{5,1},{6,4},{7,3},{8,10},{9,13},{10,... | collective-permute-start | bytes 688136 | tf_op jit(solution)/shard_map/ppermute | solution.py:46
  84.8 1.6 %collective-permute-start.9 = (bf16[4,16,1792]{2,1,0:T(8,128)(2,1)S(1)}, bf16[4,16,1792]{2,1,0:T(8,128)(2,1)S(1)}, u32[]{:S(2)}, u32[]{:S(2)}) collective-permute-start(bf16[4,16,1792]{2,1,0:T(8,128)(2,1)S(1)} %pad_maximum_fusion.5), channel_id=1, source_target_pairs={{0,2},{1,5},{2,0},{3,7},{4,6},{5,1},{6,4},{7,3},{8,10},{9,13},{10,... | collective-permute-start | bytes 688136 | tf_op jit(solution)/shard_map/ppermute | solution.py:46
  86.3 2.8 %collective-permute-done.16 = bf16[4,16,1792]{2,1,0:T(8,128)(2,1)S(1)} collective-permute-done((bf16[4,16,1792]{2,1,0:T(8,128)(2,1)S(1)}, bf16[4,16,1792]{2,1,0:T(8,128)(2,1)S(1)}, u32[]{:S(2)}, u32[]{:S(2)}) %collective-permute-start.16) | collective-permute-done | bytes 229408 | tf_op jit(solution)/shard_map/ppermute | solution.py:46
  89.3 2.3 %collective-permute-done.9 = bf16[4,16,1792]{2,1,0:T(8,128)(2,1)S(1)} collective-permute-done((bf16[4,16,1792]{2,1,0:T(8,128)(2,1)S(1)}, bf16[4,16,1792]{2,1,0:T(8,128)(2,1)S(1)}, u32[]{:S(2)}, u32[]{:S(2)}) %collective-permute-start.9) | collective-permute-done | bytes 229408 | tf_op jit(solution)/shard_map/ppermute | solution.py:46
  91.8 1.8 %collective-permute-done.10.refs_1_ = bf16[8,16,1792]{2,1,0:T(8,128)(2,1)S(1)} collective-permute-done((bf16[8,16,1792]{2,1,0:T(8,128)(2,1)S(1)}, bf16[8,16,1792]{2,1,0:T(8,128)(2,1)S(1)}, u32[]{:S(2)}, u32[]{:S(2)}) %collective-permute-start.10) | collective-permute-done | bytes 458784 | tf_op jit(solution)/shard_map/ppermute | solution.py:50
  93.6 0.7 copy-done.8
  94.3 2.1 %layer.3 = (bf16[8,16,1792]{2,1,0:T(8,128)(2,1)S(1)}, bf16[8,16,1792]{2,1,0:T(8,128)(2,1)S(1)}, bf16[8,16,1792]{2,1,0:T(8,128)(2,1)S(1)}, bf16[8,16,1792]{2,1,0:T(8,128)(2,1)S(1)}, bf16[86016,256]{1,0:T(8,128)(2,1)S(1)}) custom-call(bf16[8,16,1792]{2,1,0:T(8,128)(2,1)} %copy-done.4, ...), custom_call_target="tpu_custom_call", output_to_operand_aliasing={{4}: (10, {})} | custom-call | bytes 44040192 | tf_op jit(solution)/shard_map/layer/pallas_call | solution.py:160
  96.4 19.8 %collective-permute-start.18 = (bf16[8,16,1792]{2,1,0:T(8,128)(2,1)S(1)}, bf16[8,16,1792]{2,1,0:T(8,128)(2,1)S(1)}, u32[]{:S(2)}, u32[]{:S(2)}) collective-permute-start(bf16[8,16,1792]{2,1,0:T(8,128)(2,1)S(1)} %get-tuple-element.32), channel_id=1, source_target_pairs={{0,1},{1,0},{2,3},{3,2},{4,5},{5,4},{6,7},{7,6},{8,9},{9,8},{10,11... | collective-permute-start | bytes 1376264 | tf_op jit(solution)/shard_map/ppermute | solution.py:50
  116.3 1.4 collective-permute-done.18
  117.8 1.6 %collective-permute-start.19 = (bf16[4,16,1792]{2,1,0:T(8,128)(2,1)S(1)}, bf16[4,16,1792]{2,1,0:T(8,128)(2,1)S(1)}, u32[]{:S(2)}, u32[]{:S(2)}) collective-permute-start(bf16[4,16,1792]{2,1,0:T(8,128)(2,1)S(1)} %slice.133), channel_id=1, source_target_pairs={{0,2},{1,5},{2,0},{3,7},{4,6},{5,1},{6,4},{7,3},{8,10},{9,13},{10,... | collective-permute-start | bytes 688136 | tf_op jit(solution)/shard_map/ppermute | solution.py:46
  119.5 0.6 collective-permute-start.22
  120.1 3.8 %collective-permute-done.19 = bf16[4,16,1792]{2,1,0:T(8,128)(2,1)S(1)} collective-permute-done((bf16[4,16,1792]{2,1,0:T(8,128)(2,1)S(1)}, bf16[4,16,1792]{2,1,0:T(8,128)(2,1)S(1)}, u32[]{:S(2)}, u32[]{:S(2)}) %collective-permute-start.19) | collective-permute-done | bytes 229408 | tf_op jit(solution)/shard_map/ppermute | solution.py:46
  123.9 0.7 collective-permute-start.20
  124.6 1.8 %collective-permute-done.22 = bf16[4,16,1792]{2,1,0:T(8,128)(2,1)S(1)} collective-permute-done((bf16[4,16,1792]{2,1,0:T(8,128)(2,1)S(1)}, bf16[4,16,1792]{2,1,0:T(8,128)(2,1)S(1)}, u32[]{:S(2)}, u32[]{:S(2)}) %collective-permute-start.22) | collective-permute-done | bytes 229408 | tf_op jit(solution)/shard_map/ppermute | solution.py:46
  126.5 0.7 collective-permute-start.23
  127.2 1.6 %collective-permute-done.20 = bf16[2,16,1792]{2,1,0:T(8,128)(2,1)S(1)} collective-permute-done((bf16[2,16,1792]{2,1,0:T(8,128)(2,1)S(1)}, bf16[2,16,1792]{2,1,0:T(8,128)(2,1)S(1)}, u32[]{:S(2)}, u32[]{:S(2)}) %collective-permute-start.20) | collective-permute-done | bytes 114720 | tf_op jit(solution)/shard_map/ppermute | solution.py:46
  128.9 2.5 %collective-permute-done.23 = bf16[2,16,1792]{2,1,0:T(8,128)(2,1)S(1)} collective-permute-done((bf16[2,16,1792]{2,1,0:T(8,128)(2,1)S(1)}, bf16[2,16,1792]{2,1,0:T(8,128)(2,1)S(1)}, u32[]{:S(2)}, u32[]{:S(2)}) %collective-permute-start.23) | collective-permute-done | bytes 114720 | tf_op jit(solution)/shard_map/ppermute | solution.py:46
  131.5 2.1 %collective-permute-start.24 = (bf16[8,2,1792]{2,0,1:T(8,128)(2,1)S(1)}, bf16[8,2,1792]{2,0,1:T(8,128)(2,1)S(1)}, u32[]{:S(2)}, u32[]{:S(2)}) collective-permute-start(bf16[8,2,1792]{2,0,1:T(8,128)(2,1)S(1)} %get-tuple-element.37), channel_id=1, source_target_pairs={{0,8},{1,9},{2,10},{3,11},{4,12},{5,13},{6,14},{7,15},{8,0},{9,1},... | collective-permute-start | bytes 172040 | tf_op jit(solution)/shard_map/ppermute | solution.py:67
  133.7 1.0 collective-permute-start.26
  134.7 2.6 %collective-permute-done.24 = bf16[8,2,1792]{2,0,1:T(8,128)(2,1)S(1)} collective-permute-done((bf16[8,2,1792]{2,0,1:T(8,128)(2,1)S(1)}, bf16[8,2,1792]{2,0,1:T(8,128)(2,1)S(1)}, u32[]{:S(2)}, u32[]{:S(2)}) %collective-permute-start.24) | collective-permute-done | bytes 57376 | tf_op jit(solution)/shard_map/ppermute | solution.py:67
  137.3 1.0 collective-permute-done.26
  138.4 0.7 select_n.50
  (72 shorter events, 2.8 us)
Async XLA Ops:
  1.7 10.1 %copy-start.1 = (bf16[1,16,3712]{2,1,0:T(8,128)(2,1)S(1)}, bf16[1,16,3712]{2,1,0:T(8,128)(2,1)}, u32[]{:S(2)}) copy-start(bf16[1,16,3712]{2,1,0:T(8,128)(2,1)} %prepare.1.refs_3_) | copy-start | bytes 356356
  1.7 10.1 %collective-permute-start = (bf16[1,16,3712]{2,1,0:T(8,128)(2,1)}, bf16[1,16,3712]{2,1,0:T(8,128)(2,1)S(1)}, u32[]{:S(2)}, u32[]{:S(2)}) collective-permute-start(bf16[1,16,3712]{2,1,0:T(8,128)(2,1)} %prepare.1.refs_3_), channel_id=1, source_target_pairs={{0,8},{1,9},{2,10},{3,11},{4,12},{5,13},{6,14},{7,15},{8,0},{9,1},... | collective-permute-start | bytes 356360 | tf_op jit(solution)/shard_map/ppermute | solution.py:46
  11.8 1.2 copy-start.5
  11.8 6.7 %collective-permute-start.1 = (bf16[2,16,3712]{2,1,0:T(8,128)(2,1)S(1)}, bf16[2,16,3712]{2,1,0:T(8,128)(2,1)S(1)}, u32[]{:S(2)}, u32[]{:S(2)}) collective-permute-start(bf16[2,16,3712]{2,1,0:T(8,128)(2,1)S(1)} %pad_maximum_fusion.4.refs_3_), channel_id=1, source_target_pairs={{0,4},{1,3},{2,6},{3,1},{4,0},{5,7},{6,2},{7,5},{8,12},{9,11},{10,... | collective-permute-start | bytes 712712 | tf_op jit(solution)/shard_map/ppermute | solution.py:46
  18.7 1.6 %copy-start.2 = (bf16[4,16,3712]{2,1,0:T(8,128)(2,1)}, bf16[4,16,3712]{2,1,0:T(8,128)(2,1)S(1)}, u32[]{:S(2)}) copy-start(bf16[4,16,3712]{2,1,0:T(8,128)(2,1)S(1)} %pad_maximum_fusion.1.refs_3_) | copy-start | bytes 1425412
  18.7 8.7 %collective-permute-start.2 = (bf16[4,16,3712]{2,1,0:T(8,128)(2,1)S(1)}, bf16[4,16,3712]{2,1,0:T(8,128)(2,1)S(1)}, u32[]{:S(2)}, u32[]{:S(2)}) collective-permute-start(bf16[4,16,3712]{2,1,0:T(8,128)(2,1)S(1)} %pad_maximum_fusion.1.refs_3_), channel_id=1, source_target_pairs={{0,2},{1,5},{2,0},{3,7},{4,6},{5,1},{6,4},{7,3},{8,10},{9,13},{10,... | collective-permute-start | bytes 1425416 | tf_op jit(solution)/shard_map/ppermute | solution.py:46
  27.6 3.5 %copy-start = (bf16[8,16,3712]{2,1,0:T(8,128)(2,1)}, bf16[8,16,3712]{2,1,0:T(8,128)(2,1)S(1)}, u32[]{:S(2)}) copy-start(bf16[8,16,3712]{2,1,0:T(8,128)(2,1)S(1)} %pad_maximum_fusion.refs_0_.refs_4_.refs_6_) | copy-start | bytes 2850820
  27.6 2.6 %collective-permute-start.3 = (bf16[8,16,3712]{2,1,0:T(8,128)(2,1)S(1)}, bf16[8,16,3712]{2,1,0:T(8,128)(2,1)S(1)}, u32[]{:S(2)}, u32[]{:S(2)}) collective-permute-start(bf16[8,16,3712]{2,1,0:T(8,128)(2,1)S(1)} %pad_maximum_fusion.refs_0_.refs_4_.refs_6_), channel_id=1, source_target_pairs={{0,1},{1,0},{2,3},{3,2},{4,5},{5,4},{6,7},{7,6},{8,9},{9,8},{10,11... | collective-permute-start | bytes 2850824 | tf_op jit(solution)/shard_map/ppermute | solution.py:50
  30.2 0.9 copy-start.6
  52.7 1.9 %collective-permute-start.4 = (bf16[8,16,1792]{2,1,0:T(8,128)(2,1)S(1)}, bf16[8,16,1792]{2,1,0:T(8,128)(2,1)S(1)}, u32[]{:S(2)}, u32[]{:S(2)}) collective-permute-start(bf16[8,16,1792]{2,1,0:T(8,128)(2,1)S(1)} %get-tuple-element.27), channel_id=1, source_target_pairs={{0,1},{1,0},{2,3},{3,2},{4,5},{5,4},{6,7},{7,6},{8,9},{9,8},{10,11... | collective-permute-start | bytes 1376264 | tf_op jit(solution)/shard_map/ppermute | solution.py:50
  52.8 3.5 %collective-permute-start.11 = (bf16[8,16,1792]{2,1,0:T(8,128)(2,1)S(1)}, bf16[8,16,1792]{2,1,0:T(8,128)(2,1)S(1)}, u32[]{:S(2)}, u32[]{:S(2)}) collective-permute-start(bf16[8,16,1792]{2,1,0:T(8,128)(2,1)S(1)} %get-tuple-element.29), channel_id=1, source_target_pairs={{0,1},{1,0},{2,3},{3,2},{4,5},{5,4},{6,7},{7,6},{8,9},{9,8},{10,11... | collective-permute-start | bytes 1376264 | tf_op jit(solution)/shard_map/ppermute | solution.py:50
  54.8 6.1 %collective-permute-start.5 = (bf16[4,16,1792]{2,1,0:T(8,128)(2,1)S(1)}, bf16[4,16,1792]{2,1,0:T(8,128)(2,1)S(1)}, u32[]{:S(2)}, u32[]{:S(2)}) collective-permute-start(bf16[4,16,1792]{2,1,0:T(8,128)(2,1)S(1)} %slice.123), channel_id=1, source_target_pairs={{0,2},{1,5},{2,0},{3,7},{4,6},{5,1},{6,4},{7,3},{8,10},{9,13},{10,... | collective-permute-start | bytes 688136 | tf_op jit(solution)/shard_map/ppermute | solution.py:46
  56.5 7.2 %collective-permute-start.12 = (bf16[4,16,1792]{2,1,0:T(8,128)(2,1)S(1)}, bf16[4,16,1792]{2,1,0:T(8,128)(2,1)S(1)}, u32[]{:S(2)}, u32[]{:S(2)}) collective-permute-start(bf16[4,16,1792]{2,1,0:T(8,128)(2,1)S(1)} %slice.129), channel_id=1, source_target_pairs={{0,2},{1,5},{2,0},{3,7},{4,6},{5,1},{6,4},{7,3},{8,10},{9,13},{10,... | collective-permute-start | bytes 688136 | tf_op jit(solution)/shard_map/ppermute | solution.py:46
  60.9 4.9 %collective-permute-start.6 = (bf16[2,16,1792]{2,1,0:T(8,128)(2,1)S(1)}, bf16[2,16,1792]{2,1,0:T(8,128)(2,1)S(1)}, u32[]{:S(2)}, u32[]{:S(2)}) collective-permute-start(bf16[2,16,1792]{2,1,0:T(8,128)(2,1)S(1)} %slice.125), channel_id=1, source_target_pairs={{0,4},{1,3},{2,6},{3,1},{4,0},{5,7},{6,2},{7,5},{8,12},{9,11},{10,... | collective-permute-start | bytes 344072 | tf_op jit(solution)/shard_map/ppermute | solution.py:46
  63.8 5.1 %collective-permute-start.13 = (bf16[2,16,1792]{2,1,0:T(8,128)(2,1)S(1)}, bf16[2,16,1792]{2,1,0:T(8,128)(2,1)S(1)}, u32[]{:S(2)}, u32[]{:S(2)}) collective-permute-start(bf16[2,16,1792]{2,1,0:T(8,128)(2,1)S(1)} %slice.131), channel_id=1, source_target_pairs={{0,4},{1,3},{2,6},{3,1},{4,0},{5,7},{6,2},{7,5},{8,12},{9,11},{10,... | collective-permute-start | bytes 344072 | tf_op jit(solution)/shard_map/ppermute | solution.py:46
  65.8 10.8 %collective-permute-start.7 = (bf16[2,16,1792]{2,1,0:T(8,128)(2,1)S(1)}, bf16[2,16,1792]{2,1,0:T(8,128)(2,1)S(1)}, u32[]{:S(2)}, u32[]{:S(2)}) collective-permute-start(bf16[2,16,1792]{2,1,0:T(8,128)(2,1)S(1)} %add_convert_fusion.13), channel_id=1, source_target_pairs={{0,8},{1,9},{2,10},{3,11},{4,12},{5,13},{6,14},{7,15},{8,0},{9,1},... | collective-permute-start | bytes 344072 | tf_op jit(solution)/shard_map/ppermute | solution.py:46
  68.9 9.2 %collective-permute-start.14 = (bf16[2,16,1792]{2,1,0:T(8,128)(2,1)S(1)}, bf16[2,16,1792]{2,1,0:T(8,128)(2,1)S(1)}, u32[]{:S(2)}, u32[]{:S(2)}) collective-permute-start(bf16[2,16,1792]{2,1,0:T(8,128)(2,1)S(1)} %add_convert_fusion.11), channel_id=1, source_target_pairs={{0,8},{1,9},{2,10},{3,11},{4,12},{5,13},{6,14},{7,15},{8,0},{9,1},... | collective-permute-start | bytes 344072 | tf_op jit(solution)/shard_map/ppermute | solution.py:46
  78.2 4.9 %collective-permute-start.15 = (bf16[2,16,1792]{2,1,0:T(8,128)(2,1)S(1)}, bf16[2,16,1792]{2,1,0:T(8,128)(2,1)S(1)}, u32[]{:S(2)}, u32[]{:S(2)}) collective-permute-start(bf16[2,16,1792]{2,1,0:T(8,128)(2,1)S(1)} %get-tuple-element.35), channel_id=1, source_target_pairs={{0,4},{1,3},{2,6},{3,1},{4,0},{5,7},{6,2},{7,5},{8,12},{9,11},{10,... | collective-permute-start | bytes 344072 | tf_op jit(solution)/shard_map/ppermute | solution.py:46
  78.3 6.5 %collective-permute-start.8 = (bf16[2,16,1792]{2,1,0:T(8,128)(2,1)S(1)}, bf16[2,16,1792]{2,1,0:T(8,128)(2,1)S(1)}, u32[]{:S(2)}, u32[]{:S(2)}) collective-permute-start(bf16[2,16,1792]{2,1,0:T(8,128)(2,1)S(1)} %get-tuple-element.36), channel_id=1, source_target_pairs={{0,4},{1,3},{2,6},{3,1},{4,0},{5,7},{6,2},{7,5},{8,12},{9,11},{10,... | collective-permute-start | bytes 344072 | tf_op jit(solution)/shard_map/ppermute | solution.py:46
  83.1 6.1 %collective-permute-start.16 = (bf16[4,16,1792]{2,1,0:T(8,128)(2,1)S(1)}, bf16[4,16,1792]{2,1,0:T(8,128)(2,1)S(1)}, u32[]{:S(2)}, u32[]{:S(2)}) collective-permute-start(bf16[4,16,1792]{2,1,0:T(8,128)(2,1)S(1)} %pad_maximum_fusion.6), channel_id=1, source_target_pairs={{0,2},{1,5},{2,0},{3,7},{4,6},{5,1},{6,4},{7,3},{8,10},{9,13},{10,... | collective-permute-start | bytes 688136 | tf_op jit(solution)/shard_map/ppermute | solution.py:46
  84.8 6.8 %collective-permute-start.9 = (bf16[4,16,1792]{2,1,0:T(8,128)(2,1)S(1)}, bf16[4,16,1792]{2,1,0:T(8,128)(2,1)S(1)}, u32[]{:S(2)}, u32[]{:S(2)}) collective-permute-start(bf16[4,16,1792]{2,1,0:T(8,128)(2,1)S(1)} %pad_maximum_fusion.5), channel_id=1, source_target_pairs={{0,2},{1,5},{2,0},{3,7},{4,6},{5,1},{6,4},{7,3},{8,10},{9,13},{10,... | collective-permute-start | bytes 688136 | tf_op jit(solution)/shard_map/ppermute | solution.py:46
  89.2 4.4 %copy-start.3 = (bf16[8,16,1792]{2,1,0:T(8,128)(2,1)}, bf16[8,16,1792]{2,1,0:T(8,128)(2,1)S(1)}, u32[]{:S(2)}) copy-start(bf16[8,16,1792]{2,1,0:T(8,128)(2,1)S(1)} %pad_maximum_fusion.3.refs_2_) | copy-start | bytes 1376260
  89.2 2.5 %collective-permute-start.17 = (bf16[8,16,1792]{2,1,0:T(8,128)(2,1)S(1)}, bf16[8,16,1792]{2,1,0:T(8,128)(2,1)S(1)}, u32[]{:S(2)}, u32[]{:S(2)}) collective-permute-start(bf16[8,16,1792]{2,1,0:T(8,128)(2,1)S(1)} %pad_maximum_fusion.3.refs_2_), channel_id=1, source_target_pairs={{0,1},{1,0},{2,3},{3,2},{4,5},{5,4},{6,7},{7,6},{8,9},{9,8},{10,11... | collective-permute-start | bytes 1376264 | tf_op jit(solution)/shard_map/ppermute | solution.py:50
  91.7 1.9 %copy-start.4 = (bf16[8,16,1792]{2,1,0:T(8,128)(2,1)}, bf16[8,16,1792]{2,1,0:T(8,128)(2,1)S(1)}, u32[]{:S(2)}) copy-start(bf16[8,16,1792]{2,1,0:T(8,128)(2,1)S(1)} %pad_maximum_fusion.2.refs_0_) | copy-start | bytes 1376260
  91.7 1.9 %collective-permute-start.10 = (bf16[8,16,1792]{2,1,0:T(8,128)(2,1)S(1)}, bf16[8,16,1792]{2,1,0:T(8,128)(2,1)S(1)}, u32[]{:S(2)}, u32[]{:S(2)}) collective-permute-start(bf16[8,16,1792]{2,1,0:T(8,128)(2,1)S(1)} %pad_maximum_fusion.2.refs_0_), channel_id=1, source_target_pairs={{0,1},{1,0},{2,3},{3,2},{4,5},{5,4},{6,7},{7,6},{8,9},{9,8},{10,11... | collective-permute-start | bytes 1376264 | tf_op jit(solution)/shard_map/ppermute | solution.py:50
  91.8 1.8 %copy-start.7 = (bf16[8,16,1792]{2,1,0:T(8,128)(2,1)}, bf16[8,16,1792]{2,1,0:T(8,128)(2,1)S(1)}, u32[]{:S(2)}) copy-start(bf16[8,16,1792]{2,1,0:T(8,128)(2,1)S(1)} %collective-permute-done.17.refs_3_) | copy-start | bytes 1376260
  93.6 0.8 copy-start.8
  96.4 21.2 %collective-permute-start.18 = (bf16[8,16,1792]{2,1,0:T(8,128)(2,1)S(1)}, bf16[8,16,1792]{2,1,0:T(8,128)(2,1)S(1)}, u32[]{:S(2)}, u32[]{:S(2)}) collective-permute-start(bf16[8,16,1792]{2,1,0:T(8,128)(2,1)S(1)} %get-tuple-element.32), channel_id=1, source_target_pairs={{0,1},{1,0},{2,3},{3,2},{4,5},{5,4},{6,7},{7,6},{8,9},{9,8},{10,11... | collective-permute-start | bytes 1376264 | tf_op jit(solution)/shard_map/ppermute | solution.py:50
  116.2 3.1 %collective-permute-start.21 = (bf16[8,16,1792]{2,1,0:T(8,128)(2,1)S(1)}, bf16[8,16,1792]{2,1,0:T(8,128)(2,1)S(1)}, u32[]{:S(2)}, u32[]{:S(2)}) collective-permute-start(bf16[8,16,1792]{2,1,0:T(8,128)(2,1)S(1)} %get-tuple-element.34), channel_id=1, source_target_pairs={{0,1},{1,0},{2,3},{3,2},{4,5},{5,4},{6,7},{7,6},{8,9},{9,8},{10,11... | collective-permute-start | bytes 1376264 | tf_op jit(solution)/shard_map/ppermute | solution.py:50
  117.8 6.1 %collective-permute-start.19 = (bf16[4,16,1792]{2,1,0:T(8,128)(2,1)S(1)}, bf16[4,16,1792]{2,1,0:T(8,128)(2,1)S(1)}, u32[]{:S(2)}, u32[]{:S(2)}) collective-permute-start(bf16[4,16,1792]{2,1,0:T(8,128)(2,1)S(1)} %slice.133), channel_id=1, source_target_pairs={{0,2},{1,5},{2,0},{3,7},{4,6},{5,1},{6,4},{7,3},{8,10},{9,13},{10,... | collective-permute-start | bytes 688136 | tf_op jit(solution)/shard_map/ppermute | solution.py:46
  119.5 7.0 %collective-permute-start.22 = (bf16[4,16,1792]{2,1,0:T(8,128)(2,1)S(1)}, bf16[4,16,1792]{2,1,0:T(8,128)(2,1)S(1)}, u32[]{:S(2)}, u32[]{:S(2)}) collective-permute-start(bf16[4,16,1792]{2,1,0:T(8,128)(2,1)S(1)} %slice.139), channel_id=1, source_target_pairs={{0,2},{1,5},{2,0},{3,7},{4,6},{5,1},{6,4},{7,3},{8,10},{9,13},{10,... | collective-permute-start | bytes 688136 | tf_op jit(solution)/shard_map/ppermute | solution.py:46
  123.9 4.9 %collective-permute-start.20 = (bf16[2,16,1792]{2,1,0:T(8,128)(2,1)S(1)}, bf16[2,16,1792]{2,1,0:T(8,128)(2,1)S(1)}, u32[]{:S(2)}, u32[]{:S(2)}) collective-permute-start(bf16[2,16,1792]{2,1,0:T(8,128)(2,1)S(1)} %slice.135), channel_id=1, source_target_pairs={{0,4},{1,3},{2,6},{3,1},{4,0},{5,7},{6,2},{7,5},{8,12},{9,11},{10,... | collective-permute-start | bytes 344072 | tf_op jit(solution)/shard_map/ppermute | solution.py:46
  126.5 4.9 %collective-permute-start.23 = (bf16[2,16,1792]{2,1,0:T(8,128)(2,1)S(1)}, bf16[2,16,1792]{2,1,0:T(8,128)(2,1)S(1)}, u32[]{:S(2)}, u32[]{:S(2)}) collective-permute-start(bf16[2,16,1792]{2,1,0:T(8,128)(2,1)S(1)} %slice.141), channel_id=1, source_target_pairs={{0,4},{1,3},{2,6},{3,1},{4,0},{5,7},{6,2},{7,5},{8,12},{9,11},{10,... | collective-permute-start | bytes 344072 | tf_op jit(solution)/shard_map/ppermute | solution.py:46
  131.5 5.8 %collective-permute-start.24 = (bf16[8,2,1792]{2,0,1:T(8,128)(2,1)S(1)}, bf16[8,2,1792]{2,0,1:T(8,128)(2,1)S(1)}, u32[]{:S(2)}, u32[]{:S(2)}) collective-permute-start(bf16[8,2,1792]{2,0,1:T(8,128)(2,1)S(1)} %get-tuple-element.37), channel_id=1, source_target_pairs={{0,8},{1,9},{2,10},{3,11},{4,12},{5,13},{6,14},{7,15},{8,0},{9,1},... | collective-permute-start | bytes 172040 | tf_op jit(solution)/shard_map/ppermute | solution.py:67
  133.6 3.7 %collective-permute-start.25 = (bf16[8,2,1792]{2,0,1:T(8,128)(2,1)S(1)}, bf16[8,2,1792]{2,0,1:T(8,128)(2,1)S(1)}, u32[]{:S(2)}, u32[]{:S(2)}) collective-permute-start(bf16[8,2,1792]{2,0,1:T(8,128)(2,1)S(1)} %select_convert_fusion), channel_id=1, source_target_pairs={{0,1},{1,0},{2,3},{3,2},{4,5},{5,4},{6,7},{7,6},{8,9},{9,8},{10,11... | collective-permute-start | bytes 172040 | tf_op jit(solution)/shard_map/ppermute | solution.py:67
  133.7 4.6 %collective-permute-start.26 = (bf16[8,2,1792]{2,0,1:T(8,128)(2,1)S(1)}, bf16[8,2,1792]{2,0,1:T(8,128)(2,1)S(1)}, u32[]{:S(2)}, u32[]{:S(2)}) collective-permute-start(bf16[8,2,1792]{2,0,1:T(8,128)(2,1)S(1)} %get-tuple-element.38), channel_id=1, source_target_pairs={{0,9},{1,8},{2,11},{3,10},{4,13},{5,12},{6,15},{7,14},{8,1},{9,0},... | collective-permute-start | bytes 172040 | tf_op jit(solution)/shard_map/ppermute | solution.py:67

commit v2 on v1

--- a/solution.py
+++ b/solution.py
@@ -15,7 +15,7 @@
 SLOTS = 6
 RESIDENT = 6
 FETCHES = (2, 2, 2)
-TOP = 60 << 20
+TOP = 59 << 20
 IN_VMEM = pl.BlockSpec(memory_space=pltpu.VMEM)
 ANYWHERE = pl.BlockSpec(memory_space=pl.ANY)
 
@@ -226,7 +226,7 @@
     def block_for_other(p):
         return jnp.where(section == 0, tables[0][p], tables[1][p])
 
-    for chunk in range(CHUNKS):
+    def assemble(chunk):
         own, other = ins[:2] if together else ins[2 * chunk : 2 * chunk + 2]
         columns = slice(chunk * width, (chunk + 1) * width) if together else slice(0, width)
         mine_at = pl.multiple_of((2 * chunk + section) * width, LANES)
@@ -242,24 +242,35 @@
             square = jnp.sum(mine * mine + theirs * theirs, axis=-1, keepdims=True)
             square = jnp.where(lane == EXPERTS, square, 0.0)
             stats[at, :] = square if chunk == 0 else stats[at, :] + square
-    stats[:, :EXPERTS] = lax.dot_general(
-        scaled[...], router[0], (((1,), (1,)), ((), ())), preferred_element_type=jnp.float32
-    )
-    values = stats[...]
-    lanes = lax.broadcasted_iota(jnp.int32, values.shape, 1)
-    total = jnp.sum(jnp.where(lanes == EXPERTS, values, 0.0), axis=-1, keepdims=True)
-    factor = lax.rsqrt(total / model_width + EPSILON)
-    affinity = jax.nn.sigmoid(values * factor)
-    bring.wait()
-    experts = routes[...].astype(jnp.float32).reshape(values.shape)
-    hit = jnp.zeros(values.shape, jnp.bool_)
-    for k in range(top):
-        hit = hit | (experts[:, k : k + 1] == lanes.astype(jnp.float32))
-    picked = jnp.where(hit & (lanes < EXPERTS), affinity, 0.0)
-    gates = picked / jnp.sum(picked, axis=-1, keepdims=True)
+
+    def gates_of():
+        stats[:, :EXPERTS] = lax.dot_general(
+            scaled[...], router[0], (((1,), (1,)), ((), ())), preferred_element_type=jnp.float32
+        )
+        values = stats[...]
+        lanes = lax.broadcasted_iota(jnp.int32, values.shape, 1)
+        total = jnp.sum(jnp.where(lanes == EXPERTS, values, 0.0), axis=-1, keepdims=True)
+        factor = lax.rsqrt(total / model_width + EPSILON)
+        affinity = jax.nn.sigmoid(values * factor)
+        bring.wait()
+        experts = routes[...].astype(jnp.float32).reshape(values.shape)
+        hit = jnp.zeros(values.shape, jnp.bool_)
+        for k in range(top):
+            hit = hit | (experts[:, k : k + 1] == lanes.astype(jnp.float32))
+        picked = jnp.where(hit & (lanes < EXPERTS), affinity, 0.0)
+        gates = picked / jnp.sum(picked, axis=-1, keepdims=True)
+        return factor, gates
+
     unit_at = lax.axis_index("expert") * units
-
+    if not together:
+        for chunk in range(CHUNKS):
+            assemble(chunk)
+        factor, gates = gates_of()
     for block in range(blocks):
+        if together and block % 2 == 0:
+            assemble(block // 2)
+        if together and block == blocks - 1:
+            factor, gates = gates_of()
         value = scaled.at[:, block * width : (block + 1) * width]
         for side, sums in enumerate((gate_sum, up_sum)):
             load = 2 * block + side
@@ -277,6 +288,7 @@
                     sums[:, at] = part
                     continue
                 expert = (unit_at + t * tile) // FF
+                lanes = lax.broadcasted_iota(jnp.int32, gates.shape, 1)
                 weight = jnp.sum(jnp.where(lanes == expert, gates, 0.0), axis=-1, keepdims=True)
                 gated = jax.nn.silu(gate_sum[:, at] * factor) * (part * (factor * weight))
                 hidden[:, at] = gated.astype(jnp.bfloat16)
@@ -317,7 +329,9 @@
         pltpu.VMEM((count, rows, LANES), jnp.bfloat16),
         pltpu.SemaphoreType.DMA,
     ]
-    inputs = [value for pair in pairs for value in pair] + [gain, router, named]
+    inputs = [
+        pltpu.with_memory_space_constraint(value, pltpu.VMEM) for pair in pairs for value in pair
+    ] + [gain, router, named]
     specs = [IN_VMEM] * (len(inputs) - 1) + [ANYWHERE]
     results = call(
         functools.partial(layer_body, place, top, len(pairs) == 1),

time: 140 us -> 136 us (0.971)
  Pallas kernels: 42 us -> 39.1 us
  local copies, waits for them, and re-layouts: 2.63 us -> 0.93 us
    pallas_call x5, Pallas kernels: 40.3 us -> 37.4 us  [call(): pl.pallas_call(kernel, in_specs=(specs or [IN_VMEM] * n_in) + [ANYWHERE]...]
    unnamed x18 -> x8, local copies, waits for them, and re-layouts: 1.71 us -> 0.02 us
where the time goes in v2:
time: 136 us; the launch traced here: 135 us
  starting transfers between devices  49.6 us (36%)
  waiting for transfers between devices  43.1 us (32%)
  Pallas kernels  39.1 us (29%)
  other arithmetic  1.45 us (1%)
    pallas_call x5, Pallas kernels, call(): pl.pallas_call(kernel, in_specs=(specs or [IN_VMEM] * n_in) + [ANYWHERE]...  37.4 us
    ppermute x17, waiting for transfers between devices, exchange(): return lax.ppermute(value, ('expert', 'section'), pairs)  32.6 us
    ppermute x17, starting transfers between devices, exchange(): return lax.ppermute(value, ('expert', 'section'), pairs)  25.7 us
    ppermute x7, starting transfers between devices, swap(): return lax.ppermute(value, 'section', [(0, 1), (1, 0)])  20.8 us
    ppermute x7, waiting for transfers between devices, swap(): return lax.ppermute(value, 'section', [(0, 1), (1, 0)])  6.97 us
    ppermute x3, waiting for transfers between devices, cross(): return lax.ppermute(value, ('expert', 'section'), pairs)  3.51 us
    ppermute x3, starting transfers between devices, cross(): return lax.ppermute(value, ('expert', 'section'), pairs)  3.18 us
  transfers between devices with their start and end apart: 27, of which 21 were waited for; matrix products, arithmetic and copies ran while one was open for 1% of the time, Pallas kernels for 12%

profile of v2, /device:TPU:0, one launch (start us, length us, event | category | flops | bytes accessed | tf_op | source)
XLA Modules:
  0.0 134.6 jit_solution(14206986543526265844)
XLA Ops:
  0.0 1.7 %prepare.1.refs_3_ = bf16[1,16,3712]{2,1,0:T(8,128)(2,1)} custom-call(bf16[2,8,7168]{2,1,0:T(8,128)(2,1)} %tokens_ref.1, s32[1,2,4,8]{3,2,1,0:T(4,128)} %bitcast.18), custom_call_target="tpu_custom_call" | custom-call | tf_op jit(solution)/shard_map/prepare/pallas_call | solution.py:199
  1.7 4.0 %collective-permute-start = (bf16[1,16,3712]{2,1,0:T(8,128)(2,1)}, bf16[1,16,3712]{2,1,0:T(8,128)(2,1)S(1)}, u32[]{:S(2)}, u32[]{:S(2)}) collective-permute-start(bf16[1,16,3712]{2,1,0:T(8,128)(2,1)} %prepare.1.refs_3_), channel_id=1, source_target_pairs={{0,8},{1,9},{2,10},{3,11},{4,12},{5,13},{6,14},{7,15},{8,0},{9,1},... | collective-permute-start | bytes 356360 | tf_op jit(solution)/shard_map/ppermute | solution.py:46
  5.7 5.5 %fetch.3 = (bf16[86016,256]{1,0:T(8,128)(2,1)S(1)}, bf16[16,3712]{1,0:T(8,128)(2,1)S(1)}) custom-call(bf16[1,7168,2048]{2,1,0:T(8,128)(2,1)} %refs_7_.3, bf16[1,7168,2048]{2,1,0:T(8,128)(2,1)} %refs_8_.1, bf16[1,2048,7168]{2,1,0:T(8,128)(2,1)} %refs_9_.1, bf16[1,16,3712]{2,1,0:T(8,128)(2,1)} %prepare.1.refs_3_), custom_call_target="tpu_custom_call" | custom-call | bytes 14680064 | tf_op jit(solution)/shard_map/fetch/pallas_call | solution.py:160
  11.3 0.5 collective-permute-done
  11.9 1.2 collective-permute-start.1
  13.0 5.5 %fetch.4 = (bf16[86016,256]{1,0:T(8,128)(2,1)S(1)}, bf16[16,3712]{1,0:T(8,128)(2,1)S(1)}) custom-call(bf16[1,7168,2048]{2,1,0:T(8,128)(2,1)} %refs_7_.3, bf16[1,7168,2048]{2,1,0:T(8,128)(2,1)} %refs_8_.1, bf16[1,2048,7168]{2,1,0:T(8,128)(2,1)} %refs_9_.1, bf16[2,16,3712]{2,1,0:T(8,128)(2,1)} %copy-done.3, ...), custom_call_target="tpu_custom_call", output_to_operand_aliasing={{0}: (4, {})} | custom-call | bytes 14680064 | tf_op jit(solution)/shard_map/fetch/pallas_call | solution.py:160
  18.7 1.6 %collective-permute-start.2 = (bf16[4,16,3712]{2,1,0:T(8,128)(2,1)S(1)}, bf16[4,16,3712]{2,1,0:T(8,128)(2,1)S(1)}, u32[]{:S(2)}, u32[]{:S(2)}) collective-permute-start(bf16[4,16,3712]{2,1,0:T(8,128)(2,1)S(1)} %pad_maximum_fusion.1.refs_3_), channel_id=1, source_target_pairs={{0,2},{1,5},{2,0},{3,7},{4,6},{5,1},{6,4},{7,3},{8,10},{9,13},{10,... | collective-permute-start | bytes 1425416 | tf_op jit(solution)/shard_map/ppermute | solution.py:46
  20.3 5.5 %fetch.5 = (bf16[86016,256]{1,0:T(8,128)(2,1)S(1)}, bf16[16,3712]{1,0:T(8,128)(2,1)S(1)}) custom-call(bf16[1,7168,2048]{2,1,0:T(8,128)(2,1)} %refs_7_.3, bf16[1,7168,2048]{2,1,0:T(8,128)(2,1)} %refs_8_.1, bf16[1,2048,7168]{2,1,0:T(8,128)(2,1)} %refs_9_.1, bf16[4,16,3712]{2,1,0:T(8,128)(2,1)} %copy-done.2, ...), custom_call_target="tpu_custom_call", output_to_operand_aliasing={{0}: (4, {})} | custom-call | bytes 14680064 | tf_op jit(solution)/shard_map/fetch/pallas_call | solution.py:160
  25.8 1.6 %collective-permute-done.2 = bf16[4,16,3712]{2,1,0:T(8,128)(2,1)S(1)} collective-permute-done((bf16[4,16,3712]{2,1,0:T(8,128)(2,1)S(1)}, bf16[4,16,3712]{2,1,0:T(8,128)(2,1)S(1)}, u32[]{:S(2)}, u32[]{:S(2)}) %collective-permute-start.2) | collective-permute-done | bytes 475168 | tf_op jit(solution)/shard_map/ppermute | solution.py:46
  27.7 2.5 %collective-permute-done.3.refs_1_ = bf16[8,16,3712]{2,1,0:T(8,128)(2,1)S(1)} collective-permute-done((bf16[8,16,3712]{2,1,0:T(8,128)(2,1)S(1)}, bf16[8,16,3712]{2,1,0:T(8,128)(2,1)S(1)}, u32[]{:S(2)}, u32[]{:S(2)}) %collective-permute-start.3) | collective-permute-done | bytes 950304 | tf_op jit(solution)/shard_map/ppermute | solution.py:50
  30.2 19.2 %layer.2 = (bf16[8,16,1792]{2,1,0:T(8,128)(2,1)S(1)}, bf16[8,16,1792]{2,1,0:T(8,128)(2,1)S(1)}, bf16[8,16,1792]{2,1,0:T(8,128)(2,1)S(1)}, bf16[8,16,1792]{2,1,0:T(8,128)(2,1)S(1)}, bf16[86016,256]{1,0:T(8,128)(2,1)S(1)}) custom-call(bf16[8,16,3712]{2,1,0:T(8,128)(2,1)S(1)} %pad_maximum_fusion.refs_0_.refs_4_.refs_6_, ...), custom_call_target="tpu_custom_call", output_to_operand_aliasing={{4}: (8, {})} | custom-call | bytes 44040192 | tf_op jit(solution)/shard_map/layer/pallas_call | solution.py:160
  49.5 0.5 collective-permute-start.11
  50.0 1.3 collective-permute-done.4
  51.5 1.6 %collective-permute-start.5 = (bf16[4,16,1792]{2,1,0:T(8,128)(2,1)S(1)}, bf16[4,16,1792]{2,1,0:T(8,128)(2,1)S(1)}, u32[]{:S(2)}, u32[]{:S(2)}) collective-permute-start(bf16[4,16,1792]{2,1,0:T(8,128)(2,1)S(1)} %slice.123), channel_id=1, source_target_pairs={{0,2},{1,5},{2,0},{3,7},{4,6},{5,1},{6,4},{7,3},{8,10},{9,13},{10,... | collective-permute-start | bytes 688136 | tf_op jit(solution)/shard_map/ppermute | solution.py:46
  53.2 0.6 collective-permute-start.12
  53.8 3.8 %collective-permute-done.5 = bf16[4,16,1792]{2,1,0:T(8,128)(2,1)S(1)} collective-permute-done((bf16[4,16,1792]{2,1,0:T(8,128)(2,1)S(1)}, bf16[4,16,1792]{2,1,0:T(8,128)(2,1)S(1)}, u32[]{:S(2)}, u32[]{:S(2)}) %collective-permute-start.5) | collective-permute-done | bytes 229408 | tf_op jit(solution)/shard_map/ppermute | solution.py:46
  57.6 1.0 collective-permute-start.6
  58.6 1.7 %collective-permute-done.12 = bf16[4,16,1792]{2,1,0:T(8,128)(2,1)S(1)} collective-permute-done((bf16[4,16,1792]{2,1,0:T(8,128)(2,1)S(1)}, bf16[4,16,1792]{2,1,0:T(8,128)(2,1)S(1)}, u32[]{:S(2)}, u32[]{:S(2)}) %collective-permute-start.12) | collective-permute-done | bytes 229408 | tf_op jit(solution)/shard_map/ppermute | solution.py:46
  60.5 1.0 collective-permute-start.13
  61.5 1.0 collective-permute-done.6
  62.5 3.0 %collective-permute-start.7 = (bf16[2,16,1792]{2,1,0:T(8,128)(2,1)S(1)}, bf16[2,16,1792]{2,1,0:T(8,128)(2,1)S(1)}, u32[]{:S(2)}, u32[]{:S(2)}) collective-permute-start(bf16[2,16,1792]{2,1,0:T(8,128)(2,1)S(1)} %add_convert_fusion.13), channel_id=1, source_target_pairs={{0,8},{1,9},{2,10},{3,11},{4,12},{5,13},{6,14},{7,15},{8,0},{9,1},... | collective-permute-start | bytes 344072 | tf_op jit(solution)/shard_map/ppermute | solution.py:46
  65.6 3.0 %collective-permute-start.14 = (bf16[2,16,1792]{2,1,0:T(8,128)(2,1)S(1)}, bf16[2,16,1792]{2,1,0:T(8,128)(2,1)S(1)}, u32[]{:S(2)}, u32[]{:S(2)}) collective-permute-start(bf16[2,16,1792]{2,1,0:T(8,128)(2,1)S(1)} %add_convert_fusion.11), channel_id=1, source_target_pairs={{0,8},{1,9},{2,10},{3,11},{4,12},{5,13},{6,14},{7,15},{8,0},{9,1},... | collective-permute-start | bytes 344072 | tf_op jit(solution)/shard_map/ppermute | solution.py:46
  68.6 4.7 %collective-permute-done.7 = bf16[2,16,1792]{2,1,0:T(8,128)(2,1)S(1)} collective-permute-done((bf16[2,16,1792]{2,1,0:T(8,128)(2,1)S(1)}, bf16[2,16,1792]{2,1,0:T(8,128)(2,1)S(1)}, u32[]{:S(2)}, u32[]{:S(2)}) %collective-permute-start.7) | collective-permute-done | bytes 114720 | tf_op jit(solution)/shard_map/ppermute | solution.py:46
  73.3 1.5 %collective-permute-done.14 = bf16[2,16,1792]{2,1,0:T(8,128)(2,1)S(1)} collective-permute-done((bf16[2,16,1792]{2,1,0:T(8,128)(2,1)S(1)}, bf16[2,16,1792]{2,1,0:T(8,128)(2,1)S(1)}, u32[]{:S(2)}, u32[]{:S(2)}) %collective-permute-start.14) | collective-permute-done | bytes 114720 | tf_op jit(solution)/shard_map/ppermute | solution.py:46
  75.0 2.0 %collective-permute-start.8 = (bf16[2,16,1792]{2,1,0:T(8,128)(2,1)S(1)}, bf16[2,16,1792]{2,1,0:T(8,128)(2,1)S(1)}, u32[]{:S(2)}, u32[]{:S(2)}) collective-permute-start(bf16[2,16,1792]{2,1,0:T(8,128)(2,1)S(1)} %get-tuple-element.36), channel_id=1, source_target_pairs={{0,4},{1,3},{2,6},{3,1},{4,0},{5,7},{6,2},{7,5},{8,12},{9,11},{10,... | collective-permute-start | bytes 344072 | tf_op jit(solution)/shard_map/ppermute | solution.py:46
  77.0 2.8 %collective-permute-done.15 = bf16[2,16,1792]{2,1,0:T(8,128)(2,1)S(1)} collective-permute-done((bf16[2,16,1792]{2,1,0:T(8,128)(2,1)S(1)}, bf16[2,16,1792]{2,1,0:T(8,128)(2,1)S(1)}, u32[]{:S(2)}, u32[]{:S(2)}) %collective-permute-start.15) | collective-permute-done | bytes 114720 | tf_op jit(solution)/shard_map/ppermute | solution.py:46
  79.8 1.6 %collective-permute-start.16 = (bf16[4,16,1792]{2,1,0:T(8,128)(2,1)S(1)}, bf16[4,16,1792]{2,1,0:T(8,128)(2,1)S(1)}, u32[]{:S(2)}, u32[]{:S(2)}) collective-permute-start(bf16[4,16,1792]{2,1,0:T(8,128)(2,1)S(1)} %pad_maximum_fusion.6), channel_id=1, source_target_pairs={{0,2},{1,5},{2,0},{3,7},{4,6},{5,1},{6,4},{7,3},{8,10},{9,13},{10,... | collective-permute-start | bytes 688136 | tf_op jit(solution)/shard_map/ppermute | solution.py:46
  81.3 0.1 collective-permute-done.8
  81.5 1.6 %collective-permute-start.9 = (bf16[4,16,1792]{2,1,0:T(8,128)(2,1)S(1)}, bf16[4,16,1792]{2,1,0:T(8,128)(2,1)S(1)}, u32[]{:S(2)}, u32[]{:S(2)}) collective-permute-start(bf16[4,16,1792]{2,1,0:T(8,128)(2,1)S(1)} %pad_maximum_fusion.5), channel_id=1, source_target_pairs={{0,2},{1,5},{2,0},{3,7},{4,6},{5,1},{6,4},{7,3},{8,10},{9,13},{10,... | collective-permute-start | bytes 688136 | tf_op jit(solution)/shard_map/ppermute | solution.py:46
  83.0 2.8 %collective-permute-done.16 = bf16[4,16,1792]{2,1,0:T(8,128)(2,1)S(1)} collective-permute-done((bf16[4,16,1792]{2,1,0:T(8,128)(2,1)S(1)}, bf16[4,16,1792]{2,1,0:T(8,128)(2,1)S(1)}, u32[]{:S(2)}, u32[]{:S(2)}) %collective-permute-start.16) | collective-permute-done | bytes 229408 | tf_op jit(solution)/shard_map/ppermute | solution.py:46
  86.0 2.3 %collective-permute-done.9 = bf16[4,16,1792]{2,1,0:T(8,128)(2,1)S(1)} collective-permute-done((bf16[4,16,1792]{2,1,0:T(8,128)(2,1)S(1)}, bf16[4,16,1792]{2,1,0:T(8,128)(2,1)S(1)}, u32[]{:S(2)}, u32[]{:S(2)}) %collective-permute-start.9) | collective-permute-done | bytes 229408 | tf_op jit(solution)/shard_map/ppermute | solution.py:46
  88.5 1.8 %collective-permute-done.10.refs_1_ = bf16[8,16,1792]{2,1,0:T(8,128)(2,1)S(1)} collective-permute-done((bf16[8,16,1792]{2,1,0:T(8,128)(2,1)S(1)}, bf16[8,16,1792]{2,1,0:T(8,128)(2,1)S(1)}, u32[]{:S(2)}, u32[]{:S(2)}) %collective-permute-start.10) | collective-permute-done | bytes 458784 | tf_op jit(solution)/shard_map/ppermute | solution.py:50
  90.2 1.5 %layer.3 = (bf16[8,16,1792]{2,1,0:T(8,128)(2,1)S(1)}, bf16[8,16,1792]{2,1,0:T(8,128)(2,1)S(1)}, bf16[8,16,1792]{2,1,0:T(8,128)(2,1)S(1)}, bf16[8,16,1792]{2,1,0:T(8,128)(2,1)S(1)}, bf16[86016,256]{1,0:T(8,128)(2,1)S(1)}) custom-call(bf16[8,16,1792]{2,1,0:T(8,128)(2,1)S(1)} %pad_maximum_fusion.2.refs_0_, ...), custom_call_target="tpu_custom_call", output_to_operand_aliasing={{4}: (10, {})} | custom-call | bytes 44040192 | tf_op jit(solution)/shard_map/layer/pallas_call | solution.py:160
  91.8 19.9 %collective-permute-start.18 = (bf16[8,16,1792]{2,1,0:T(8,128)(2,1)S(1)}, bf16[8,16,1792]{2,1,0:T(8,128)(2,1)S(1)}, u32[]{:S(2)}, u32[]{:S(2)}) collective-permute-start(bf16[8,16,1792]{2,1,0:T(8,128)(2,1)S(1)} %get-tuple-element.32), channel_id=1, source_target_pairs={{0,1},{1,0},{2,3},{3,2},{4,5},{5,4},{6,7},{7,6},{8,9},{9,8},{10,11... | collective-permute-start | bytes 1376264 | tf_op jit(solution)/shard_map/ppermute | solution.py:50
  111.8 1.4 %collective-permute-done.18 = bf16[8,16,1792]{2,1,0:T(8,128)(2,1)S(1)} collective-permute-done((bf16[8,16,1792]{2,1,0:T(8,128)(2,1)S(1)}, bf16[8,16,1792]{2,1,0:T(8,128)(2,1)S(1)}, u32[]{:S(2)}, u32[]{:S(2)}) %collective-permute-start.18) | collective-permute-done | bytes 458784 | tf_op jit(solution)/shard_map/ppermute | solution.py:50
  113.3 1.6 %collective-permute-start.19 = (bf16[4,16,1792]{2,1,0:T(8,128)(2,1)S(1)}, bf16[4,16,1792]{2,1,0:T(8,128)(2,1)S(1)}, u32[]{:S(2)}, u32[]{:S(2)}) collective-permute-start(bf16[4,16,1792]{2,1,0:T(8,128)(2,1)S(1)} %slice.133), channel_id=1, source_target_pairs={{0,2},{1,5},{2,0},{3,7},{4,6},{5,1},{6,4},{7,3},{8,10},{9,13},{10,... | collective-permute-start | bytes 688136 | tf_op jit(solution)/shard_map/ppermute | solution.py:46
  115.0 0.6 collective-permute-start.22
  115.6 3.8 %collective-permute-done.19 = bf16[4,16,1792]{2,1,0:T(8,128)(2,1)S(1)} collective-permute-done((bf16[4,16,1792]{2,1,0:T(8,128)(2,1)S(1)}, bf16[4,16,1792]{2,1,0:T(8,128)(2,1)S(1)}, u32[]{:S(2)}, u32[]{:S(2)}) %collective-permute-start.19) | collective-permute-done | bytes 229408 | tf_op jit(solution)/shard_map/ppermute | solution.py:46
  119.4 0.7 collective-permute-start.20
  120.1 1.8 %collective-permute-done.22 = bf16[4,16,1792]{2,1,0:T(8,128)(2,1)S(1)} collective-permute-done((bf16[4,16,1792]{2,1,0:T(8,128)(2,1)S(1)}, bf16[4,16,1792]{2,1,0:T(8,128)(2,1)S(1)}, u32[]{:S(2)}, u32[]{:S(2)}) %collective-permute-start.22) | collective-permute-done | bytes 229408 | tf_op jit(solution)/shard_map/ppermute | solution.py:46
  122.0 0.7 collective-permute-start.23
  122.7 1.6 %collective-permute-done.20 = bf16[2,16,1792]{2,1,0:T(8,128)(2,1)S(1)} collective-permute-done((bf16[2,16,1792]{2,1,0:T(8,128)(2,1)S(1)}, bf16[2,16,1792]{2,1,0:T(8,128)(2,1)S(1)}, u32[]{:S(2)}, u32[]{:S(2)}) %collective-permute-start.20) | collective-permute-done | bytes 114720 | tf_op jit(solution)/shard_map/ppermute | solution.py:46
  124.4 2.5 %collective-permute-done.23 = bf16[2,16,1792]{2,1,0:T(8,128)(2,1)S(1)} collective-permute-done((bf16[2,16,1792]{2,1,0:T(8,128)(2,1)S(1)}, bf16[2,16,1792]{2,1,0:T(8,128)(2,1)S(1)}, u32[]{:S(2)}, u32[]{:S(2)}) %collective-permute-start.23) | collective-permute-done | bytes 114720 | tf_op jit(solution)/shard_map/ppermute | solution.py:46
  127.0 2.1 %collective-permute-start.24 = (bf16[8,2,1792]{2,0,1:T(8,128)(2,1)S(1)}, bf16[8,2,1792]{2,0,1:T(8,128)(2,1)S(1)}, u32[]{:S(2)}, u32[]{:S(2)}) collective-permute-start(bf16[8,2,1792]{2,0,1:T(8,128)(2,1)S(1)} %get-tuple-element.37), channel_id=1, source_target_pairs={{0,8},{1,9},{2,10},{3,11},{4,12},{5,13},{6,14},{7,15},{8,0},{9,1},... | collective-permute-start | bytes 172040 | tf_op jit(solution)/shard_map/ppermute | solution.py:67
  129.2 1.0 collective-permute-start.26
  130.2 2.6 %collective-permute-done.24 = bf16[8,2,1792]{2,0,1:T(8,128)(2,1)S(1)} collective-permute-done((bf16[8,2,1792]{2,0,1:T(8,128)(2,1)S(1)}, bf16[8,2,1792]{2,0,1:T(8,128)(2,1)S(1)}, u32[]{:S(2)}, u32[]{:S(2)}) %collective-permute-start.24) | collective-permute-done | bytes 57376 | tf_op jit(solution)/shard_map/ppermute | solution.py:67
  132.8 1.0 collective-permute-done.26
  133.9 0.7 select_n.50
  (62 shorter events, 2.2 us)
Async XLA Ops:
  1.7 10.1 %copy-start.1 = (bf16[1,16,3712]{2,1,0:T(8,128)(2,1)S(1)}, bf16[1,16,3712]{2,1,0:T(8,128)(2,1)}, u32[]{:S(2)}) copy-start(bf16[1,16,3712]{2,1,0:T(8,128)(2,1)} %prepare.1.refs_3_) | copy-start | bytes 356356
  1.7 10.1 %collective-permute-start = (bf16[1,16,3712]{2,1,0:T(8,128)(2,1)}, bf16[1,16,3712]{2,1,0:T(8,128)(2,1)S(1)}, u32[]{:S(2)}, u32[]{:S(2)}) collective-permute-start(bf16[1,16,3712]{2,1,0:T(8,128)(2,1)} %prepare.1.refs_3_), channel_id=1, source_target_pairs={{0,8},{1,9},{2,10},{3,11},{4,12},{5,13},{6,14},{7,15},{8,0},{9,1},... | collective-permute-start | bytes 356360 | tf_op jit(solution)/shard_map/ppermute | solution.py:46
  11.8 1.2 copy-start.3
  11.9 6.7 %collective-permute-start.1 = (bf16[2,16,3712]{2,1,0:T(8,128)(2,1)S(1)}, bf16[2,16,3712]{2,1,0:T(8,128)(2,1)S(1)}, u32[]{:S(2)}, u32[]{:S(2)}) collective-permute-start(bf16[2,16,3712]{2,1,0:T(8,128)(2,1)S(1)} %pad_maximum_fusion.4.refs_3_), channel_id=1, source_target_pairs={{0,4},{1,3},{2,6},{3,1},{4,0},{5,7},{6,2},{7,5},{8,12},{9,11},{10,... | collective-permute-start | bytes 712712 | tf_op jit(solution)/shard_map/ppermute | solution.py:46
  18.7 1.6 %copy-start.2 = (bf16[4,16,3712]{2,1,0:T(8,128)(2,1)}, bf16[4,16,3712]{2,1,0:T(8,128)(2,1)S(1)}, u32[]{:S(2)}) copy-start(bf16[4,16,3712]{2,1,0:T(8,128)(2,1)S(1)} %pad_maximum_fusion.1.refs_3_) | copy-start | bytes 1425412
  18.7 8.7 %collective-permute-start.2 = (bf16[4,16,3712]{2,1,0:T(8,128)(2,1)S(1)}, bf16[4,16,3712]{2,1,0:T(8,128)(2,1)S(1)}, u32[]{:S(2)}, u32[]{:S(2)}) collective-permute-start(bf16[4,16,3712]{2,1,0:T(8,128)(2,1)S(1)} %pad_maximum_fusion.1.refs_3_), channel_id=1, source_target_pairs={{0,2},{1,5},{2,0},{3,7},{4,6},{5,1},{6,4},{7,3},{8,10},{9,13},{10,... | collective-permute-start | bytes 1425416 | tf_op jit(solution)/shard_map/ppermute | solution.py:46
  27.6 21.8 %copy-start = (bf16[8,16,3712]{2,1,0:T(8,128)(2,1)}, bf16[8,16,3712]{2,1,0:T(8,128)(2,1)S(1)}, u32[]{:S(2)}) copy-start(bf16[8,16,3712]{2,1,0:T(8,128)(2,1)S(1)} %pad_maximum_fusion.refs_0_.refs_4_.refs_6_) | copy-start | bytes 2850820
  27.6 2.6 %collective-permute-start.3 = (bf16[8,16,3712]{2,1,0:T(8,128)(2,1)S(1)}, bf16[8,16,3712]{2,1,0:T(8,128)(2,1)S(1)}, u32[]{:S(2)}, u32[]{:S(2)}) collective-permute-start(bf16[8,16,3712]{2,1,0:T(8,128)(2,1)S(1)} %pad_maximum_fusion.refs_0_.refs_4_.refs_6_), channel_id=1, source_target_pairs={{0,1},{1,0},{2,3},{3,2},{4,5},{5,4},{6,7},{7,6},{8,9},{9,8},{10,11... | collective-permute-start | bytes 2850824 | tf_op jit(solution)/shard_map/ppermute | solution.py:50
  49.5 1.9 %collective-permute-start.4 = (bf16[8,16,1792]{2,1,0:T(8,128)(2,1)S(1)}, bf16[8,16,1792]{2,1,0:T(8,128)(2,1)S(1)}, u32[]{:S(2)}, u32[]{:S(2)}) collective-permute-start(bf16[8,16,1792]{2,1,0:T(8,128)(2,1)S(1)} %get-tuple-element.27), channel_id=1, source_target_pairs={{0,1},{1,0},{2,3},{3,2},{4,5},{5,4},{6,7},{7,6},{8,9},{9,8},{10,11... | collective-permute-start | bytes 1376264 | tf_op jit(solution)/shard_map/ppermute | solution.py:50
  49.5 3.5 %collective-permute-start.11 = (bf16[8,16,1792]{2,1,0:T(8,128)(2,1)S(1)}, bf16[8,16,1792]{2,1,0:T(8,128)(2,1)S(1)}, u32[]{:S(2)}, u32[]{:S(2)}) collective-permute-start(bf16[8,16,1792]{2,1,0:T(8,128)(2,1)S(1)} %get-tuple-element.29), channel_id=1, source_target_pairs={{0,1},{1,0},{2,3},{3,2},{4,5},{5,4},{6,7},{7,6},{8,9},{9,8},{10,11... | collective-permute-start | bytes 1376264 | tf_op jit(solution)/shard_map/ppermute | solution.py:50
  51.5 6.1 %collective-permute-start.5 = (bf16[4,16,1792]{2,1,0:T(8,128)(2,1)S(1)}, bf16[4,16,1792]{2,1,0:T(8,128)(2,1)S(1)}, u32[]{:S(2)}, u32[]{:S(2)}) collective-permute-start(bf16[4,16,1792]{2,1,0:T(8,128)(2,1)S(1)} %slice.123), channel_id=1, source_target_pairs={{0,2},{1,5},{2,0},{3,7},{4,6},{5,1},{6,4},{7,3},{8,10},{9,13},{10,... | collective-permute-start | bytes 688136 | tf_op jit(solution)/shard_map/ppermute | solution.py:46
  53.2 7.2 %collective-permute-start.12 = (bf16[4,16,1792]{2,1,0:T(8,128)(2,1)S(1)}, bf16[4,16,1792]{2,1,0:T(8,128)(2,1)S(1)}, u32[]{:S(2)}, u32[]{:S(2)}) collective-permute-start(bf16[4,16,1792]{2,1,0:T(8,128)(2,1)S(1)} %slice.129), channel_id=1, source_target_pairs={{0,2},{1,5},{2,0},{3,7},{4,6},{5,1},{6,4},{7,3},{8,10},{9,13},{10,... | collective-permute-start | bytes 688136 | tf_op jit(solution)/shard_map/ppermute | solution.py:46
  57.6 4.9 %collective-permute-start.6 = (bf16[2,16,1792]{2,1,0:T(8,128)(2,1)S(1)}, bf16[2,16,1792]{2,1,0:T(8,128)(2,1)S(1)}, u32[]{:S(2)}, u32[]{:S(2)}) collective-permute-start(bf16[2,16,1792]{2,1,0:T(8,128)(2,1)S(1)} %slice.125), channel_id=1, source_target_pairs={{0,4},{1,3},{2,6},{3,1},{4,0},{5,7},{6,2},{7,5},{8,12},{9,11},{10,... | collective-permute-start | bytes 344072 | tf_op jit(solution)/shard_map/ppermute | solution.py:46
  60.5 5.1 %collective-permute-start.13 = (bf16[2,16,1792]{2,1,0:T(8,128)(2,1)S(1)}, bf16[2,16,1792]{2,1,0:T(8,128)(2,1)S(1)}, u32[]{:S(2)}, u32[]{:S(2)}) collective-permute-start(bf16[2,16,1792]{2,1,0:T(8,128)(2,1)S(1)} %slice.131), channel_id=1, source_target_pairs={{0,4},{1,3},{2,6},{3,1},{4,0},{5,7},{6,2},{7,5},{8,12},{9,11},{10,... | collective-permute-start | bytes 344072 | tf_op jit(solution)/shard_map/ppermute | solution.py:46
  62.5 10.8 %collective-permute-start.7 = (bf16[2,16,1792]{2,1,0:T(8,128)(2,1)S(1)}, bf16[2,16,1792]{2,1,0:T(8,128)(2,1)S(1)}, u32[]{:S(2)}, u32[]{:S(2)}) collective-permute-start(bf16[2,16,1792]{2,1,0:T(8,128)(2,1)S(1)} %add_convert_fusion.13), channel_id=1, source_target_pairs={{0,8},{1,9},{2,10},{3,11},{4,12},{5,13},{6,14},{7,15},{8,0},{9,1},... | collective-permute-start | bytes 344072 | tf_op jit(solution)/shard_map/ppermute | solution.py:46
  65.6 9.2 %collective-permute-start.14 = (bf16[2,16,1792]{2,1,0:T(8,128)(2,1)S(1)}, bf16[2,16,1792]{2,1,0:T(8,128)(2,1)S(1)}, u32[]{:S(2)}, u32[]{:S(2)}) collective-permute-start(bf16[2,16,1792]{2,1,0:T(8,128)(2,1)S(1)} %add_convert_fusion.11), channel_id=1, source_target_pairs={{0,8},{1,9},{2,10},{3,11},{4,12},{5,13},{6,14},{7,15},{8,0},{9,1},... | collective-permute-start | bytes 344072 | tf_op jit(solution)/shard_map/ppermute | solution.py:46
  74.9 4.9 %collective-permute-start.15 = (bf16[2,16,1792]{2,1,0:T(8,128)(2,1)S(1)}, bf16[2,16,1792]{2,1,0:T(8,128)(2,1)S(1)}, u32[]{:S(2)}, u32[]{:S(2)}) collective-permute-start(bf16[2,16,1792]{2,1,0:T(8,128)(2,1)S(1)} %get-tuple-element.35), channel_id=1, source_target_pairs={{0,4},{1,3},{2,6},{3,1},{4,0},{5,7},{6,2},{7,5},{8,12},{9,11},{10,... | collective-permute-start | bytes 344072 | tf_op jit(solution)/shard_map/ppermute | solution.py:46
  75.0 6.5 %collective-permute-start.8 = (bf16[2,16,1792]{2,1,0:T(8,128)(2,1)S(1)}, bf16[2,16,1792]{2,1,0:T(8,128)(2,1)S(1)}, u32[]{:S(2)}, u32[]{:S(2)}) collective-permute-start(bf16[2,16,1792]{2,1,0:T(8,128)(2,1)S(1)} %get-tuple-element.36), channel_id=1, source_target_pairs={{0,4},{1,3},{2,6},{3,1},{4,0},{5,7},{6,2},{7,5},{8,12},{9,11},{10,... | collective-permute-start | bytes 344072 | tf_op jit(solution)/shard_map/ppermute | solution.py:46
  79.8 6.1 %collective-permute-start.16 = (bf16[4,16,1792]{2,1,0:T(8,128)(2,1)S(1)}, bf16[4,16,1792]{2,1,0:T(8,128)(2,1)S(1)}, u32[]{:S(2)}, u32[]{:S(2)}) collective-permute-start(bf16[4,16,1792]{2,1,0:T(8,128)(2,1)S(1)} %pad_maximum_fusion.6), channel_id=1, source_target_pairs={{0,2},{1,5},{2,0},{3,7},{4,6},{5,1},{6,4},{7,3},{8,10},{9,13},{10,... | collective-permute-start | bytes 688136 | tf_op jit(solution)/shard_map/ppermute | solution.py:46
  81.5 6.8 %collective-permute-start.9 = (bf16[4,16,1792]{2,1,0:T(8,128)(2,1)S(1)}, bf16[4,16,1792]{2,1,0:T(8,128)(2,1)S(1)}, u32[]{:S(2)}, u32[]{:S(2)}) collective-permute-start(bf16[4,16,1792]{2,1,0:T(8,128)(2,1)S(1)} %pad_maximum_fusion.5), channel_id=1, source_target_pairs={{0,2},{1,5},{2,0},{3,7},{4,6},{5,1},{6,4},{7,3},{8,10},{9,13},{10,... | collective-permute-start | bytes 688136 | tf_op jit(solution)/shard_map/ppermute | solution.py:46
  85.9 2.5 %collective-permute-start.17 = (bf16[8,16,1792]{2,1,0:T(8,128)(2,1)S(1)}, bf16[8,16,1792]{2,1,0:T(8,128)(2,1)S(1)}, u32[]{:S(2)}, u32[]{:S(2)}) collective-permute-start(bf16[8,16,1792]{2,1,0:T(8,128)(2,1)S(1)} %pad_maximum_fusion.3.refs_2_), channel_id=1, source_target_pairs={{0,1},{1,0},{2,3},{3,2},{4,5},{5,4},{6,7},{7,6},{8,9},{9,8},{10,11... | collective-permute-start | bytes 1376264 | tf_op jit(solution)/shard_map/ppermute | solution.py:50
  88.4 1.9 %collective-permute-start.10 = (bf16[8,16,1792]{2,1,0:T(8,128)(2,1)S(1)}, bf16[8,16,1792]{2,1,0:T(8,128)(2,1)S(1)}, u32[]{:S(2)}, u32[]{:S(2)}) collective-permute-start(bf16[8,16,1792]{2,1,0:T(8,128)(2,1)S(1)} %pad_maximum_fusion.2.refs_0_), channel_id=1, source_target_pairs={{0,1},{1,0},{2,3},{3,2},{4,5},{5,4},{6,7},{7,6},{8,9},{9,8},{10,11... | collective-permute-start | bytes 1376264 | tf_op jit(solution)/shard_map/ppermute | solution.py:50
  91.8 21.4 %collective-permute-start.18 = (bf16[8,16,1792]{2,1,0:T(8,128)(2,1)S(1)}, bf16[8,16,1792]{2,1,0:T(8,128)(2,1)S(1)}, u32[]{:S(2)}, u32[]{:S(2)}) collective-permute-start(bf16[8,16,1792]{2,1,0:T(8,128)(2,1)S(1)} %get-tuple-element.32), channel_id=1, source_target_pairs={{0,1},{1,0},{2,3},{3,2},{4,5},{5,4},{6,7},{7,6},{8,9},{9,8},{10,11... | collective-permute-start | bytes 1376264 | tf_op jit(solution)/shard_map/ppermute | solution.py:50
  111.7 3.1 %collective-permute-start.21 = (bf16[8,16,1792]{2,1,0:T(8,128)(2,1)S(1)}, bf16[8,16,1792]{2,1,0:T(8,128)(2,1)S(1)}, u32[]{:S(2)}, u32[]{:S(2)}) collective-permute-start(bf16[8,16,1792]{2,1,0:T(8,128)(2,1)S(1)} %get-tuple-element.34), channel_id=1, source_target_pairs={{0,1},{1,0},{2,3},{3,2},{4,5},{5,4},{6,7},{7,6},{8,9},{9,8},{10,11... | collective-permute-start | bytes 1376264 | tf_op jit(solution)/shard_map/ppermute | solution.py:50
  113.3 6.1 %collective-permute-start.19 = (bf16[4,16,1792]{2,1,0:T(8,128)(2,1)S(1)}, bf16[4,16,1792]{2,1,0:T(8,128)(2,1)S(1)}, u32[]{:S(2)}, u32[]{:S(2)}) collective-permute-start(bf16[4,16,1792]{2,1,0:T(8,128)(2,1)S(1)} %slice.133), channel_id=1, source_target_pairs={{0,2},{1,5},{2,0},{3,7},{4,6},{5,1},{6,4},{7,3},{8,10},{9,13},{10,... | collective-permute-start | bytes 688136 | tf_op jit(solution)/shard_map/ppermute | solution.py:46
  115.0 7.0 %collective-permute-start.22 = (bf16[4,16,1792]{2,1,0:T(8,128)(2,1)S(1)}, bf16[4,16,1792]{2,1,0:T(8,128)(2,1)S(1)}, u32[]{:S(2)}, u32[]{:S(2)}) collective-permute-start(bf16[4,16,1792]{2,1,0:T(8,128)(2,1)S(1)} %slice.139), channel_id=1, source_target_pairs={{0,2},{1,5},{2,0},{3,7},{4,6},{5,1},{6,4},{7,3},{8,10},{9,13},{10,... | collective-permute-start | bytes 688136 | tf_op jit(solution)/shard_map/ppermute | solution.py:46
  119.4 4.9 %collective-permute-start.20 = (bf16[2,16,1792]{2,1,0:T(8,128)(2,1)S(1)}, bf16[2,16,1792]{2,1,0:T(8,128)(2,1)S(1)}, u32[]{:S(2)}, u32[]{:S(2)}) collective-permute-start(bf16[2,16,1792]{2,1,0:T(8,128)(2,1)S(1)} %slice.135), channel_id=1, source_target_pairs={{0,4},{1,3},{2,6},{3,1},{4,0},{5,7},{6,2},{7,5},{8,12},{9,11},{10,... | collective-permute-start | bytes 344072 | tf_op jit(solution)/shard_map/ppermute | solution.py:46
  122.0 4.9 %collective-permute-start.23 = (bf16[2,16,1792]{2,1,0:T(8,128)(2,1)S(1)}, bf16[2,16,1792]{2,1,0:T(8,128)(2,1)S(1)}, u32[]{:S(2)}, u32[]{:S(2)}) collective-permute-start(bf16[2,16,1792]{2,1,0:T(8,128)(2,1)S(1)} %slice.141), channel_id=1, source_target_pairs={{0,4},{1,3},{2,6},{3,1},{4,0},{5,7},{6,2},{7,5},{8,12},{9,11},{10,... | collective-permute-start | bytes 344072 | tf_op jit(solution)/shard_map/ppermute | solution.py:46
  127.0 5.8 %collective-permute-start.24 = (bf16[8,2,1792]{2,0,1:T(8,128)(2,1)S(1)}, bf16[8,2,1792]{2,0,1:T(8,128)(2,1)S(1)}, u32[]{:S(2)}, u32[]{:S(2)}) collective-permute-start(bf16[8,2,1792]{2,0,1:T(8,128)(2,1)S(1)} %get-tuple-element.37), channel_id=1, source_target_pairs={{0,8},{1,9},{2,10},{3,11},{4,12},{5,13},{6,14},{7,15},{8,0},{9,1},... | collective-permute-start | bytes 172040 | tf_op jit(solution)/shard_map/ppermute | solution.py:67
  129.1 3.7 %collective-permute-start.25 = (bf16[8,2,1792]{2,0,1:T(8,128)(2,1)S(1)}, bf16[8,2,1792]{2,0,1:T(8,128)(2,1)S(1)}, u32[]{:S(2)}, u32[]{:S(2)}) collective-permute-start(bf16[8,2,1792]{2,0,1:T(8,128)(2,1)S(1)} %select_convert_fusion), channel_id=1, source_target_pairs={{0,1},{1,0},{2,3},{3,2},{4,5},{5,4},{6,7},{7,6},{8,9},{9,8},{10,11... | collective-permute-start | bytes 172040 | tf_op jit(solution)/shard_map/ppermute | solution.py:67
  129.2 4.6 %collective-permute-start.26 = (bf16[8,2,1792]{2,0,1:T(8,128)(2,1)S(1)}, bf16[8,2,1792]{2,0,1:T(8,128)(2,1)S(1)}, u32[]{:S(2)}, u32[]{:S(2)}) collective-permute-start(bf16[8,2,1792]{2,0,1:T(8,128)(2,1)S(1)} %get-tuple-element.38), channel_id=1, source_target_pairs={{0,9},{1,8},{2,11},{3,10},{4,13},{5,12},{6,15},{7,14},{8,1},{9,0},... | collective-permute-start | bytes 172040 | tf_op jit(solution)/shard_map/ppermute | solution.py:67

commit v3 on v2

--- a/solution.py
+++ b/solution.py
@@ -262,14 +262,12 @@
         return factor, gates
 
     unit_at = lax.axis_index("expert") * units
-    if not together:
-        for chunk in range(CHUNKS):
-            assemble(chunk)
-        factor, gates = gates_of()
     for block in range(blocks):
-        if together and block % 2 == 0:
-            assemble(block // 2)
-        if together and block == blocks - 1:
+        if block == 0:
+            assemble(0)
+        if block == 1:
+            for chunk in range(1, CHUNKS):
+                assemble(chunk)
             factor, gates = gates_of()
         value = scaled.at[:, block * width : (block + 1) * width]
         for side, sums in enumerate((gate_sum, up_sum)):

time: 136 us -> 136 us (level)
  no operation moved by 1% of the time
where the time goes in v3:
time: 136 us; the launch traced here: 134 us
  starting transfers between devices  49.1 us (36%)
  waiting for transfers between devices  43.1 us (32%)
  Pallas kernels  39.2 us (29%)
  other arithmetic  1.45 us (1%)
    pallas_call x5, Pallas kernels, call(): pl.pallas_call(kernel, in_specs=(specs or [IN_VMEM] * n_in) + [ANYWHERE]...  37.5 us
    ppermute x17, waiting for transfers between devices, exchange(): return lax.ppermute(value, ('expert', 'section'), pairs)  32.6 us
    ppermute x17, starting transfers between devices, exchange(): return lax.ppermute(value, ('expert', 'section'), pairs)  25.7 us
    ppermute x7, starting transfers between devices, swap(): return lax.ppermute(value, 'section', [(0, 1), (1, 0)])  20.3 us
    ppermute x7, waiting for transfers between devices, swap(): return lax.ppermute(value, 'section', [(0, 1), (1, 0)])  6.97 us
    ppermute x3, waiting for transfers between devices, cross(): return lax.ppermute(value, ('expert', 'section'), pairs)  3.52 us
    ppermute x3, starting transfers between devices, cross(): return lax.ppermute(value, ('expert', 'section'), pairs)  3.18 us
  transfers between devices with their start and end apart: 27, of which 21 were waited for; matrix products, arithmetic and copies ran while one was open for 1% of the time, Pallas kernels for 12%

profile of v3, /device:TPU:0, one launch (start us, length us, event | category | flops | bytes accessed | tf_op | source)
XLA Modules:
  0.0 134.2 jit_solution(15228161345481092093)
XLA Ops:
  0.0 1.7 %prepare.1.refs_3_ = bf16[1,16,3712]{2,1,0:T(8,128)(2,1)} custom-call(bf16[2,8,7168]{2,1,0:T(8,128)(2,1)} %tokens_ref.1, s32[1,2,4,8]{3,2,1,0:T(4,128)} %bitcast.18), custom_call_target="tpu_custom_call" | custom-call | tf_op jit(solution)/shard_map/prepare/pallas_call | solution.py:199
  1.7 4.0 %collective-permute-start = (bf16[1,16,3712]{2,1,0:T(8,128)(2,1)}, bf16[1,16,3712]{2,1,0:T(8,128)(2,1)S(1)}, u32[]{:S(2)}, u32[]{:S(2)}) collective-permute-start(bf16[1,16,3712]{2,1,0:T(8,128)(2,1)} %prepare.1.refs_3_), channel_id=1, source_target_pairs={{0,8},{1,9},{2,10},{3,11},{4,12},{5,13},{6,14},{7,15},{8,0},{9,1},... | collective-permute-start | bytes 356360 | tf_op jit(solution)/shard_map/ppermute | solution.py:46
  5.7 5.5 %fetch.3 = (bf16[86016,256]{1,0:T(8,128)(2,1)S(1)}, bf16[16,3712]{1,0:T(8,128)(2,1)S(1)}) custom-call(bf16[1,7168,2048]{2,1,0:T(8,128)(2,1)} %refs_7_.3, bf16[1,7168,2048]{2,1,0:T(8,128)(2,1)} %refs_8_.1, bf16[1,2048,7168]{2,1,0:T(8,128)(2,1)} %refs_9_.1, bf16[1,16,3712]{2,1,0:T(8,128)(2,1)} %prepare.1.refs_3_), custom_call_target="tpu_custom_call" | custom-call | bytes 14680064 | tf_op jit(solution)/shard_map/fetch/pallas_call | solution.py:160
  11.3 0.5 collective-permute-done
  11.9 1.2 collective-permute-start.1
  13.0 5.5 %fetch.4 = (bf16[86016,256]{1,0:T(8,128)(2,1)S(1)}, bf16[16,3712]{1,0:T(8,128)(2,1)S(1)}) custom-call(bf16[1,7168,2048]{2,1,0:T(8,128)(2,1)} %refs_7_.3, bf16[1,7168,2048]{2,1,0:T(8,128)(2,1)} %refs_8_.1, bf16[1,2048,7168]{2,1,0:T(8,128)(2,1)} %refs_9_.1, bf16[2,16,3712]{2,1,0:T(8,128)(2,1)} %copy-done.3, ...), custom_call_target="tpu_custom_call", output_to_operand_aliasing={{0}: (4, {})} | custom-call | bytes 14680064 | tf_op jit(solution)/shard_map/fetch/pallas_call | solution.py:160
  18.7 1.6 %collective-permute-start.2 = (bf16[4,16,3712]{2,1,0:T(8,128)(2,1)S(1)}, bf16[4,16,3712]{2,1,0:T(8,128)(2,1)S(1)}, u32[]{:S(2)}, u32[]{:S(2)}) collective-permute-start(bf16[4,16,3712]{2,1,0:T(8,128)(2,1)S(1)} %pad_maximum_fusion.1.refs_3_), channel_id=1, source_target_pairs={{0,2},{1,5},{2,0},{3,7},{4,6},{5,1},{6,4},{7,3},{8,10},{9,13},{10,... | collective-permute-start | bytes 1425416 | tf_op jit(solution)/shard_map/ppermute | solution.py:46
  20.3 5.5 %fetch.5 = (bf16[86016,256]{1,0:T(8,128)(2,1)S(1)}, bf16[16,3712]{1,0:T(8,128)(2,1)S(1)}) custom-call(bf16[1,7168,2048]{2,1,0:T(8,128)(2,1)} %refs_7_.3, bf16[1,7168,2048]{2,1,0:T(8,128)(2,1)} %refs_8_.1, bf16[1,2048,7168]{2,1,0:T(8,128)(2,1)} %refs_9_.1, bf16[4,16,3712]{2,1,0:T(8,128)(2,1)} %copy-done.2, ...), custom_call_target="tpu_custom_call", output_to_operand_aliasing={{0}: (4, {})} | custom-call | bytes 14680064 | tf_op jit(solution)/shard_map/fetch/pallas_call | solution.py:160
  25.8 1.6 %collective-permute-done.2 = bf16[4,16,3712]{2,1,0:T(8,128)(2,1)S(1)} collective-permute-done((bf16[4,16,3712]{2,1,0:T(8,128)(2,1)S(1)}, bf16[4,16,3712]{2,1,0:T(8,128)(2,1)S(1)}, u32[]{:S(2)}, u32[]{:S(2)}) %collective-permute-start.2) | collective-permute-done | bytes 475168 | tf_op jit(solution)/shard_map/ppermute | solution.py:46
  27.5 0.1 pad_maximum_fusion.refs_0_.refs_4_.refs_6_
  27.7 2.5 %collective-permute-done.3.refs_1_ = bf16[8,16,3712]{2,1,0:T(8,128)(2,1)S(1)} collective-permute-done((bf16[8,16,3712]{2,1,0:T(8,128)(2,1)S(1)}, bf16[8,16,3712]{2,1,0:T(8,128)(2,1)S(1)}, u32[]{:S(2)}, u32[]{:S(2)}) %collective-permute-start.3) | collective-permute-done | bytes 950304 | tf_op jit(solution)/shard_map/ppermute | solution.py:50
  30.2 19.3 %layer.2 = (bf16[8,16,1792]{2,1,0:T(8,128)(2,1)S(1)}, bf16[8,16,1792]{2,1,0:T(8,128)(2,1)S(1)}, bf16[8,16,1792]{2,1,0:T(8,128)(2,1)S(1)}, bf16[8,16,1792]{2,1,0:T(8,128)(2,1)S(1)}, bf16[86016,256]{1,0:T(8,128)(2,1)S(1)}) custom-call(bf16[8,16,3712]{2,1,0:T(8,128)(2,1)S(1)} %pad_maximum_fusion.refs_0_.refs_4_.refs_6_, ...), custom_call_target="tpu_custom_call", output_to_operand_aliasing={{4}: (8, {})} | custom-call | bytes 44040192 | tf_op jit(solution)/shard_map/layer/pallas_call | solution.py:160
  49.6 0.5 collective-permute-start.11
  50.1 1.3 collective-permute-done.4
  51.6 1.6 %collective-permute-start.5 = (bf16[4,16,1792]{2,1,0:T(8,128)(2,1)S(1)}, bf16[4,16,1792]{2,1,0:T(8,128)(2,1)S(1)}, u32[]{:S(2)}, u32[]{:S(2)}) collective-permute-start(bf16[4,16,1792]{2,1,0:T(8,128)(2,1)S(1)} %slice.123), channel_id=1, source_target_pairs={{0,2},{1,5},{2,0},{3,7},{4,6},{5,1},{6,4},{7,3},{8,10},{9,13},{10,... | collective-permute-start | bytes 688136 | tf_op jit(solution)/shard_map/ppermute | solution.py:46
  53.3 0.6 collective-permute-start.12
  53.9 3.8 %collective-permute-done.5 = bf16[4,16,1792]{2,1,0:T(8,128)(2,1)S(1)} collective-permute-done((bf16[4,16,1792]{2,1,0:T(8,128)(2,1)S(1)}, bf16[4,16,1792]{2,1,0:T(8,128)(2,1)S(1)}, u32[]{:S(2)}, u32[]{:S(2)}) %collective-permute-start.5) | collective-permute-done | bytes 229408 | tf_op jit(solution)/shard_map/ppermute | solution.py:46
  57.7 1.0 collective-permute-start.6
  58.7 1.7 %collective-permute-done.12 = bf16[4,16,1792]{2,1,0:T(8,128)(2,1)S(1)} collective-permute-done((bf16[4,16,1792]{2,1,0:T(8,128)(2,1)S(1)}, bf16[4,16,1792]{2,1,0:T(8,128)(2,1)S(1)}, u32[]{:S(2)}, u32[]{:S(2)}) %collective-permute-start.12) | collective-permute-done | bytes 229408 | tf_op jit(solution)/shard_map/ppermute | solution.py:46
  60.6 1.0 collective-permute-start.13
  61.6 1.0 collective-permute-done.6
  62.6 3.0 %collective-permute-start.7 = (bf16[2,16,1792]{2,1,0:T(8,128)(2,1)S(1)}, bf16[2,16,1792]{2,1,0:T(8,128)(2,1)S(1)}, u32[]{:S(2)}, u32[]{:S(2)}) collective-permute-start(bf16[2,16,1792]{2,1,0:T(8,128)(2,1)S(1)} %add_convert_fusion.13), channel_id=1, source_target_pairs={{0,8},{1,9},{2,10},{3,11},{4,12},{5,13},{6,14},{7,15},{8,0},{9,1},... | collective-permute-start | bytes 344072 | tf_op jit(solution)/shard_map/ppermute | solution.py:46
  65.7 3.0 %collective-permute-start.14 = (bf16[2,16,1792]{2,1,0:T(8,128)(2,1)S(1)}, bf16[2,16,1792]{2,1,0:T(8,128)(2,1)S(1)}, u32[]{:S(2)}, u32[]{:S(2)}) collective-permute-start(bf16[2,16,1792]{2,1,0:T(8,128)(2,1)S(1)} %add_convert_fusion.11), channel_id=1, source_target_pairs={{0,8},{1,9},{2,10},{3,11},{4,12},{5,13},{6,14},{7,15},{8,0},{9,1},... | collective-permute-start | bytes 344072 | tf_op jit(solution)/shard_map/ppermute | solution.py:46
  68.7 4.7 %collective-permute-done.7 = bf16[2,16,1792]{2,1,0:T(8,128)(2,1)S(1)} collective-permute-done((bf16[2,16,1792]{2,1,0:T(8,128)(2,1)S(1)}, bf16[2,16,1792]{2,1,0:T(8,128)(2,1)S(1)}, u32[]{:S(2)}, u32[]{:S(2)}) %collective-permute-start.7) | collective-permute-done | bytes 114720 | tf_op jit(solution)/shard_map/ppermute | solution.py:46
  73.4 1.5 %collective-permute-done.14 = bf16[2,16,1792]{2,1,0:T(8,128)(2,1)S(1)} collective-permute-done((bf16[2,16,1792]{2,1,0:T(8,128)(2,1)S(1)}, bf16[2,16,1792]{2,1,0:T(8,128)(2,1)S(1)}, u32[]{:S(2)}, u32[]{:S(2)}) %collective-permute-start.14) | collective-permute-done | bytes 114720 | tf_op jit(solution)/shard_map/ppermute | solution.py:46
  75.1 2.0 %collective-permute-start.8 = (bf16[2,16,1792]{2,1,0:T(8,128)(2,1)S(1)}, bf16[2,16,1792]{2,1,0:T(8,128)(2,1)S(1)}, u32[]{:S(2)}, u32[]{:S(2)}) collective-permute-start(bf16[2,16,1792]{2,1,0:T(8,128)(2,1)S(1)} %get-tuple-element.36), channel_id=1, source_target_pairs={{0,4},{1,3},{2,6},{3,1},{4,0},{5,7},{6,2},{7,5},{8,12},{9,11},{10,... | collective-permute-start | bytes 344072 | tf_op jit(solution)/shard_map/ppermute | solution.py:46
  77.1 2.8 %collective-permute-done.15 = bf16[2,16,1792]{2,1,0:T(8,128)(2,1)S(1)} collective-permute-done((bf16[2,16,1792]{2,1,0:T(8,128)(2,1)S(1)}, bf16[2,16,1792]{2,1,0:T(8,128)(2,1)S(1)}, u32[]{:S(2)}, u32[]{:S(2)}) %collective-permute-start.15) | collective-permute-done | bytes 114720 | tf_op jit(solution)/shard_map/ppermute | solution.py:46
  79.9 1.6 %collective-permute-start.16 = (bf16[4,16,1792]{2,1,0:T(8,128)(2,1)S(1)}, bf16[4,16,1792]{2,1,0:T(8,128)(2,1)S(1)}, u32[]{:S(2)}, u32[]{:S(2)}) collective-permute-start(bf16[4,16,1792]{2,1,0:T(8,128)(2,1)S(1)} %pad_maximum_fusion.6), channel_id=1, source_target_pairs={{0,2},{1,5},{2,0},{3,7},{4,6},{5,1},{6,4},{7,3},{8,10},{9,13},{10,... | collective-permute-start | bytes 688136 | tf_op jit(solution)/shard_map/ppermute | solution.py:46
  81.6 1.6 %collective-permute-start.9 = (bf16[4,16,1792]{2,1,0:T(8,128)(2,1)S(1)}, bf16[4,16,1792]{2,1,0:T(8,128)(2,1)S(1)}, u32[]{:S(2)}, u32[]{:S(2)}) collective-permute-start(bf16[4,16,1792]{2,1,0:T(8,128)(2,1)S(1)} %pad_maximum_fusion.5), channel_id=1, source_target_pairs={{0,2},{1,5},{2,0},{3,7},{4,6},{5,1},{6,4},{7,3},{8,10},{9,13},{10,... | collective-permute-start | bytes 688136 | tf_op jit(solution)/shard_map/ppermute | solution.py:46
  83.1 2.8 %collective-permute-done.16 = bf16[4,16,1792]{2,1,0:T(8,128)(2,1)S(1)} collective-permute-done((bf16[4,16,1792]{2,1,0:T(8,128)(2,1)S(1)}, bf16[4,16,1792]{2,1,0:T(8,128)(2,1)S(1)}, u32[]{:S(2)}, u32[]{:S(2)}) %collective-permute-start.16) | collective-permute-done | bytes 229408 | tf_op jit(solution)/shard_map/ppermute | solution.py:46
  86.1 2.3 %collective-permute-done.9 = bf16[4,16,1792]{2,1,0:T(8,128)(2,1)S(1)} collective-permute-done((bf16[4,16,1792]{2,1,0:T(8,128)(2,1)S(1)}, bf16[4,16,1792]{2,1,0:T(8,128)(2,1)S(1)}, u32[]{:S(2)}, u32[]{:S(2)}) %collective-permute-start.9) | collective-permute-done | bytes 229408 | tf_op jit(solution)/shard_map/ppermute | solution.py:46
  88.6 1.8 %collective-permute-done.10.refs_1_ = bf16[8,16,1792]{2,1,0:T(8,128)(2,1)S(1)} collective-permute-done((bf16[8,16,1792]{2,1,0:T(8,128)(2,1)S(1)}, bf16[8,16,1792]{2,1,0:T(8,128)(2,1)S(1)}, u32[]{:S(2)}, u32[]{:S(2)}) %collective-permute-start.10) | collective-permute-done | bytes 458784 | tf_op jit(solution)/shard_map/ppermute | solution.py:50
  90.3 1.5 %layer.3 = (bf16[8,16,1792]{2,1,0:T(8,128)(2,1)S(1)}, bf16[8,16,1792]{2,1,0:T(8,128)(2,1)S(1)}, bf16[8,16,1792]{2,1,0:T(8,128)(2,1)S(1)}, bf16[8,16,1792]{2,1,0:T(8,128)(2,1)S(1)}, bf16[86016,256]{1,0:T(8,128)(2,1)S(1)}) custom-call(bf16[8,16,1792]{2,1,0:T(8,128)(2,1)S(1)} %pad_maximum_fusion.2.refs_0_, ...), custom_call_target="tpu_custom_call", output_to_operand_aliasing={{4}: (10, {})} | custom-call | bytes 44040192 | tf_op jit(solution)/shard_map/layer/pallas_call | solution.py:160
  91.9 19.4 %collective-permute-start.18 = (bf16[8,16,1792]{2,1,0:T(8,128)(2,1)S(1)}, bf16[8,16,1792]{2,1,0:T(8,128)(2,1)S(1)}, u32[]{:S(2)}, u32[]{:S(2)}) collective-permute-start(bf16[8,16,1792]{2,1,0:T(8,128)(2,1)S(1)} %get-tuple-element.32), channel_id=1, source_target_pairs={{0,1},{1,0},{2,3},{3,2},{4,5},{5,4},{6,7},{7,6},{8,9},{9,8},{10,11... | collective-permute-start | bytes 1376264 | tf_op jit(solution)/shard_map/ppermute | solution.py:50
  111.4 1.4 %collective-permute-done.18 = bf16[8,16,1792]{2,1,0:T(8,128)(2,1)S(1)} collective-permute-done((bf16[8,16,1792]{2,1,0:T(8,128)(2,1)S(1)}, bf16[8,16,1792]{2,1,0:T(8,128)(2,1)S(1)}, u32[]{:S(2)}, u32[]{:S(2)}) %collective-permute-start.18) | collective-permute-done | bytes 458784 | tf_op jit(solution)/shard_map/ppermute | solution.py:50
  112.8 1.6 %collective-permute-start.19 = (bf16[4,16,1792]{2,1,0:T(8,128)(2,1)S(1)}, bf16[4,16,1792]{2,1,0:T(8,128)(2,1)S(1)}, u32[]{:S(2)}, u32[]{:S(2)}) collective-permute-start(bf16[4,16,1792]{2,1,0:T(8,128)(2,1)S(1)} %slice.133), channel_id=1, source_target_pairs={{0,2},{1,5},{2,0},{3,7},{4,6},{5,1},{6,4},{7,3},{8,10},{9,13},{10,... | collective-permute-start | bytes 688136 | tf_op jit(solution)/shard_map/ppermute | solution.py:46
  114.5 0.6 collective-permute-start.22
  115.1 3.8 %collective-permute-done.19 = bf16[4,16,1792]{2,1,0:T(8,128)(2,1)S(1)} collective-permute-done((bf16[4,16,1792]{2,1,0:T(8,128)(2,1)S(1)}, bf16[4,16,1792]{2,1,0:T(8,128)(2,1)S(1)}, u32[]{:S(2)}, u32[]{:S(2)}) %collective-permute-start.19) | collective-permute-done | bytes 229408 | tf_op jit(solution)/shard_map/ppermute | solution.py:46
  119.0 0.7 collective-permute-start.20
  119.7 1.8 %collective-permute-done.22 = bf16[4,16,1792]{2,1,0:T(8,128)(2,1)S(1)} collective-permute-done((bf16[4,16,1792]{2,1,0:T(8,128)(2,1)S(1)}, bf16[4,16,1792]{2,1,0:T(8,128)(2,1)S(1)}, u32[]{:S(2)}, u32[]{:S(2)}) %collective-permute-start.22) | collective-permute-done | bytes 229408 | tf_op jit(solution)/shard_map/ppermute | solution.py:46
  121.6 0.7 collective-permute-start.23
  122.3 1.6 %collective-permute-done.20 = bf16[2,16,1792]{2,1,0:T(8,128)(2,1)S(1)} collective-permute-done((bf16[2,16,1792]{2,1,0:T(8,128)(2,1)S(1)}, bf16[2,16,1792]{2,1,0:T(8,128)(2,1)S(1)}, u32[]{:S(2)}, u32[]{:S(2)}) %collective-permute-start.20) | collective-permute-done | bytes 114720 | tf_op jit(solution)/shard_map/ppermute | solution.py:46
  123.9 2.5 %collective-permute-done.23 = bf16[2,16,1792]{2,1,0:T(8,128)(2,1)S(1)} collective-permute-done((bf16[2,16,1792]{2,1,0:T(8,128)(2,1)S(1)}, bf16[2,16,1792]{2,1,0:T(8,128)(2,1)S(1)}, u32[]{:S(2)}, u32[]{:S(2)}) %collective-permute-start.23) | collective-permute-done | bytes 114720 | tf_op jit(solution)/shard_map/ppermute | solution.py:46
  126.6 2.1 %collective-permute-start.24 = (bf16[8,2,1792]{2,0,1:T(8,128)(2,1)S(1)}, bf16[8,2,1792]{2,0,1:T(8,128)(2,1)S(1)}, u32[]{:S(2)}, u32[]{:S(2)}) collective-permute-start(bf16[8,2,1792]{2,0,1:T(8,128)(2,1)S(1)} %get-tuple-element.37), channel_id=1, source_target_pairs={{0,8},{1,9},{2,10},{3,11},{4,12},{5,13},{6,14},{7,15},{8,0},{9,1},... | collective-permute-start | bytes 172040 | tf_op jit(solution)/shard_map/ppermute | solution.py:67
  128.7 1.0 collective-permute-start.26
  129.8 2.6 %collective-permute-done.24 = bf16[8,2,1792]{2,0,1:T(8,128)(2,1)S(1)} collective-permute-done((bf16[8,2,1792]{2,0,1:T(8,128)(2,1)S(1)}, bf16[8,2,1792]{2,0,1:T(8,128)(2,1)S(1)}, u32[]{:S(2)}, u32[]{:S(2)}) %collective-permute-start.24) | collective-permute-done | bytes 57376 | tf_op jit(solution)/shard_map/ppermute | solution.py:67
  132.4 1.0 collective-permute-done.26
  133.5 0.7 select_n.50
  (62 shorter events, 2.2 us)
Async XLA Ops:
  1.7 10.1 %copy-start.1 = (bf16[1,16,3712]{2,1,0:T(8,128)(2,1)S(1)}, bf16[1,16,3712]{2,1,0:T(8,128)(2,1)}, u32[]{:S(2)}) copy-start(bf16[1,16,3712]{2,1,0:T(8,128)(2,1)} %prepare.1.refs_3_) | copy-start | bytes 356356
  1.7 10.1 %collective-permute-start = (bf16[1,16,3712]{2,1,0:T(8,128)(2,1)}, bf16[1,16,3712]{2,1,0:T(8,128)(2,1)S(1)}, u32[]{:S(2)}, u32[]{:S(2)}) collective-permute-start(bf16[1,16,3712]{2,1,0:T(8,128)(2,1)} %prepare.1.refs_3_), channel_id=1, source_target_pairs={{0,8},{1,9},{2,10},{3,11},{4,12},{5,13},{6,14},{7,15},{8,0},{9,1},... | collective-permute-start | bytes 356360 | tf_op jit(solution)/shard_map/ppermute | solution.py:46
  11.8 1.2 copy-start.3
  11.9 6.7 %collective-permute-start.1 = (bf16[2,16,3712]{2,1,0:T(8,128)(2,1)S(1)}, bf16[2,16,3712]{2,1,0:T(8,128)(2,1)S(1)}, u32[]{:S(2)}, u32[]{:S(2)}) collective-permute-start(bf16[2,16,3712]{2,1,0:T(8,128)(2,1)S(1)} %pad_maximum_fusion.4.refs_3_), channel_id=1, source_target_pairs={{0,4},{1,3},{2,6},{3,1},{4,0},{5,7},{6,2},{7,5},{8,12},{9,11},{10,... | collective-permute-start | bytes 712712 | tf_op jit(solution)/shard_map/ppermute | solution.py:46
  18.7 1.6 %copy-start.2 = (bf16[4,16,3712]{2,1,0:T(8,128)(2,1)}, bf16[4,16,3712]{2,1,0:T(8,128)(2,1)S(1)}, u32[]{:S(2)}) copy-start(bf16[4,16,3712]{2,1,0:T(8,128)(2,1)S(1)} %pad_maximum_fusion.1.refs_3_) | copy-start | bytes 1425412
  18.7 8.7 %collective-permute-start.2 = (bf16[4,16,3712]{2,1,0:T(8,128)(2,1)S(1)}, bf16[4,16,3712]{2,1,0:T(8,128)(2,1)S(1)}, u32[]{:S(2)}, u32[]{:S(2)}) collective-permute-start(bf16[4,16,3712]{2,1,0:T(8,128)(2,1)S(1)} %pad_maximum_fusion.1.refs_3_), channel_id=1, source_target_pairs={{0,2},{1,5},{2,0},{3,7},{4,6},{5,1},{6,4},{7,3},{8,10},{9,13},{10,... | collective-permute-start | bytes 1425416 | tf_op jit(solution)/shard_map/ppermute | solution.py:46
  27.6 21.9 %copy-start = (bf16[8,16,3712]{2,1,0:T(8,128)(2,1)}, bf16[8,16,3712]{2,1,0:T(8,128)(2,1)S(1)}, u32[]{:S(2)}) copy-start(bf16[8,16,3712]{2,1,0:T(8,128)(2,1)S(1)} %pad_maximum_fusion.refs_0_.refs_4_.refs_6_) | copy-start | bytes 2850820
  27.6 2.6 %collective-permute-start.3 = (bf16[8,16,3712]{2,1,0:T(8,128)(2,1)S(1)}, bf16[8,16,3712]{2,1,0:T(8,128)(2,1)S(1)}, u32[]{:S(2)}, u32[]{:S(2)}) collective-permute-start(bf16[8,16,3712]{2,1,0:T(8,128)(2,1)S(1)} %pad_maximum_fusion.refs_0_.refs_4_.refs_6_), channel_id=1, source_target_pairs={{0,1},{1,0},{2,3},{3,2},{4,5},{5,4},{6,7},{7,6},{8,9},{9,8},{10,11... | collective-permute-start | bytes 2850824 | tf_op jit(solution)/shard_map/ppermute | solution.py:50
  49.6 1.9 %collective-permute-start.4 = (bf16[8,16,1792]{2,1,0:T(8,128)(2,1)S(1)}, bf16[8,16,1792]{2,1,0:T(8,128)(2,1)S(1)}, u32[]{:S(2)}, u32[]{:S(2)}) collective-permute-start(bf16[8,16,1792]{2,1,0:T(8,128)(2,1)S(1)} %get-tuple-element.27), channel_id=1, source_target_pairs={{0,1},{1,0},{2,3},{3,2},{4,5},{5,4},{6,7},{7,6},{8,9},{9,8},{10,11... | collective-permute-start | bytes 1376264 | tf_op jit(solution)/shard_map/ppermute | solution.py:50
  49.6 3.5 %collective-permute-start.11 = (bf16[8,16,1792]{2,1,0:T(8,128)(2,1)S(1)}, bf16[8,16,1792]{2,1,0:T(8,128)(2,1)S(1)}, u32[]{:S(2)}, u32[]{:S(2)}) collective-permute-start(bf16[8,16,1792]{2,1,0:T(8,128)(2,1)S(1)} %get-tuple-element.29), channel_id=1, source_target_pairs={{0,1},{1,0},{2,3},{3,2},{4,5},{5,4},{6,7},{7,6},{8,9},{9,8},{10,11... | collective-permute-start | bytes 1376264 | tf_op jit(solution)/shard_map/ppermute | solution.py:50
  51.6 6.1 %collective-permute-start.5 = (bf16[4,16,1792]{2,1,0:T(8,128)(2,1)S(1)}, bf16[4,16,1792]{2,1,0:T(8,128)(2,1)S(1)}, u32[]{:S(2)}, u32[]{:S(2)}) collective-permute-start(bf16[4,16,1792]{2,1,0:T(8,128)(2,1)S(1)} %slice.123), channel_id=1, source_target_pairs={{0,2},{1,5},{2,0},{3,7},{4,6},{5,1},{6,4},{7,3},{8,10},{9,13},{10,... | collective-permute-start | bytes 688136 | tf_op jit(solution)/shard_map/ppermute | solution.py:46
  53.3 7.2 %collective-permute-start.12 = (bf16[4,16,1792]{2,1,0:T(8,128)(2,1)S(1)}, bf16[4,16,1792]{2,1,0:T(8,128)(2,1)S(1)}, u32[]{:S(2)}, u32[]{:S(2)}) collective-permute-start(bf16[4,16,1792]{2,1,0:T(8,128)(2,1)S(1)} %slice.129), channel_id=1, source_target_pairs={{0,2},{1,5},{2,0},{3,7},{4,6},{5,1},{6,4},{7,3},{8,10},{9,13},{10,... | collective-permute-start | bytes 688136 | tf_op jit(solution)/shard_map/ppermute | solution.py:46
  57.7 4.9 %collective-permute-start.6 = (bf16[2,16,1792]{2,1,0:T(8,128)(2,1)S(1)}, bf16[2,16,1792]{2,1,0:T(8,128)(2,1)S(1)}, u32[]{:S(2)}, u32[]{:S(2)}) collective-permute-start(bf16[2,16,1792]{2,1,0:T(8,128)(2,1)S(1)} %slice.125), channel_id=1, source_target_pairs={{0,4},{1,3},{2,6},{3,1},{4,0},{5,7},{6,2},{7,5},{8,12},{9,11},{10,... | collective-permute-start | bytes 344072 | tf_op jit(solution)/shard_map/ppermute | solution.py:46
  60.6 5.1 %collective-permute-start.13 = (bf16[2,16,1792]{2,1,0:T(8,128)(2,1)S(1)}, bf16[2,16,1792]{2,1,0:T(8,128)(2,1)S(1)}, u32[]{:S(2)}, u32[]{:S(2)}) collective-permute-start(bf16[2,16,1792]{2,1,0:T(8,128)(2,1)S(1)} %slice.131), channel_id=1, source_target_pairs={{0,4},{1,3},{2,6},{3,1},{4,0},{5,7},{6,2},{7,5},{8,12},{9,11},{10,... | collective-permute-start | bytes 344072 | tf_op jit(solution)/shard_map/ppermute | solution.py:46
  62.6 10.8 %collective-permute-start.7 = (bf16[2,16,1792]{2,1,0:T(8,128)(2,1)S(1)}, bf16[2,16,1792]{2,1,0:T(8,128)(2,1)S(1)}, u32[]{:S(2)}, u32[]{:S(2)}) collective-permute-start(bf16[2,16,1792]{2,1,0:T(8,128)(2,1)S(1)} %add_convert_fusion.13), channel_id=1, source_target_pairs={{0,8},{1,9},{2,10},{3,11},{4,12},{5,13},{6,14},{7,15},{8,0},{9,1},... | collective-permute-start | bytes 344072 | tf_op jit(solution)/shard_map/ppermute | solution.py:46
  65.7 9.2 %collective-permute-start.14 = (bf16[2,16,1792]{2,1,0:T(8,128)(2,1)S(1)}, bf16[2,16,1792]{2,1,0:T(8,128)(2,1)S(1)}, u32[]{:S(2)}, u32[]{:S(2)}) collective-permute-start(bf16[2,16,1792]{2,1,0:T(8,128)(2,1)S(1)} %add_convert_fusion.11), channel_id=1, source_target_pairs={{0,8},{1,9},{2,10},{3,11},{4,12},{5,13},{6,14},{7,15},{8,0},{9,1},... | collective-permute-start | bytes 344072 | tf_op jit(solution)/shard_map/ppermute | solution.py:46
  75.0 4.9 %collective-permute-start.15 = (bf16[2,16,1792]{2,1,0:T(8,128)(2,1)S(1)}, bf16[2,16,1792]{2,1,0:T(8,128)(2,1)S(1)}, u32[]{:S(2)}, u32[]{:S(2)}) collective-permute-start(bf16[2,16,1792]{2,1,0:T(8,128)(2,1)S(1)} %get-tuple-element.35), channel_id=1, source_target_pairs={{0,4},{1,3},{2,6},{3,1},{4,0},{5,7},{6,2},{7,5},{8,12},{9,11},{10,... | collective-permute-start | bytes 344072 | tf_op jit(solution)/shard_map/ppermute | solution.py:46
  75.1 6.5 %collective-permute-start.8 = (bf16[2,16,1792]{2,1,0:T(8,128)(2,1)S(1)}, bf16[2,16,1792]{2,1,0:T(8,128)(2,1)S(1)}, u32[]{:S(2)}, u32[]{:S(2)}) collective-permute-start(bf16[2,16,1792]{2,1,0:T(8,128)(2,1)S(1)} %get-tuple-element.36), channel_id=1, source_target_pairs={{0,4},{1,3},{2,6},{3,1},{4,0},{5,7},{6,2},{7,5},{8,12},{9,11},{10,... | collective-permute-start | bytes 344072 | tf_op jit(solution)/shard_map/ppermute | solution.py:46
  79.9 6.1 %collective-permute-start.16 = (bf16[4,16,1792]{2,1,0:T(8,128)(2,1)S(1)}, bf16[4,16,1792]{2,1,0:T(8,128)(2,1)S(1)}, u32[]{:S(2)}, u32[]{:S(2)}) collective-permute-start(bf16[4,16,1792]{2,1,0:T(8,128)(2,1)S(1)} %pad_maximum_fusion.6), channel_id=1, source_target_pairs={{0,2},{1,5},{2,0},{3,7},{4,6},{5,1},{6,4},{7,3},{8,10},{9,13},{10,... | collective-permute-start | bytes 688136 | tf_op jit(solution)/shard_map/ppermute | solution.py:46
  81.6 6.8 %collective-permute-start.9 = (bf16[4,16,1792]{2,1,0:T(8,128)(2,1)S(1)}, bf16[4,16,1792]{2,1,0:T(8,128)(2,1)S(1)}, u32[]{:S(2)}, u32[]{:S(2)}) collective-permute-start(bf16[4,16,1792]{2,1,0:T(8,128)(2,1)S(1)} %pad_maximum_fusion.5), channel_id=1, source_target_pairs={{0,2},{1,5},{2,0},{3,7},{4,6},{5,1},{6,4},{7,3},{8,10},{9,13},{10,... | collective-permute-start | bytes 688136 | tf_op jit(solution)/shard_map/ppermute | solution.py:46
  86.0 2.5 %collective-permute-start.17 = (bf16[8,16,1792]{2,1,0:T(8,128)(2,1)S(1)}, bf16[8,16,1792]{2,1,0:T(8,128)(2,1)S(1)}, u32[]{:S(2)}, u32[]{:S(2)}) collective-permute-start(bf16[8,16,1792]{2,1,0:T(8,128)(2,1)S(1)} %pad_maximum_fusion.3.refs_2_), channel_id=1, source_target_pairs={{0,1},{1,0},{2,3},{3,2},{4,5},{5,4},{6,7},{7,6},{8,9},{9,8},{10,11... | collective-permute-start | bytes 1376264 | tf_op jit(solution)/shard_map/ppermute | solution.py:50
  88.5 1.9 %collective-permute-start.10 = (bf16[8,16,1792]{2,1,0:T(8,128)(2,1)S(1)}, bf16[8,16,1792]{2,1,0:T(8,128)(2,1)S(1)}, u32[]{:S(2)}, u32[]{:S(2)}) collective-permute-start(bf16[8,16,1792]{2,1,0:T(8,128)(2,1)S(1)} %pad_maximum_fusion.2.refs_0_), channel_id=1, source_target_pairs={{0,1},{1,0},{2,3},{3,2},{4,5},{5,4},{6,7},{7,6},{8,9},{9,8},{10,11... | collective-permute-start | bytes 1376264 | tf_op jit(solution)/shard_map/ppermute | solution.py:50
  91.9 20.8 %collective-permute-start.18 = (bf16[8,16,1792]{2,1,0:T(8,128)(2,1)S(1)}, bf16[8,16,1792]{2,1,0:T(8,128)(2,1)S(1)}, u32[]{:S(2)}, u32[]{:S(2)}) collective-permute-start(bf16[8,16,1792]{2,1,0:T(8,128)(2,1)S(1)} %get-tuple-element.32), channel_id=1, source_target_pairs={{0,1},{1,0},{2,3},{3,2},{4,5},{5,4},{6,7},{7,6},{8,9},{9,8},{10,11... | collective-permute-start | bytes 1376264 | tf_op jit(solution)/shard_map/ppermute | solution.py:50
  111.3 3.1 %collective-permute-start.21 = (bf16[8,16,1792]{2,1,0:T(8,128)(2,1)S(1)}, bf16[8,16,1792]{2,1,0:T(8,128)(2,1)S(1)}, u32[]{:S(2)}, u32[]{:S(2)}) collective-permute-start(bf16[8,16,1792]{2,1,0:T(8,128)(2,1)S(1)} %get-tuple-element.34), channel_id=1, source_target_pairs={{0,1},{1,0},{2,3},{3,2},{4,5},{5,4},{6,7},{7,6},{8,9},{9,8},{10,11... | collective-permute-start | bytes 1376264 | tf_op jit(solution)/shard_map/ppermute | solution.py:50
  112.8 6.1 %collective-permute-start.19 = (bf16[4,16,1792]{2,1,0:T(8,128)(2,1)S(1)}, bf16[4,16,1792]{2,1,0:T(8,128)(2,1)S(1)}, u32[]{:S(2)}, u32[]{:S(2)}) collective-permute-start(bf16[4,16,1792]{2,1,0:T(8,128)(2,1)S(1)} %slice.133), channel_id=1, source_target_pairs={{0,2},{1,5},{2,0},{3,7},{4,6},{5,1},{6,4},{7,3},{8,10},{9,13},{10,... | collective-permute-start | bytes 688136 | tf_op jit(solution)/shard_map/ppermute | solution.py:46
  114.5 7.0 %collective-permute-start.22 = (bf16[4,16,1792]{2,1,0:T(8,128)(2,1)S(1)}, bf16[4,16,1792]{2,1,0:T(8,128)(2,1)S(1)}, u32[]{:S(2)}, u32[]{:S(2)}) collective-permute-start(bf16[4,16,1792]{2,1,0:T(8,128)(2,1)S(1)} %slice.139), channel_id=1, source_target_pairs={{0,2},{1,5},{2,0},{3,7},{4,6},{5,1},{6,4},{7,3},{8,10},{9,13},{10,... | collective-permute-start | bytes 688136 | tf_op jit(solution)/shard_map/ppermute | solution.py:46
  119.0 4.9 %collective-permute-start.20 = (bf16[2,16,1792]{2,1,0:T(8,128)(2,1)S(1)}, bf16[2,16,1792]{2,1,0:T(8,128)(2,1)S(1)}, u32[]{:S(2)}, u32[]{:S(2)}) collective-permute-start(bf16[2,16,1792]{2,1,0:T(8,128)(2,1)S(1)} %slice.135), channel_id=1, source_target_pairs={{0,4},{1,3},{2,6},{3,1},{4,0},{5,7},{6,2},{7,5},{8,12},{9,11},{10,... | collective-permute-start | bytes 344072 | tf_op jit(solution)/shard_map/ppermute | solution.py:46
  121.6 4.9 %collective-permute-start.23 = (bf16[2,16,1792]{2,1,0:T(8,128)(2,1)S(1)}, bf16[2,16,1792]{2,1,0:T(8,128)(2,1)S(1)}, u32[]{:S(2)}, u32[]{:S(2)}) collective-permute-start(bf16[2,16,1792]{2,1,0:T(8,128)(2,1)S(1)} %slice.141), channel_id=1, source_target_pairs={{0,4},{1,3},{2,6},{3,1},{4,0},{5,7},{6,2},{7,5},{8,12},{9,11},{10,... | collective-permute-start | bytes 344072 | tf_op jit(solution)/shard_map/ppermute | solution.py:46
  126.6 5.8 %collective-permute-start.24 = (bf16[8,2,1792]{2,0,1:T(8,128)(2,1)S(1)}, bf16[8,2,1792]{2,0,1:T(8,128)(2,1)S(1)}, u32[]{:S(2)}, u32[]{:S(2)}) collective-permute-start(bf16[8,2,1792]{2,0,1:T(8,128)(2,1)S(1)} %get-tuple-element.37), channel_id=1, source_target_pairs={{0,8},{1,9},{2,10},{3,11},{4,12},{5,13},{6,14},{7,15},{8,0},{9,1},... | collective-permute-start | bytes 172040 | tf_op jit(solution)/shard_map/ppermute | solution.py:67
  128.7 3.7 %collective-permute-start.25 = (bf16[8,2,1792]{2,0,1:T(8,128)(2,1)S(1)}, bf16[8,2,1792]{2,0,1:T(8,128)(2,1)S(1)}, u32[]{:S(2)}, u32[]{:S(2)}) collective-permute-start(bf16[8,2,1792]{2,0,1:T(8,128)(2,1)S(1)} %select_convert_fusion), channel_id=1, source_target_pairs={{0,1},{1,0},{2,3},{3,2},{4,5},{5,4},{6,7},{7,6},{8,9},{9,8},{10,11... | collective-permute-start | bytes 172040 | tf_op jit(solution)/shard_map/ppermute | solution.py:67
  128.7 4.6 %collective-permute-start.26 = (bf16[8,2,1792]{2,0,1:T(8,128)(2,1)S(1)}, bf16[8,2,1792]{2,0,1:T(8,128)(2,1)S(1)}, u32[]{:S(2)}, u32[]{:S(2)}) collective-permute-start(bf16[8,2,1792]{2,0,1:T(8,128)(2,1)S(1)} %get-tuple-element.38), channel_id=1, source_target_pairs={{0,9},{1,8},{2,11},{3,10},{4,13},{5,12},{6,15},{7,14},{8,1},{9,0},... | collective-permute-start | bytes 172040 | tf_op jit(solution)/shard_map/ppermute | solution.py:67
